TPU v7x, 32 devices: a whole 2x2x4 slice. The times are simulated.
32 devices in a mesh: dp: 4 (over y, x), seq: 4 (over z), mp: 2 (over core).
Axes of the slice: x: 2, y: 2, z: 4, core: 2. Of those that a mesh axis runs over, the one named last changes fastest.
Arguments:
- inputs: bfloat16 [8, 1024, 2304], P('dp', 'seq', 'mp'), may hold values from -6 to 6
- starts: int32 [8, 1024], P('dp', 'seq'), may hold values from 0 to 1, as said below
- init_state: float32 [2, 8, 2304], P(None, 'dp', 'mp'), may hold values from -4 to 4
- weight_one: bfloat16 [2, 2304, 3, 2304], P(None, None, None, 'mp'), may hold values from -0.09375 to 0.09375
- bias_one: float32 [3, 2304], P(None, 'mp'), may hold values from -1.5 to 8.5
- weight_two: bfloat16 [2304, 3, 2304], P(None, None, 'mp'), may hold values from -0.25 to 0.25
- bias_two: float32 [3, 2304], P(None, 'mp'), may hold values from -1.5 to 8.5
- cotangent: bfloat16 [8, 1024, 2304], P('dp', 'seq', 'mp'), may hold values from -6 to 6
Outputs:
- pooled_two: bfloat16 [8, 1024, 2304], P('dp', 'seq', 'mp')
- input_grad: float32 [8, 1024, 2304], P('dp', 'seq', 'mp')
- weight_one_grad: float32 [2, 2304, 3, 2304], P(None, None, None, 'mp')
- bias_one_grad: float32 [3, 2304], P(None, 'mp')
- weight_two_grad: float32 [2304, 3, 2304], P(None, None, 'mp')
- bias_two_grad: float32 [3, 2304], P(None, 'mp')
Inputs may be any that keep to these rules, and one draw needn't show every extreme that they name: `starts`: 1 marks a token that begins a new document; among the 2 sequences of each index of dp one has no mark.
All inputs are finite; a program needn't handle non-finite values.
Results may differ from a plain program's by a relative error of at most 0.0047.
Values may be sent and summed in bfloat16 or wider, within the bound.
A program may use at most 704 MiB of HBM per device.

v0:
```python
import functools

import jax
import jax.numpy as jnp
from jax import lax
from jax.experimental import pallas as pl
from jax.experimental.pallas import tpu as pltpu
from jax.sharding import PartitionSpec as P

F32 = jnp.float32
BF16 = jnp.bfloat16
SUB = 8
STEP = 16
VMEM = pl.BlockSpec(memory_space=pltpu.VMEM)


def sigmoid(x):
    return 0.5 * jnp.tanh(0.5 * x) + 0.5


def lane_blocks(channels):
    width = 384 if channels % 384 == 0 else channels
    return [slice(at, at + width) for at in range(0, channels, width)]


def scan_down(scale, shift):
    row = lax.broadcasted_iota(jnp.int32, scale.shape, 0)
    for step in (1, 2, 4):
        earlier = row >= step
        scale_before = jnp.where(earlier, pltpu.roll(scale, step, 0), 1.0)
        shift_before = jnp.where(earlier, pltpu.roll(shift, step, 0), 0.0)
        shift = scale * shift_before + shift
        scale = scale * scale_before
    return scale, shift


def scan_up(scale, shift):
    row = lax.broadcasted_iota(jnp.int32, scale.shape, 0)
    for step in (1, 2, 4):
        later = row < SUB - step
        scale_after = jnp.where(later, pltpu.roll(scale, SUB - step, 0), 1.0)
        shift_after = jnp.where(later, pltpu.roll(shift, SUB - step, 0), 0.0)
        shift = scale * shift_after + shift
        scale = scale * scale_after
    return scale, shift


def greet(axis):
    count = lax.axis_size(axis)
    me = lax.axis_index(axis)
    barrier = pltpu.get_barrier_semaphore()
    for step in range(1, count):
        pl.semaphore_signal(
            barrier, inc=1, device_id={axis: lax.rem(me + step, count)}, device_id_type=pl.DeviceIdType.MESH
        )
    pl.semaphore_wait(barrier, count - 1)


def to_all(src, slots, send_sems, recv_sems, axis):
    count = lax.axis_size(axis)
    me = lax.axis_index(axis)
    copies = []
    for step in range(1, count):
        copies.append(
            pltpu.make_async_remote_copy(
                src_ref=src,
                dst_ref=slots.at[step - 1],
                send_sem=send_sems.at[step - 1],
                recv_sem=recv_sems.at[step - 1],
                device_id={axis: lax.rem(me + step, count)},
                device_id_type=pl.DeviceIdType.MESH,
            )
        )
    for copy in copies:
        copy.start()
    return copies


def from_earlier(slots, initial, scale_rows, shift_rows, axis):
    count = lax.axis_size(axis)
    me = lax.axis_index(axis)
    state = initial
    for block in range(count - 1):
        slot = jnp.maximum(me - block - 1, 0)
        after = slots[slot, scale_rows, :] * state + slots[slot, shift_rows, :]
        state = jnp.where(block < me, after, state)
    return state


def from_later(slots, shape, scale_rows, shift_rows, axis):
    count = lax.axis_size(axis)
    me = lax.axis_index(axis)
    message = jnp.zeros(shape, F32)
    for block in range(count - 1, 0, -1):
        slot = jnp.minimum(me + count - block - 1, count - 2)
        after = slots[slot, scale_rows, :] * message + slots[slot, shift_rows, :]
        message = jnp.where(block > me, after, message)
    return message


def first_pass(seqs, tokens, channels, gates, bias, keep, upd, fgt, out, scale, shift, summary):
    def body(at, carried):
        given = list(carried)
        for seq in range(seqs):
            for half in range(STEP // SUB):
                rows = pl.ds(pl.multiple_of(seq * tokens + at * STEP + half * SUB, SUB), SUB)
                kept = keep[rows, :][:, 0:1]
                for number, lanes in enumerate(lane_blocks(channels)):
                    u = jnp.tanh(gates[0, rows, lanes] + bias[0:1, lanes])
                    f = sigmoid(gates[1, rows, lanes] + bias[1:2, lanes])
                    o = sigmoid(gates[2, rows, lanes] + bias[2:3, lanes])
                    upd[rows, lanes] = u
                    fgt[rows, lanes] = f
                    out[rows, lanes] = o
                    a, b = scan_down(f * kept, (1.0 - f) * u)
                    place = (seq * len(lane_blocks(channels)) + number) * 2
                    b = a * given[place + 1] + b
                    a = a * given[place]
                    scale[rows, lanes] = a
                    shift[rows, lanes] = b
                    given[place] = a[SUB - 1 : SUB]
                    given[place + 1] = b[SUB - 1 : SUB]
        return tuple(given)

    begin = []
    for seq in range(seqs):
        for lanes in lane_blocks(channels):
            width = lanes.stop - lanes.start
            begin += [jnp.ones((1, width), F32), jnp.zeros((1, width), F32)]
    end = lax.fori_loop(0, tokens // STEP, body, tuple(begin))
    place = 0
    for seq in range(seqs):
        for lanes in lane_blocks(channels):
            summary[seq : seq + 1, lanes] = end[place]
            summary[seqs + seq : seqs + seq + 1, lanes] = end[place + 1]
            place += 2


def back_pass(seqs, tokens, channels, upstream, keep, fgt, out, scale, shift, summary, row0):
    steps = tokens // STEP

    def body(index, carried):
        at = steps - 1 - index
        given = list(carried)
        for seq in range(seqs):
            whole = pl.ds(pl.multiple_of(seq * tokens + at * STEP, STEP), STEP)
            for number, lanes in enumerate(lane_blocks(channels)):
                ups = upstream[whole, lanes].astype(F32)
                place = (seq * len(lane_blocks(channels)) + number) * 2
                for half in reversed(range(STEP // SUB)):
                    rows = pl.ds(pl.multiple_of(seq * tokens + at * STEP + half * SUB, SUB), SUB)
                    kept = keep[rows, :][:, 0:1]
                    retain = fgt[rows, lanes] * kept
                    direct = ups[half * SUB : half * SUB + SUB] * out[rows, lanes]
                    a, b = scan_up(retain, retain * direct)
                    b = a * given[place + 1] + b
                    a = a * given[place]
                    scale[rows, lanes] = a
                    shift[rows, lanes] = b
                    given[place] = a[0:1]
                    given[place + 1] = b[0:1]
        return tuple(given)

    begin = []
    for seq in range(seqs):
        for lanes in lane_blocks(channels):
            width = lanes.stop - lanes.start
            begin += [jnp.ones((1, width), F32), jnp.zeros((1, width), F32)]
    end = lax.fori_loop(0, steps, body, tuple(begin))
    place = 0
    for seq in range(seqs):
        for lanes in lane_blocks(channels):
            summary[row0 + seq : row0 + seq + 1, lanes] = end[place]
            summary[row0 + seqs + seq : row0 + seqs + seq + 1, lanes] = end[place + 1]
            place += 2


def states_pass(seqs, tokens, channels, entering, out, scale, shift, state, pooled):
    def body(at, none):
        for seq in range(seqs):
            rows = pl.ds(pl.multiple_of(seq * tokens + at * STEP, STEP), STEP)
            for lanes in lane_blocks(channels):
                value = scale[rows, lanes] * entering[seq : seq + 1, lanes] + shift[rows, lanes]
                state[rows, lanes] = value
                pooled[rows, lanes] = (out[rows, lanes] * value).astype(BF16)
        return none

    lax.fori_loop(0, tokens // STEP, body, 0)


def grads_pass(seqs, tokens, channels, message, entering, upstream, keep, upd, fgt, out, state, scale, shift, grads, sums):
    steps = tokens // STEP
    sums[...] = jnp.zeros_like(sums)
    for seq in range(seqs):
        for lanes in lane_blocks(channels):
            width = lanes.stop - lanes.start

            def body(index, later, seq=seq, lanes=lanes, width=width):
                at = steps - 1 - index
                whole = pl.ds(pl.multiple_of(seq * tokens + at * STEP, STEP), STEP)
                row = lax.broadcasted_iota(jnp.int32, (STEP, width), 0)
                kept = keep[whole, :][:, 0:1]
                ups = upstream[whole, lanes].astype(F32)
                u, f, o = upd[whole, lanes], fgt[whole, lanes], out[whole, lanes]
                states = state[whole, lanes]
                arriving = scale[whole, lanes] * message[seq : seq + 1, lanes] + shift[whole, lanes]
                adjoint = ups * o + jnp.where(row == STEP - 1, later, pltpu.roll(arriving, STEP - 1, 0))
                tile = pl.ds(pl.multiple_of(seq * tokens + jnp.maximum(at * STEP - SUB, 0), SUB), SUB)
                last = state[tile, lanes][SUB - 1 : SUB]
                first = jnp.where(at == 0, entering[seq : seq + 1, lanes], last)
                before = jnp.where(row == 0, first, pltpu.roll(states, 1, 0))
                given = [
                    adjoint * (1.0 - f) * (1.0 - u * u),
                    adjoint * (before * kept - u) * f * (1.0 - f),
                    ups * states * o * (1.0 - o),
                ]
                for gate, value in enumerate(given):
                    value = value.astype(BF16)
                    grads[whole, gate * channels + lanes.start : gate * channels + lanes.stop] = value
                    value = value.astype(F32)
                    total = value[:SUB]
                    for half in range(1, STEP // SUB):
                        total = total + value[half * SUB : half * SUB + SUB]
                    sums[gate, :, lanes] += total
                return arriving[0:1]

            lax.fori_loop(0, steps, body, message[seq : seq + 1, lanes])


def forward_kernel(seqs, tokens, channels, gates, bias, keep, initial, hidden, upd, fgt, out, state, entering, scale, shift, summary, slots, send_sems, recv_sems):
    greet("seq")
    first_pass(seqs, tokens, channels, gates, bias, keep, upd, fgt, out, scale, shift, summary)
    copies = to_all(summary, slots, send_sems, recv_sems, "seq")
    for copy in copies:
        copy.wait()
    entering[...] = from_earlier(slots, initial[...], slice(0, seqs), slice(seqs, 2 * seqs), "seq")
    states_pass(seqs, tokens, channels, entering, out, scale, shift, state, hidden)


def top_kernel(seqs, tokens, channels, gates, bias, keep, initial, cotangent, pooled, grads, sums, upd, fgt, out, state, entering, message, scale, shift, back_scale, back_shift, summary, slots, send_sems, recv_sems):
    greet("seq")
    first_pass(seqs, tokens, channels, gates, bias, keep, upd, fgt, out, scale, shift, summary)
    back_pass(seqs, tokens, channels, cotangent, keep, fgt, out, back_scale, back_shift, summary, 2 * seqs)
    copies = to_all(summary, slots, send_sems, recv_sems, "seq")
    for copy in copies:
        copy.wait()
    entering[...] = from_earlier(slots, initial[...], slice(0, seqs), slice(seqs, 2 * seqs), "seq")
    message[...] = from_later(
        slots, (seqs, channels), slice(2 * seqs, 3 * seqs), slice(3 * seqs, 4 * seqs), "seq"
    )
    states_pass(seqs, tokens, channels, entering, out, scale, shift, state, pooled)
    grads_pass(seqs, tokens, channels, message, entering, cotangent, keep, upd, fgt, out, state, back_scale, back_shift, grads, sums)


def backward_kernel(seqs, tokens, channels, upstream, keep, upd, fgt, out, state, entering, grads, sums, message, scale, shift, summary, slots, send_sems, recv_sems):
    greet("seq")
    back_pass(seqs, tokens, channels, upstream, keep, fgt, out, scale, shift, summary, 0)
    copies = to_all(summary, slots, send_sems, recv_sems, "seq")
    for copy in copies:
        copy.wait()
    message[...] = from_later(slots, (seqs, channels), slice(0, seqs), slice(seqs, 2 * seqs), "seq")
    grads_pass(seqs, tokens, channels, message, entering, upstream, keep, upd, fgt, out, state, scale, shift, grads, sums)


def exchange_scratch(rows, channels):
    count = lax.axis_size("seq")
    return [
        pltpu.VMEM((rows, channels), F32),
        pltpu.VMEM((count - 1, rows, channels), F32),
        pltpu.SemaphoreType.DMA((count - 1,)),
        pltpu.SemaphoreType.DMA((count - 1,)),
    ]


def params(number):
    return pltpu.CompilerParams(collective_id=number, has_side_effects=True, vmem_limit_bytes=56 * 2**20)


def cost(elements, ops, moved):
    return pl.CostEstimate(flops=elements * ops, bytes_accessed=moved, transcendentals=elements * 3)


def pool_forward(seqs, tokens, gates, bias, keep, initial):
    channels = gates.shape[2]
    rows = seqs * tokens
    whole = jax.ShapeDtypeStruct((rows, channels), F32)
    return pl.pallas_call(
        functools.partial(forward_kernel, seqs, tokens, channels),
        out_shape=(
            jax.ShapeDtypeStruct((rows, channels), BF16),
            whole,
            whole,
            whole,
            whole,
            jax.ShapeDtypeStruct((seqs, channels), F32),
        ),
        in_specs=[VMEM] * 4,
        out_specs=[VMEM] * 6,
        scratch_shapes=[pltpu.VMEM((rows, channels), F32)] * 2 + exchange_scratch(2 * seqs, channels),
        compiler_params=params(1),
        cost_estimate=cost(rows * channels, 60, rows * channels * 30),
        name="pool_forward",
    )(gates, bias, keep, initial)


def pool_top(seqs, tokens, gates, bias, keep, initial, cotangent):
    channels = gates.shape[2]
    rows = seqs * tokens
    whole = pltpu.VMEM((rows, channels), F32)
    edge = pltpu.VMEM((seqs, channels), F32)
    return pl.pallas_call(
        functools.partial(top_kernel, seqs, tokens, channels),
        out_shape=(
            jax.ShapeDtypeStruct((rows, channels), BF16),
            jax.ShapeDtypeStruct((rows, 3 * channels), BF16),
            jax.ShapeDtypeStruct((3, SUB, channels), F32),
        ),
        in_specs=[VMEM] * 5,
        out_specs=[VMEM] * 3,
        scratch_shapes=[whole] * 4 + [edge] * 2 + [whole] * 4 + exchange_scratch(4 * seqs, channels),
        compiler_params=params(2),
        cost_estimate=cost(rows * channels, 120, rows * channels * 22),
        name="pool_top",
    )(gates, bias, keep, initial, cotangent)


def pool_backward(seqs, tokens, upstream, keep, upd, fgt, out, state, entering):
    rows, channels = upstream.shape
    whole = pltpu.VMEM((rows, channels), F32)
    return pl.pallas_call(
        functools.partial(backward_kernel, seqs, tokens, channels),
        out_shape=(
            jax.ShapeDtypeStruct((rows, 3 * channels), BF16),
            jax.ShapeDtypeStruct((3, SUB, channels), F32),
        ),
        in_specs=[VMEM] * 7,
        out_specs=[VMEM] * 2,
        scratch_shapes=[pltpu.VMEM((seqs, channels), F32)] + [whole] * 2 + exchange_scratch(2 * seqs, channels),
        compiler_params=params(3),
        cost_estimate=cost(rows * channels, 60, rows * channels * 26),
        name="pool_backward",
    )(upstream, keep, upd, fgt, out, state, entering)


def shifted(value, axis, steps):
    count = lax.axis_size(axis)
    initial, last = (max(0, -steps), min(count, count - steps))
    return lax.ppermute(value, axis, [(source, source + steps) for source in range(initial, last)])


def gather_channels(value):
    count = lax.axis_size("mp")
    if count != 2:
        return lax.all_gather(value, "mp", axis=value.ndim - 1, tiled=True)
    other = lax.ppermute(value, "mp", [(0, 1), (1, 0)])
    second = lax.axis_index("mp") == 1
    return jnp.concatenate([jnp.where(second, other, value), jnp.where(second, value, other)], value.ndim - 1)


def sum_channels(terms):
    count = lax.axis_size("mp")
    if count != 2:
        return lax.psum_scatter(terms, "mp", scatter_dimension=1, tiled=True)
    width = terms.shape[1] // 2
    second = lax.axis_index("mp") == 1
    low, high = terms[:, :width], terms[:, width:]
    other = lax.ppermute(jnp.where(second, low, high), "mp", [(0, 1), (1, 0)])
    return jnp.where(second, high, low) + other


def dot(lhs, rhs, dims):
    return lax.dot_general(lhs, rhs, (dims, ((), ())), preferred_element_type=F32)


def reduce_weights(partial):
    shard = lax.psum_scatter(partial.astype(BF16), ("dp", "seq"), scatter_dimension=0, tiled=True)
    return lax.all_gather(shard, ("dp", "seq"), axis=0, tiled=True).astype(F32)


def local(inputs, starts, init_state, weight_one, bias_one, weight_two, bias_two, cotangent):
    seqs, tokens, channels = inputs.shape
    rows = seqs * tokens
    width = weight_one.shape[1]
    keep = jnp.broadcast_to((1 - starts).astype(F32).reshape(rows, 1), (rows, 128))
    taps = weight_one.transpose(0, 2, 1, 3)
    mix = weight_two.transpose(1, 0, 2)

    edge = gather_channels(shifted(inputs[:, -1], "seq", 1))
    full = gather_channels(inputs)
    previous = jnp.concatenate([edge[:, None], full[:, :-1]], 1).reshape(rows, width)
    full = full.reshape(rows, width)
    both = jnp.concatenate([full, previous], 1)
    gates_one = jnp.einsum(
        "tkd,kgdc->gtc", both.reshape(rows, 2, width), taps, preferred_element_type=F32
    )
    hidden, upd, fgt, out, state, entering = pool_forward(seqs, tokens, gates_one, bias_one, keep, init_state[0])
    full_hidden = gather_channels(hidden)
    gates_two = jnp.einsum("td,gdc->gtc", full_hidden, mix, preferred_element_type=F32)
    pooled_two, grad_two, sums_two = pool_top(
        seqs, tokens, gates_two, bias_two, keep, init_state[1], cotangent.reshape(rows, channels)
    )
    hidden_terms = jnp.einsum(
        "tgc,gdc->td", grad_two.reshape(rows, 3, channels), mix, preferred_element_type=F32
    )
    hidden_grad = sum_channels(hidden_terms)
    grad_one, sums_one = pool_backward(seqs, tokens, hidden_grad, keep, upd, fgt, out, state, entering)
    weight_two_grad = dot(full_hidden, grad_two, ((0,), (0,)))
    weight_two_grad = reduce_weights(weight_two_grad)
    next_first = shifted(grad_one.reshape(seqs, tokens, -1)[:, 0], "seq", -1)
    following = jnp.concatenate([grad_one.reshape(seqs, tokens, -1)[:, 1:], next_first[:, None]], 1).reshape(rows, -1)
    weight_one_grad = jnp.stack(
        [
            reduce_weights(dot(full, grad_one, ((0,), (0,)))),
            reduce_weights(dot(previous, grad_one, ((0,), (0,)))),
        ]
    )
    input_terms = jnp.einsum(
        "tgc,gdc->td", grad_one.reshape(rows, 3, channels), taps[0], preferred_element_type=F32
    ) + jnp.einsum("tgc,gdc->td", following.reshape(rows, 3, channels), taps[1], preferred_element_type=F32)
    input_grad = sum_channels(input_terms)
    bias_one_grad, bias_two_grad = lax.psum((jnp.sum(sums_one, 1), jnp.sum(sums_two, 1)), ("dp", "seq"))
    return (
        pooled_two.reshape(seqs, tokens, channels),
        input_grad.reshape(seqs, tokens, channels),
        weight_one_grad.reshape(2, width, 3, channels),
        bias_one_grad,
        weight_two_grad.reshape(width, 3, channels),
        bias_two_grad,
    )


def solution(mesh):
    return jax.shard_map(
        local,
        mesh=mesh,
        in_specs=(
            P("dp", "seq", "mp"),
            P("dp", "seq"),
            P(None, "dp", "mp"),
            P(None, None, None, "mp"),
            P(None, "mp"),
            P(None, None, "mp"),
            P(None, "mp"),
            P("dp", "seq", "mp"),
        ),
        out_specs=(
            P("dp", "seq", "mp"),
            P("dp", "seq", "mp"),
            P(None, None, None, "mp"),
            P(None, "mp"),
            P(None, None, "mp"),
            P(None, "mp"),
        ),
        check_vma=False,
    )
```

profile of v0, /device:TPU:0, one launch (start us, length us, event | category | flops | bytes accessed | tf_op | source)
XLA Modules:
  0.0 1574.9 jit_solution(11478258010303236534)
XLA Ops:
  8.5 4.5 collective-permute-start.1
  18.0 25.5 %convolution_bitcast_fusion.gates = f32[3,512,1152]{2,1,0:T(8,128)} fusion(bf16[512,1,2304]{2,0,1:T(8,128)(2,1)S(1)} %bitcast.97, bf16[512,1,2304]{2,0,1:T(8,128)(2,1)S(1)} %bitcast.95, bf16[2,2304,3,1152]{3,1,2,0:T(8,128)(2,1)} %param.11), kind=kOutput, calls=%fused_computation.12 | convolution fusion | flops 16316891136 | bytes 43646976 | tf_op jit(solution)/shard_map/tkd,kgdc->gtc/dot_general | solution.py:393
  44.4 18.1 %pool_forward.1 = (bf16[512,1152]{1,0:T(8,128)(2,1)}, f32[512,1152]{1,0:T(8,128)}, f32[512,1152]{1,0:T(8,128)}, f32[512,1152]{1,0:T(8,128)}, f32[512,1152]{1,0:T(8,128)}, /*index=5*/f32[2,1152]{1,0:T(2,128)}) custom-call(f32[3,512,1152]{2,1,0:T(8,128)} %convolution_bitcast_fusion.gates, f32[3,1152]{1,0:T(4,128)} %bias.2, f32[512,128]{1,0:T(8,128)} %broadcast_in_dim.15.keep, ...), custom_call_target="tpu_custom_call" | custom-call | flops 35389440 | bytes 17694720 | tf_op jit(solution)/shard_map/pool_forward/pallas_call | solution.py:287
  67.1 14.6 fusion.6.gates
  81.7 28.1 %pool_top.1 = (bf16[512,1152]{1,0:T(8,128)(2,1)}, bf16[512,3456]{1,0:T(8,128)(2,1)}, f32[3,8,1152]{2,1,0:T(8,128)}) custom-call(f32[3,512,1152]{2,1,0:T(8,128)} %fusion.6.gates, f32[3,1152]{1,0:T(4,128)} %bias.3, f32[512,128]{1,0:T(8,128)} %broadcast_in_dim.15.keep, f32[2,1152]{1,0:T(2,128)} %get-tuple-element.52.initial, bf16[512,1152]{1,0:T(8,128)(2,1)} %bitcast.101), custom_call_target="tpu_custom_call" | custom-call | flops 70778880 | bytes 12976128 | tf_op jit(solution)/shard_map/pool_top/pallas_call | solution.py:311
  109.8 13.6 convolution_convert_fusion
  125.4 3.7 copy.39
  129.2 13.1 fusion.9
  142.6 4.5 collective-permute-done.4
  149.1 24.8 %pool_backward.1 = (bf16[512,3456]{1,0:T(8,128)(2,1)}, f32[3,8,1152]{2,1,0:T(8,128)}) custom-call(f32[512,1152]{1,0:T(8,128)} %select_add_fusion.1.upstream, f32[512,128]{1,0:T(8,128)} %broadcast_in_dim.15.keep, f32[512,1152]{1,0:T(8,128)} %get-tuple-element.20.upd, f32[512,1152]{1,0:T(8,128)} %get-tuple-element.21.fgt, f32[512,1152]{1,0:T(8,128)} %get-tuple-element.22.out, ...), custom_call_target="tpu_custom_call" | custom-call | flops 35389440 | bytes 15335424 | tf_op jit(solution)/shard_map/pool_backward/pallas_call | solution.py:330
  173.9 13.6 convolution_convert_fusion.1
  189.5 14.0 convolution_convert_fusion.2
  203.6 175.3 %reduce-scatter.8.cloned.1.call-done = bf16[144,3456]{1,0:T(8,128)(2,1)} async-done(((bf16[2304,3456]{1,0:T(8,128)(2,1)}), bf16[144,3456]{1,0:T(8,128)(2,1)}) %reduce-scatter.8.cloned.1.call-update) | async-done | bytes 995344 | tf_op jit(solution)/shard_map/reduce_scatter | solution.py:376
  378.9 258.4 %reduce-scatter.6.cloned.1.call-done = bf16[144,3456]{1,0:T(8,128)(2,1)} async-done(((bf16[2304,3456]{1,0:T(8,128)(2,1)}), bf16[144,3456]{1,0:T(8,128)(2,1)}) %reduce-scatter.6.cloned.1.call-update) | async-done | bytes 995344 | tf_op jit(solution)/shard_map/reduce_scatter | solution.py:376
  637.4 258.4 %reduce-scatter.4.cloned.1.call-done = bf16[144,3456]{1,0:T(8,128)(2,1)} async-done(((bf16[2304,3456]{1,0:T(8,128)(2,1)}), bf16[144,3456]{1,0:T(8,128)(2,1)}) %reduce-scatter.4.cloned.1.call-update) | async-done | bytes 995344 | tf_op jit(solution)/shard_map/reduce_scatter | solution.py:376
  895.9 3.6 copy.41
  901.4 15.8 %fusion.12 = f32[512,2304]{1,0:T(8,128)} fusion(bf16[512,3,1152]{0,2,1:T(8,128)(2,1)} %bitcast.93, bf16[2,3,2304,1152]{3,2,1,0:T(8,128)(2,1)} %bitcast.105), kind=kOutput, calls=%fused_computation.15 | convolution fusion | flops 8153726976 | bytes 24182784 | tf_op jit(solution)/shard_map/tgc,gdc->td/dot_general | solution.py:417
  919.7 9.0 copy.57
  931.9 9.4 pad_maximum_fusion
  941.3 7.6 reshape_reshape.3
  948.9 14.2 fusion.14
  965.4 81.0 %all-reduce = (f32[3,1152]{1,0:T(4,128)}, f32[3,1152]{1,0:T(4,128)}) all-reduce(f32[3,1152]{1,0:T(4,128)S(1)} %reduce_sum.18, f32[3,1152]{1,0:T(4,128)S(1)} %reduce_sum.19), channel_id=1, replica_groups=mesh['dp'=4,'seq'=4,'mp'=2] {'dp','seq'}, use_global_device_ids=true, to_apply=%region_3.4 | all-reduce | flops 6912 | bytes 55296 | tf_op jit(solution)/shard_map/psum | solution.py:421
  1046.5 4.8 select_add_fusion
  1051.3 31.2 %all-gather.8.cloned.1.call-done = bf16[2304,3456]{1,0:T(8,128)(2,1)} async-done(((bf16[144,3456]{1,0:T(8,128)(2,1)}), bf16[2304,3456]{1,0:T(8,128)(2,1)}) %all-gather.8.cloned.1.call-update) | async-done | bytes 15925264 | tf_op jit(solution)/shard_map/all_gather | solution.py:377
  1082.5 22.6 %copy.49 = f32[2304,3456]{0,1:T(8,128)} copy(bf16[2304,3456]{1,0:T(8,128)(2,1)} %all-gather.8.cloned.1.call-done) | data formatting | bytes 47775744 | tf_op jit(solution)/shard_map/reshape | solution.py:427
  1105.1 31.8 %copy.51 = f32[2304,3,1152]{2,0,1:T(8,128)} copy(f32[2304,3,1152]{0,2,1:T(8,128)} %bitcast.88) | data formatting | bytes 63700992
  1136.9 130.8 %all-gather.6.cloned.1.call-done = bf16[2304,3456]{1,0:T(8,128)(2,1)} async-done(((bf16[144,3456]{1,0:T(8,128)(2,1)}), bf16[2304,3456]{1,0:T(8,128)(2,1)}) %all-gather.6.cloned.1.call-update) | async-done | bytes 15925264 | tf_op jit(solution)/shard_map/all_gather | solution.py:377
  1267.7 21.7 %copy.48 = bf16[2304,3456]{0,1:T(8,128)(2,1)} copy(bf16[2304,3456]{1,0:T(8,128)(2,1)} %all-gather.6.cloned.1.call-done) | data formatting | bytes 31850496 | tf_op jit(solution)/shard_map/all_gather | solution.py:377
  1289.4 162.7 %all-gather.4.cloned.1.call-done = bf16[2304,3456]{1,0:T(8,128)(2,1)} async-done(((bf16[144,3456]{1,0:T(8,128)(2,1)}), bf16[2304,3456]{1,0:T(8,128)(2,1)}) %all-gather.4.cloned.1.call-update) | async-done | bytes 15925264 | tf_op jit(solution)/shard_map/all_gather | solution.py:377
  1452.2 21.7 %copy.47 = bf16[2304,3456]{0,1:T(8,128)(2,1)} copy(bf16[2304,3456]{1,0:T(8,128)(2,1)} %all-gather.4.cloned.1.call-done) | data formatting | bytes 31850496 | tf_op jit(solution)/shard_map/all_gather | solution.py:377
  1473.9 31.0 %maximum_convert_fusion = f32[2,2304,3,1152]{1,3,2,0:T(8,128)} fusion(bf16[1,2304,3,1152]{1,3,2,0:T(8,128)(2,1)} %bitcast.89, bf16[1,2304,3,1152]{1,3,2,0:T(8,128)(2,1)} %bitcast.90), kind=kLoop, calls=%fused_computation | loop fusion | flops 31850496 | bytes 95551488 | tf_op jit(solution)/shard_map/stack | solution.py:411
  1504.9 61.7 %copy.50 = f32[2,2304,3,1152]{3,1,2,0:T(8,128)} copy(f32[2,2304,3,1152]{1,3,2,0:T(8,128)} %maximum_convert_fusion) | data formatting | bytes 127401984
  (66 shorter events, 29.1 us)
Async XLA Ops:
  7.2 371.7 %reduce-scatter.8.cloned.1.call-start = ((), (), s32[]{:S(2)}) async-start(), calls=%async_computation.7 | async-start | bytes 16920576 | tf_op jit(solution)/shard_map/reduce_scatter | solution.py:376
  7.2 8.4 collective-permute-start
  8.5 5.8 collective-permute-start.1
  14.4 1.2 collective-permute-start.2
  17.4 26.1 %copy-start.3 = (bf16[2,256,2304]{2,1,0:T(8,128)(2,1)}, bf16[2,256,2304]{2,1,0:T(8,128)(2,1)S(1)}, u32[]{:S(2)}) copy-start(bf16[2,256,2304]{2,1,0:T(8,128)(2,1)S(1)} %pad_maximum_fusion.1) | copy-start | bytes 7077892
  18.0 25.6 %copy-start.4 = (bf16[2,256,2304]{2,1,0:T(8,128)(2,1)}, bf16[2,256,2304]{2,1,0:T(8,128)(2,1)S(1)}, u32[]{:S(2)}) copy-start(bf16[2,256,2304]{2,1,0:T(8,128)(2,1)S(1)} %pad_maximum_fusion.2) | copy-start | bytes 7077892
  62.5 3.1 collective-permute-start.3
  123.4 2.0 copy-start.2
  123.5 513.9 %reduce-scatter.6.cloned.1.call-start = ((), (), s32[]{:S(2)}) async-start(), calls=%async_computation.5 | async-start | bytes 16920576 | tf_op jit(solution)/shard_map/reduce_scatter | solution.py:376
  142.5 4.6 collective-permute-start.4
  149.1 24.8 %copy-start.5 = (bf16[2,256,2304]{2,1,0:T(8,128)(2,1)S(1)}, bf16[2,256,2304]{2,1,0:T(8,128)(2,1)}, u32[]{:S(2)}) copy-start(bf16[2,256,2304]{2,1,0:T(8,128)(2,1)} %copy-done.4) | copy-start | bytes 7077892
  187.5 2.0 copy-start.1
  187.5 708.3 %reduce-scatter.4.cloned.1.call-start = ((), (), s32[]{:S(2)}) async-start(), calls=%async_computation.3 | async-start | bytes 16920576 | tf_op jit(solution)/shard_map/reduce_scatter | solution.py:376
  203.5 879.0 %all-gather.8.cloned.1.call-start = ((), (), s32[]{:S(2)}) async-start(), calls=%async_computation.8 | async-start | bytes 16920576 | tf_op jit(solution)/shard_map/all_gather | solution.py:377
  378.9 888.8 %all-gather.6.cloned.1.call-start = ((), (), s32[]{:S(2)}) async-start(), calls=%async_computation.6 | async-start | bytes 16920576 | tf_op jit(solution)/shard_map/all_gather | solution.py:377
  637.4 814.8 %all-gather.4.cloned.1.call-start = ((), (), s32[]{:S(2)}) async-start(), calls=%async_computation.4 | async-start | bytes 16920576 | tf_op jit(solution)/shard_map/all_gather | solution.py:377
  900.1 28.7 %collective-permute-start.5 = (bf16[2,3456]{1,0:T(2,128)(2,1)}, bf16[2,3456]{1,0:T(2,128)(2,1)S(1)}, u32[]{:S(2)}, u32[]{:S(2)}) collective-permute-start(bf16[2,3456]{1,0:T(2,128)(2,1)} %bitcast.86), channel_id=1, source_target_pairs={{2,0},{4,2},{6,4},{3,1},{5,3},{7,5},{10,8},{12,10},{14,12},{11,9},... | collective-permute-start | bytes 41480 | tf_op jit(solution)/shard_map/ppermute | solution.py:348
  963.1 2.2 copy-start
  963.1 2.2 copy-start.7
  963.2 2.2 copy-start.8
  965.3 81.2 %collective-permute-start.6 = (f32[512,1152]{1,0:T(8,128)S(1)}, f32[512,1152]{1,0:T(8,128)}, u32[]{:S(2)}, u32[]{:S(2)}) collective-permute-start(f32[512,1152]{1,0:T(8,128)S(1)} %slice_select_fusion), channel_id=1, source_target_pairs={{0,1},{1,0},{2,3},{3,2},{4,5},{5,4},{6,7},{7,6},{8,9},{9,8},{10,11... | collective-permute-start | bytes 7077896 | tf_op jit(solution)/shard_map/ppermute | solution.py:367
  1504.9 61.7 %copy-start.6 = (bf16[512,1152]{1,0:T(8,128)(2,1)S(1)}, bf16[512,1152]{1,0:T(8,128)(2,1)}, u32[]{:S(2)}) copy-start(bf16[512,1152]{1,0:T(8,128)(2,1)} %get-tuple-element.18) | copy-start | bytes 3538948
Sparse Core Ops, SparseCore 0:
  123.6 255.2 reduce-scatter.7
  385.2 252.0 reduce-scatter.5
  643.7 252.0 reduce-scatter.3
  898.5 184.0 all-gather.7
  1085.2 182.5 all-gather.5
  1270.3 181.7 all-gather.3
where the time goes:
time: 1590 us; the launch traced here: 1570 us
  waiting for transfers between devices  1020 us (64%)
  local copies, waits for them, and re-layouts  199 us (13%)
  matrix products  124 us (8%)
  blocking collectives  81 us (5%)
  Pallas kernels  71 us (4%)
  other arithmetic  52.3 us (3%)
    reduce_scatter x3, waiting for transfers between devices, reduce_weights(): lax.psum_scatter(partial.astype(BF16), ('dp', 'seq'), scatter_dimension=0...  692 us
    all_gather x3, waiting for transfers between devices, reduce_weights(): return lax.all_gather(shard, ('dp', 'seq'), axis=0, tiled=True).astype(F32)  325 us
    unnamed x25, local copies, waits for them, and re-layouts  110 us
    psum x1, blocking collectives, local(): lax.psum((jnp.sum(sums_one, 1), jnp.sum(sums_two, 1)), ('dp', 'seq'))  81 us
    all_gather x2, local copies, waits for them, and re-layouts, reduce_weights(): return lax.all_gather(shard, ('dp', 'seq'), axis=0, tiled=True).astype(F32)  43.4 us
    dot_general x3, matrix products, dot(): lax.dot_general(lhs, rhs, (dims, ((), ())), preferred_element_type=F32)  41.2 us
  transfers between devices with their start and end apart: 13, of which 9 were waited for; matrix products, arithmetic and copies ran while one was open for 12% of the time, Pallas kernels for 2%

commit v1 on v0

--- a/solution.py
+++ b/solution.py
@@ -11,6 +11,9 @@
 BF16 = jnp.bfloat16
 SUB = 8
 STEP = 16
+EDGE = 16
+PART = 64
+LAG = 1
 VMEM = pl.BlockSpec(memory_space=pltpu.VMEM)
 
 
@@ -191,6 +194,8 @@
 def grads_pass(seqs, tokens, channels, message, entering, upstream, keep, upd, fgt, out, state, scale, shift, grads, sums):
     steps = tokens // STEP
     sums[...] = jnp.zeros_like(sums)
+    if grads.shape[1] > 3 * channels:
+        grads[:, 3 * channels :] = jnp.zeros((grads.shape[0], grads.shape[1] - 3 * channels), BF16)
     for seq in range(seqs):
         for lanes in lane_blocks(channels):
             width = lanes.stop - lanes.start
@@ -252,7 +257,44 @@
     grads_pass(seqs, tokens, channels, message, entering, cotangent, keep, upd, fgt, out, state, back_scale, back_shift, grads, sums)
 
 
-def backward_kernel(seqs, tokens, channels, upstream, keep, upd, fgt, out, state, entering, grads, sums, message, scale, shift, summary, slots, send_sems, recv_sems):
+def pass_edges(seqs, tokens, grads, edges, arrived, edge_sems):
+    count = lax.axis_size("seq")
+    me = lax.axis_index("seq")
+    row = lax.broadcasted_iota(jnp.int32, edges.shape, 0)
+    firsts = jnp.zeros(edges.shape, F32)
+    for seq in range(seqs):
+        tile = grads[seq * tokens : seq * tokens + EDGE, :].astype(F32)
+        firsts = jnp.where(row == seq, pltpu.roll(tile, seq, 0) if seq else tile, firsts)
+    edges[...] = firsts.astype(BF16)
+    copy = pltpu.make_async_remote_copy(
+        src_ref=edges,
+        dst_ref=arrived,
+        send_sem=edge_sems.at[0],
+        recv_sem=edge_sems.at[1],
+        device_id={"seq": lax.rem(me + count - 1, count)},
+        device_id_type=pl.DeviceIdType.MESH,
+    )
+    rows = slice(seqs * tokens, seqs * tokens + EDGE)
+
+    @pl.when(me > 0)
+    def _():
+        copy.start()
+
+    @pl.when(me < count - 1)
+    def _():
+        copy.wait_recv()
+        grads[rows, :] = arrived[...]
+
+    @pl.when(me == count - 1)
+    def _():
+        grads[rows, :] = jnp.zeros(edges.shape, BF16)
+
+    @pl.when(me > 0)
+    def _():
+        copy.wait_send()
+
+
+def backward_kernel(seqs, tokens, channels, upstream, keep, upd, fgt, out, state, entering, grads, sums, message, scale, shift, summary, slots, send_sems, recv_sems, edges, arrived, edge_sems):
     greet("seq")
     back_pass(seqs, tokens, channels, upstream, keep, fgt, out, scale, shift, summary, 0)
     copies = to_all(summary, slots, send_sems, recv_sems, "seq")
@@ -260,6 +302,7 @@
         copy.wait()
     message[...] = from_later(slots, (seqs, channels), slice(0, seqs), slice(seqs, 2 * seqs), "seq")
     grads_pass(seqs, tokens, channels, message, entering, upstream, keep, upd, fgt, out, state, scale, shift, grads, sums)
+    pass_edges(seqs, tokens, grads, edges, arrived, edge_sems)
 
 
 def exchange_scratch(rows, channels):
@@ -303,7 +346,7 @@
     )(gates, bias, keep, initial)
 
 
-def pool_top(seqs, tokens, gates, bias, keep, initial, cotangent):
+def pool_top(seqs, tokens, lanes, gates, bias, keep, initial, cotangent):
     channels = gates.shape[2]
     rows = seqs * tokens
     whole = pltpu.VMEM((rows, channels), F32)
@@ -312,7 +355,7 @@
         functools.partial(top_kernel, seqs, tokens, channels),
         out_shape=(
             jax.ShapeDtypeStruct((rows, channels), BF16),
-            jax.ShapeDtypeStruct((rows, 3 * channels), BF16),
+            jax.ShapeDtypeStruct((rows, lanes), BF16),
             jax.ShapeDtypeStruct((3, SUB, channels), F32),
         ),
         in_specs=[VMEM] * 5,
@@ -324,22 +367,375 @@
     )(gates, bias, keep, initial, cotangent)
 
 
-def pool_backward(seqs, tokens, upstream, keep, upd, fgt, out, state, entering):
+def pool_backward(seqs, tokens, lanes, upstream, keep, upd, fgt, out, state, entering):
     rows, channels = upstream.shape
     whole = pltpu.VMEM((rows, channels), F32)
     return pl.pallas_call(
         functools.partial(backward_kernel, seqs, tokens, channels),
         out_shape=(
-            jax.ShapeDtypeStruct((rows, 3 * channels), BF16),
+            jax.ShapeDtypeStruct((rows + EDGE, lanes), BF16),
             jax.ShapeDtypeStruct((3, SUB, channels), F32),
         ),
         in_specs=[VMEM] * 7,
         out_specs=[VMEM] * 2,
-        scratch_shapes=[pltpu.VMEM((seqs, channels), F32)] + [whole] * 2 + exchange_scratch(2 * seqs, channels),
+        scratch_shapes=[pltpu.VMEM((seqs, channels), F32)]
+        + [whole] * 2
+        + exchange_scratch(2 * seqs, channels)
+        + [pltpu.VMEM((EDGE, lanes), BF16)] * 2
+        + [pltpu.SemaphoreType.DMA((2,))],
         compiler_params=params(3),
         cost_estimate=cost(rows * channels, 60, rows * channels * 26),
         name="pool_backward",
     )(upstream, keep, upd, fgt, out, state, entering)
+
+
+def spread_kernel(layers, parts, loads, sums, out, sums_out, own, ups, downs, acc, across, around, load_sems, up_sems, down_sems, line_send, line_recv, kept_sems, plane_send, plane_recv, sums_sems):
+    line, plane = lax.axis_size("seq"), lax.axis_size("dp")
+    at, here = lax.axis_index("seq"), lax.axis_index("dp")
+    unit = line * parts
+    depth = own.shape[0] // layers
+    units = own.shape[0] // unit
+    half = unit // 2
+    beside = here + 1 - 2 * lax.rem(here, 2)
+    below = lax.rem(here + 2, plane)
+    across_from = lax.rem(beside + 2, plane)
+
+    barrier = pltpu.get_barrier_semaphore()
+    for axis, me, count in (("seq", at, line), ("dp", here, plane)):
+        for step in range(1, count):
+            pl.semaphore_signal(
+                barrier, inc=1, device_id={axis: lax.rem(me + step, count)}, device_id_type=pl.DeviceIdType.MESH
+            )
+    pl.semaphore_wait(barrier, line + plane - 2)
+
+    def remote(src, dst, send, recv, axis, target):
+        return pltpu.make_async_remote_copy(
+            src_ref=src,
+            dst_ref=dst,
+            send_sem=send,
+            recv_sem=recv,
+            device_id={axis: target},
+            device_id_type=pl.DeviceIdType.MESH,
+        )
+
+    def load(layer):
+        return pltpu.make_async_copy(loads[layer], own.at[pl.ds(layer * depth, depth)], load_sems.at[layer])
+
+    def chunk(u, j):
+        return pl.ds(pl.multiple_of(u * unit + j * parts, parts), parts)
+
+    def up(src, u, j):
+        number = u * (line - 1) + j - 1
+        return remote(src, ups.at[u, j - 1], up_sems.at[0, number], up_sems.at[1, number], "seq", lax.rem(at + 1, line))
+
+    def down(src, u, j):
+        number = u * (line - 1) + j
+        return remote(
+            src, downs.at[u, j], down_sems.at[0, number], down_sems.at[1, number], "seq", lax.rem(at + line - 1, line)
+        )
+
+    def along(src, u, j, way, hop):
+        return remote(
+            src,
+            out.at[here, chunk(u, j)],
+            line_send.at[(u * 2 + way) * (line - 1) + hop],
+            line_recv.at[u * line + j],
+            "seq",
+            lax.rem(at + (1 if way == 0 else line - 1), line),
+        )
+
+    def keep(u):
+        return pltpu.make_async_copy(own.at[chunk(u, at)], out.at[here, chunk(u, at)], kept_sems.at[u])
+
+    def rows(u, first, count):
+        return pl.ds(pl.multiple_of(u * unit + first, half), count)
+
+    def over(u, way):
+        place = out.at[here, rows(u, 0, unit)]
+        return remote(place, place, plane_send.at[u * 4 + way], plane_recv.at[u * 4 + way], "dp", (beside, below)[way])
+
+    def onward(u, way):
+        place = out.at[(beside, below)[way], rows(u, way * half, half)]
+        return remote(
+            place, place, plane_send.at[u * 4 + 2 + way], plane_recv.at[u * 4 + 2 + way], "dp", (below, beside)[way]
+        )
+
+    def corner(u, way):
+        place = out.at[across_from, rows(u, way * half, half)]
+        return remote(place, place, plane_send.at[u * 4 + 2 + way], plane_recv.at[u * 4 + 2 + way], "dp", (below, beside)[way])
+
+    def sums_copy(slots, me, count, axis, number, step):
+        return remote(
+            slots.at[me],
+            slots.at[me],
+            sums_sems.at[number, 0, step - 1],
+            sums_sems.at[number, 1, step - 1],
+            axis,
+            lax.rem(me + step, count),
+        )
+
+    def sums_arrival(slots, me, count, axis, number, step):
+        place = slots.at[lax.rem(me + count - step, count)]
+        return remote(place, place, sums_sems.at[number, 0, step - 1], sums_sems.at[number, 1, step - 1], axis, lax.rem(me + step, count))
+
+    for layer in range(layers):
+        load(layer).start()
+    across[at] = sums[...]
+    for step in range(1, line):
+        sums_copy(across, at, line, "seq", 0, step).start()
+    load(0).wait()
+
+    def stage(index, none):
+        @pl.when(index == 1)
+        def _():
+            for layer in range(1, layers):
+                load(layer).wait()
+            for step in range(1, line):
+                sums_arrival(across, at, line, "seq", 0, step).wait_recv()
+            total = across[0]
+            for other in range(1, line):
+                total = total + across[other]
+            around[here] = total
+            for step in range(1, plane):
+                sums_copy(around, here, plane, "dp", 1, step).start()
+
+        @pl.when(index == 3)
+        def _():
+            for step in range(1, plane):
+                sums_arrival(around, here, plane, "dp", 1, step).wait_recv()
+            total = around[0]
+            for other in range(1, plane):
+                total = total + around[other]
+            sums_out[...] = total
+
+        u = index - at
+
+        @pl.when((u >= 0) & (u < units))
+        def _():
+            for j in range(1, line):
+
+                @pl.when(at == 0)
+                def _(j=j):
+                    up(own.at[chunk(u, j)], u, j).start()
+
+                @pl.when((at > 0) & (at <= j))
+                def _(j=j):
+                    up(ups.at[u, j - 1], u, j).wait_recv()
+
+                @pl.when((at > 0) & (at < j))
+                def _(j=j):
+                    ups[u, j - 1] = (ups[u, j - 1].astype(F32) + own[chunk(u, j)].astype(F32)).astype(BF16)
+                    up(ups.at[u, j - 1], u, j).start()
+
+        v = index - (line - 1 - at)
+
+        @pl.when((v >= 0) & (v < units))
+        def _():
+            for j in range(line - 1):
+
+                @pl.when(at == line - 1)
+                def _(j=j):
+                    down(own.at[chunk(v, j)], v, j).start()
+
+                @pl.when((at < line - 1) & (at >= j))
+                def _(j=j):
+                    down(downs.at[v, j], v, j).wait_recv()
+
+                @pl.when((at < line - 1) & (at > j))
+                def _(j=j):
+                    downs[v, j] = (downs[v, j].astype(F32) + own[chunk(v, j)].astype(F32)).astype(BF16)
+                    down(downs.at[v, j], v, j).start()
+
+        w = index - (line - 1)
+
+        @pl.when((w >= 0) & (w < units))
+        def _():
+            acc[...] = own[chunk(w, at)].astype(F32)
+
+            @pl.when(at > 0)
+            def _():
+                acc[...] += ups[w, at - 1].astype(F32)
+
+            @pl.when(at < line - 1)
+            def _():
+                acc[...] += downs[w, at].astype(F32)
+
+            own[chunk(w, at)] = acc[...].astype(BF16)
+            keep(w).start()
+
+            @pl.when(at < line - 1)
+            def _():
+                along(own.at[chunk(w, at)], w, at, 0, 0).start()
+
+            @pl.when(at > 0)
+            def _():
+                along(own.at[chunk(w, at)], w, at, 1, 0).start()
+
+        for hop in range(1, line):
+            x = index - (line - 1) - hop
+
+            @pl.when((x >= 0) & (x < units))
+            def _(x=x, hop=hop):
+                @pl.when(at >= hop)
+                def _():
+                    src = out.at[here, chunk(x, at - hop)]
+                    along(src, x, at - hop, 0, 0).wait_recv()
+                    if hop < line - 1:
+
+                        @pl.when(at < line - 1)
+                        def _():
+                            along(src, x, at - hop, 0, hop).start()
+
+                @pl.when(at + hop < line)
+                def _():
+                    src = out.at[here, chunk(x, at + hop)]
+                    along(src, x, at + hop, 1, 0).wait_recv()
+                    if hop < line - 1:
+
+                        @pl.when(at > 0)
+                        def _():
+                            along(src, x, at + hop, 1, hop).start()
+
+        y = index - 2 * (line - 1)
+
+        @pl.when((y >= 0) & (y < units))
+        def _():
+            keep(y).wait()
+            over(y, 0).start()
+            over(y, 1).start()
+
+        z = y - LAG
+
+        @pl.when((z >= 0) & (z < units))
+        def _():
+            for way in range(2):
+                place = out.at[(beside, below)[way], rows(z, 0, unit)]
+                remote(place, place, plane_send.at[z * 4 + way], plane_recv.at[z * 4 + way], "dp", (beside, below)[way]).wait_recv()
+                onward(z, way).start()
+
+        t = z - LAG
+
+        @pl.when((t >= 0) & (t < units))
+        def _():
+            for way in range(2):
+                corner(t, way).wait_recv()
+
+        return none
+
+    lax.fori_loop(0, units + 2 * (line - 1) + 2 * LAG, stage, 0)
+
+    def settle(u, none):
+        for j in range(1, line):
+
+            @pl.when(at < j)
+            def _(j=j):
+                up(ups.at[u, j - 1], u, j).wait_send()
+
+        for j in range(line - 1):
+
+            @pl.when(at > j)
+            def _(j=j):
+                down(downs.at[u, j], u, j).wait_send()
+
+        for hop in range(line - 1):
+
+            @pl.when((at >= hop) & (at < line - 1))
+            def _(hop=hop):
+                along(out.at[here, chunk(u, at - hop)], u, at - hop, 0, hop).wait_send()
+
+            @pl.when((at + hop < line) & (at > 0))
+            def _(hop=hop):
+                along(out.at[here, chunk(u, at + hop)], u, at + hop, 1, hop).wait_send()
+
+        for way in range(2):
+            over(u, way).wait_send()
+            onward(u, way).wait_send()
+        return none
+
+    lax.fori_loop(0, units, settle, 0)
+    for step in range(1, line):
+        sums_copy(across, at, line, "seq", 0, step).wait_send()
+    for step in range(1, plane):
+        sums_copy(around, here, plane, "dp", 1, step).wait_send()
+
+
+def spread(partials, sums):
+    line, plane = lax.axis_size("seq"), lax.axis_size("dp")
+    layers = len(partials)
+    depth, width = partials[0].shape
+    units = layers * depth // (line * PART)
+
+    def kernel(*refs):
+        spread_kernel(layers, PART, refs[:layers], *refs[layers:])
+
+    dma = pltpu.SemaphoreType.DMA
+    return pl.pallas_call(
+        kernel,
+        out_shape=(
+            jax.ShapeDtypeStruct((plane, layers * depth, width), BF16),
+            jax.ShapeDtypeStruct(sums.shape, F32),
+        ),
+        in_specs=[pl.BlockSpec(memory_space=pl.ANY)] * layers + [VMEM],
+        out_specs=[pl.BlockSpec(memory_space=pl.ANY), VMEM],
+        scratch_shapes=[
+            pltpu.VMEM((layers * depth, width), BF16),
+            pltpu.VMEM((units, line - 1, PART, width), BF16),
+            pltpu.VMEM((units, line - 1, PART, width), BF16),
+            pltpu.VMEM((PART, width), F32),
+            pltpu.VMEM((line,) + sums.shape, F32),
+            pltpu.VMEM((plane,) + sums.shape, F32),
+            dma((layers,)),
+            dma((2, units * (line - 1))),
+            dma((2, units * (line - 1))),
+            dma((units * 2 * (line - 1),)),
+            dma((units * line,)),
+            dma((units,)),
+            dma((units * 4,)),
+            dma((units * 4,)),
+            dma((2, 2, max(line, plane) - 1)),
+        ],
+        compiler_params=params(4),
+        cost_estimate=pl.CostEstimate(flops=0, bytes_accessed=layers * depth * width * 16, transcendentals=0),
+        name="spread",
+    )(*partials, sums)
+
+
+def widen_kernel(tiles, blocks, given, out):
+    per = given.shape[2] // 128
+    for tile in range(tiles * blocks):
+        source, place = divmod(tile, per)
+        gate, column = divmod(tile, blocks)
+        out[0, gate, :, column * 128 : column * 128 + 128] = given[
+            source, :, place * 128 : place * 128 + 128
+        ].astype(F32)
+
+
+def widen(gathered, first, layers, depth, channels):
+    plane, _, width = gathered.shape
+    rows = 128
+    steps = depth // rows
+    return pl.pallas_call(
+        functools.partial(widen_kernel, 3, channels // 128),
+        grid=(layers, steps),
+        out_shape=jax.ShapeDtypeStruct((layers, 3, depth, channels), F32),
+        in_specs=[pl.BlockSpec((plane, rows, width), lambda layer, step: (0, (first + layer) * steps + step, 0))],
+        out_specs=pl.BlockSpec((1, 3, rows, channels), lambda layer, step: (layer, 0, step, 0)),
+        compiler_params=pltpu.CompilerParams(vmem_limit_bytes=32 * 2**20),
+        name="widen",
+    )(gathered)
+
+
+def around_plane(value, steps):
+    return lax.ppermute(value, "dp", [(at, at ^ steps) for at in range(4)])
+
+
+def to_owners(grads, width):
+    here = lax.axis_index("dp")
+    blocks = []
+    for steps, owner in enumerate((here, here + 1 - 2 * lax.rem(here, 2), lax.rem(here + 2, 4), 3 - here)):
+        block = lax.dynamic_slice(grads, (0, owner * width), (grads.shape[0], width))
+        blocks.append(around_plane(block, steps) if steps else block)
+    return blocks
 
 
 def shifted(value, axis, steps):
@@ -396,36 +792,62 @@
     hidden, upd, fgt, out, state, entering = pool_forward(seqs, tokens, gates_one, bias_one, keep, init_state[0])
     full_hidden = gather_channels(hidden)
     gates_two = jnp.einsum("td,gdc->gtc", full_hidden, mix, preferred_element_type=F32)
+    line, plane = lax.axis_size("seq"), lax.axis_size("dp")
+    tiles = 3 * channels // 128
+    spreads = plane == 4 and channels % 128 == 0 and width % (line * PART) == 0 and line > 1
+    block = -(-tiles // plane) * 128
+    lanes = plane * block if spreads else 3 * channels
     pooled_two, grad_two, sums_two = pool_top(
-        seqs, tokens, gates_two, bias_two, keep, init_state[1], cotangent.reshape(rows, channels)
+        seqs, tokens, lanes, gates_two, bias_two, keep, init_state[1], cotangent.reshape(rows, channels)
     )
     hidden_terms = jnp.einsum(
-        "tgc,gdc->td", grad_two.reshape(rows, 3, channels), mix, preferred_element_type=F32
+        "tgc,gdc->td", grad_two[:, : 3 * channels].reshape(rows, 3, channels), mix, preferred_element_type=F32
     )
     hidden_grad = sum_channels(hidden_terms)
-    grad_one, sums_one = pool_backward(seqs, tokens, hidden_grad, keep, upd, fgt, out, state, entering)
-    weight_two_grad = dot(full_hidden, grad_two, ((0,), (0,)))
-    weight_two_grad = reduce_weights(weight_two_grad)
-    next_first = shifted(grad_one.reshape(seqs, tokens, -1)[:, 0], "seq", -1)
-    following = jnp.concatenate([grad_one.reshape(seqs, tokens, -1)[:, 1:], next_first[:, None]], 1).reshape(rows, -1)
-    weight_one_grad = jnp.stack(
-        [
-            reduce_weights(dot(full, grad_one, ((0,), (0,)))),
-            reduce_weights(dot(previous, grad_one, ((0,), (0,)))),
-        ]
-    )
+    extended, sums_one = pool_backward(seqs, tokens, lanes, hidden_grad, keep, upd, fgt, out, state, entering)
+    grad_one = extended[:rows, : 3 * channels]
     input_terms = jnp.einsum(
-        "tgc,gdc->td", grad_one.reshape(rows, 3, channels), taps[0], preferred_element_type=F32
-    ) + jnp.einsum("tgc,gdc->td", following.reshape(rows, 3, channels), taps[1], preferred_element_type=F32)
-    input_grad = sum_channels(input_terms)
-    bias_one_grad, bias_two_grad = lax.psum((jnp.sum(sums_one, 1), jnp.sum(sums_two, 1)), ("dp", "seq"))
+        "tgc,kgdc->ktd", grad_one.reshape(rows, 3, channels), taps, preferred_element_type=F32
+    ).reshape(2, seqs, tokens, width)
+    late = input_terms[1]
+    late = jnp.concatenate([late[:, 1:], shifted(late[:, 0], "seq", -1)[:, None]], 1)
+    input_grad = sum_channels((input_terms[0] + late).reshape(rows, width))
+    sums = jnp.concatenate([jnp.sum(sums_one, 1), jnp.sum(sums_two, 1)])
+    if spreads:
+        every = [full] + [around_plane(full, steps) for steps in range(1, 4)]
+        every_hidden = [full_hidden] + [around_plane(full_hidden, steps) for steps in range(1, 4)]
+        blocks_two = to_owners(grad_two, block)
+        blocks_one = to_owners(extended, block)
+        partial_two = dot(jnp.concatenate(every_hidden), jnp.concatenate(blocks_two), ((0,), (0,))).astype(BF16)
+        every = jnp.concatenate(every)
+        partial_one = dot(every, jnp.concatenate([given[:rows] for given in blocks_one]), ((0,), (0,))).astype(BF16)
+        following = []
+        for given in blocks_one:
+            for seq in range(seqs):
+                following += [
+                    given[seq * tokens + 1 : seq * tokens + tokens],
+                    given[rows + seq : rows + seq + 1],
+                ]
+        partial_late = dot(every, jnp.concatenate(following), ((0,), (0,))).astype(BF16)
+        gathered, sums = spread([partial_two, partial_one, partial_late], sums)
+        weight_two_grad = widen(gathered, 0, 1, width, channels)[0].transpose(1, 0, 2)
+        weight_one_grad = widen(gathered, 1, 2, width, channels).transpose(0, 2, 1, 3)
+    else:
+        sums = lax.psum(sums, ("dp", "seq"))
+        weight_two_grad = reduce_weights(dot(full_hidden, grad_two, ((0,), (0,)))).reshape(width, 3, channels)
+        weight_one_grad = jnp.stack(
+            [
+                reduce_weights(dot(full, grad_one, ((0,), (0,)))),
+                reduce_weights(dot(previous, grad_one, ((0,), (0,)))),
+            ]
+        ).reshape(2, width, 3, channels)
     return (
         pooled_two.reshape(seqs, tokens, channels),
         input_grad.reshape(seqs, tokens, channels),
-        weight_one_grad.reshape(2, width, 3, channels),
-        bias_one_grad,
-        weight_two_grad.reshape(width, 3, channels),
-        bias_two_grad,
+        weight_one_grad,
+        sums[:3],
+        weight_two_grad,
+        sums[3:],
     )
 
 

time: 1590 us -> 1050 us (0.66)
  waiting for transfers between devices: 1020 us -> 203 us
  Pallas kernels: 71 us -> 600 us
  local copies, waits for them, and re-layouts: 199 us -> 70.7 us
  blocking collectives: 81 us -> 0 us
  other arithmetic: 52.3 us -> 19.9 us
    reduce_scatter x3 -> x0, waiting for transfers between devices: 692 us -> none  [reduce_weights(): lax.psum_scatter(partial.astype(BF16), ('dp', 'seq'), scatter_dimension=0...]
    pallas_call x0 -> x3, Pallas kernels: none -> 527 us  [the longest x1 467 us: spread(): pl.pallas_call(kernel, out_shape=(jax.ShapeDtypeStruct((plane, layers * d...]
    all_gather x3 -> x0, waiting for transfers between devices: 325 us -> none  [reduce_weights(): return lax.all_gather(shard, ('dp', 'seq'), axis=0, tiled=True).astype(F32)]
    ppermute x0 -> x12, waiting for transfers between devices: none -> 200 us  [around_plane(): return lax.ppermute(value, 'dp', [(at, at ^ steps) for at in range(4)])]
    unnamed x25 -> x50, local copies, waits for them, and re-layouts: 110 us -> 6.74 us
    psum x1 -> x0, blocking collectives: 81 us -> none  [local(): lax.psum((jnp.sum(sums_one, 1), jnp.sum(sums_two, 1)), ('dp', 'seq'))]
    all_gather x2 -> x0, local copies, waits for them, and re-layouts: 43.4 us -> none  [reduce_weights(): return lax.all_gather(shard, ('dp', 'seq'), axis=0, tiled=True).astype(F32)]
    another operation x1 -> x0, other arithmetic: 31 us -> none  [local(): jnp.stack([reduce_weights(dot(full, grad_one, ((0,), (0,)))), reduce_weig...]
  transfers between devices with their start and end apart: 13 -> 19, of which waited for: 9 -> 6; matrix products, arithmetic and copies ran while one was open for 12% -> 13% of each run, Pallas kernels for 2% -> 53%
where the time goes in v1:
time: 1050 us; the launch traced here: 1040 us
  Pallas kernels  600 us (57%)
  waiting for transfers between devices  203 us (19%)
  matrix products  122 us (12%)
  local copies, waits for them, and re-layouts  70.7 us (7%)
  starting transfers between devices  20.6 us (2%)
  other arithmetic  19.9 us (2%)
    pallas_call x1, Pallas kernels, spread(): pl.pallas_call(kernel, out_shape=(jax.ShapeDtypeStruct((plane, layers * d...  467 us
    ppermute x12, waiting for transfers between devices, around_plane(): return lax.ppermute(value, 'dp', [(at, at ^ steps) for at in range(4)])  200 us
    pallas_call x2, Pallas kernels, widen(): pl.pallas_call(functools.partial(widen_kernel, 3, channels // 128), grid=...  59.9 us
    dot_general x3, matrix products, dot(): lax.dot_general(lhs, rhs, (dims, ((), ())), preferred_element_type=F32)  43.8 us
    concatenate x1, local copies, waits for them, and re-layouts, local(): jnp.concatenate(following)  30.4 us
    pallas_call x1, Pallas kernels, pool_top(): pl.pallas_call(functools.partial(top_kernel, seqs, tokens, channels), out...  28.1 us
    pallas_call x1, Pallas kernels, pool_backward(): pl.pallas_call(functools.partial(backward_kernel, seqs, tokens, channels)...  27.7 us
    dot_general x1, matrix products, local(): jnp.einsum('tkd,kgdc->gtc', both.reshape(rows, 2, width), taps, preferred...  25.1 us
  transfers between devices with their start and end apart: 19, of which 6 were waited for; matrix products, arithmetic and copies ran while one was open for 13% of the time, Pallas kernels for 53%

profile of v1, /device:TPU:0, one launch (start us, length us, event | category | flops | bytes accessed | tf_op | source)
XLA Modules:
  0.0 1037.7 jit_solution(11688191865217903730)
XLA Ops:
  1.9 4.5 collective-permute-start.1
  12.8 25.1 %fusion.24.gates = f32[3,512,1152]{2,1,0:T(8,128)} fusion(bf16[2,2304,3,1152]{3,1,2,0:T(8,128)(2,1)} %param.11, bf16[512,1,2304]{2,0,1:T(8,128)(2,1)S(1)} %bitcast.91, bf16[512,1,2304]{2,0,1:T(8,128)(2,1)} %bitcast), kind=kOutput, calls=%fused_computation.23 | convolution fusion | flops 16316891136 | bytes 43646976 | tf_op jit(solution)/shard_map/tkd,kgdc->gtc/dot_general | solution.py:789
  38.7 18.1 %pool_forward.1 = (bf16[512,1152]{1,0:T(8,128)(2,1)}, f32[512,1152]{1,0:T(8,128)}, f32[512,1152]{1,0:T(8,128)}, f32[512,1152]{1,0:T(8,128)}, f32[512,1152]{1,0:T(8,128)}, /*index=5*/f32[2,1152]{1,0:T(2,128)}) custom-call(f32[3,512,1152]{2,1,0:T(8,128)} %fusion.24.gates, f32[3,1152]{1,0:T(4,128)} %bias.2, f32[512,128]{1,0:T(8,128)} %broadcast_in_dim.15.keep, ...), custom_call_target="tpu_custom_call" | custom-call | flops 35389440 | bytes 17694720 | tf_op jit(solution)/shard_map/pool_forward/pallas_call | solution.py:330
  56.9 3.0 collective-permute-done.3
  61.5 15.4 %fusion.27.gates = f32[3,512,1152]{2,1,0:T(8,128)} fusion(bf16[2304,3,1152]{2,0,1:T(8,128)(2,1)} %param.13, bf16[512,1152]{1,0:T(8,128)(2,1)S(1)} %get-tuple-element.44, bf16[512,1152]{1,0:T(8,128)(2,1)S(1)} %get-tuple-element.43), kind=kOutput, calls=%fused_computation.24 | convolution fusion | flops 8158445568 | bytes 25362432 | tf_op jit(solution)/shard_map/td,gdc->gtc/dot_general | solution.py:794
  76.9 28.1 %pool_top.1 = (bf16[512,1152]{1,0:T(8,128)(2,1)}, bf16[512,3584]{1,0:T(8,128)(2,1)}, f32[3,8,1152]{2,1,0:T(8,128)}) custom-call(f32[3,512,1152]{2,1,0:T(8,128)} %fusion.27.gates, f32[3,1152]{1,0:T(4,128)} %bias.3, f32[512,128]{1,0:T(8,128)} %broadcast_in_dim.15.keep, f32[2,1152]{1,0:T(2,128)} %get-tuple-element.61.initial, bf16[512,1152]{1,0:T(8,128)(2,1)} %bitcast.94), custom_call_target="tpu_custom_call" | custom-call | flops 70778880 | bytes 12976128 | tf_op jit(solution)/shard_map/pool_top/pallas_call | solution.py:354
  105.0 2.2 slice.114
  107.3 3.6 copy.28
  110.9 13.0 %fusion.30 = f32[512,2304]{1,0:T(8,128)S(1)} fusion(bf16[512,3,1152]{0,2,1:T(8,128)(2,1)} %bitcast.90, bf16[2304,3,1152]{2,0,1:T(8,128)(2,1)} %param.13), kind=kOutput, calls=%fused_computation.25 | convolution fusion | flops 8153726976 | bytes 24182784 | tf_op jit(solution)/shard_map/tgc,gdc->td/dot_general | solution.py:803
  123.9 2.2 copy-done.1
  126.4 4.1 constant_dynamic-slice_fusion.7
  130.5 2.4 collective-permute-start.12
  135.6 2.4 collective-permute-start.9
  139.2 4.8 select_add_fusion.1.upstream
  144.0 27.7 %pool_backward.1 = (bf16[528,3584]{1,0:T(8,128)(2,1)}, f32[3,8,1152]{2,1,0:T(8,128)}) custom-call(f32[512,1152]{1,0:T(8,128)} %select_add_fusion.1.upstream, f32[512,128]{1,0:T(8,128)} %broadcast_in_dim.15.keep, f32[512,1152]{1,0:T(8,128)} %get-tuple-element.22.upd, f32[512,1152]{1,0:T(8,128)} %get-tuple-element.23.fgt, f32[512,1152]{1,0:T(8,128)} %get-tuple-element.24.out, ...), custom_call_target="tpu_custom_call" | custom-call | flops 35389440 | bytes 15335424 | tf_op jit(solution)/shard_map/pool_backward/pallas_call | solution.py:373
  171.7 2.2 slice.117
  173.9 3.6 copy.30
  178.1 24.4 %fusion.18 = f32[2,512,2304]{2,1,0:T(8,128)} fusion(bf16[512,3,1152,1]{0,2,1,3:T(8,128)(2,1)} %bitcast.89, bf16[2,2304,3,1152]{3,1,2,0:T(8,128)(2,1)} %param.11), kind=kOutput, calls=%fused_computation.19 | convolution fusion | flops 16307453952 | bytes 44826624 | tf_op jit(solution)/shard_map/tgc,kgdc->ktd/dot_general | solution.py:809
  202.5 2.8 slice.151
  210.7 64.5 %collective-permute-done.11 = bf16[512,896]{1,0:T(8,128)(2,1)} collective-permute-done((bf16[512,896]{1,0:T(8,128)(2,1)}, bf16[512,896]{1,0:T(8,128)(2,1)}, u32[]{:S(2)}, u32[]{:S(2)}) %collective-permute-start.11) | collective-permute-done | bytes 917536 | tf_op jit(solution)/shard_map/ppermute | solution.py:729
  275.2 2.4 collective-permute-start.15
  281.5 15.6 %fusion.21.refs_0_ = bf16[2304,896]{1,0:T(8,128)(2,1)} fusion(bf16[512,2304]{1,0:T(8,128)(2,1)} %collective-permute-done.9, bf16[512,2304]{1,0:T(8,128)(2,1)} %collective-permute-done.8, bf16[512,2304]{1,0:T(8,128)(2,1)} %collective-permute-done.7, bf16[512,1152]{1,0:T(8,128)(2,1)} %copy-done.5, bf16[512,1152]{1,0:T(8,128)(2,1)} %copy-done.3, ...), kind=kOutput, calls=%fused_computation.20 | convolution fusion | flops 8519647232 | bytes 17235968 | tf_op jit(solution)/shard_map/dot_general | solution.py:768
  302.7 98.7 %collective-permute-done.16 = bf16[528,896]{1,0:T(8,128)(2,1)} collective-permute-done((bf16[528,896]{1,0:T(8,128)(2,1)}, bf16[528,896]{1,0:T(8,128)(2,1)}, u32[]{:S(2)}, u32[]{:S(2)}) %collective-permute-start.16) | collective-permute-done | bytes 946208 | tf_op jit(solution)/shard_map/ppermute | solution.py:729
  404.5 16.3 %collective-permute-done.18 = bf16[528,896]{1,0:T(8,128)(2,1)S(1)} collective-permute-done((bf16[528,896]{1,0:T(8,128)(2,1)S(1)}, bf16[528,896]{1,0:T(8,128)(2,1)S(1)}, u32[]{:S(2)}, u32[]{:S(2)}) %collective-permute-start.18) | collective-permute-done | bytes 946208 | tf_op jit(solution)/shard_map/ppermute | solution.py:729
  420.8 20.2 %collective-permute-done.17 = bf16[528,896]{1,0:T(8,128)(2,1)S(1)} collective-permute-done((bf16[528,896]{1,0:T(8,128)(2,1)S(1)}, bf16[528,896]{1,0:T(8,128)(2,1)S(1)}, u32[]{:S(2)}, u32[]{:S(2)}) %collective-permute-start.17) | collective-permute-done | bytes 946208 | tf_op jit(solution)/shard_map/ppermute | solution.py:729
  444.9 30.4 %concatenate.56 = bf16[2048,896]{1,0:T(8,128)(2,1)} concatenate(bf16[255,896]{1,0:T(8,128)(2,1)} %get-tuple-element.35, bf16[1,896]{1,0:T(2,128)(2,1)S(1)} %get-tuple-element.33, bf16[255,896]{1,0:T(8,128)(2,1)} %get-tuple-element.34, bf16[1,896]{1,0:T(2,128)(2,1)S(1)} %get-tuple-element.32, bf16[255,896]{1,0:T(8,128)(2,1)S(1)} %get-tuple-element.58, ...), dimensions={0} | concatenate | bytes 7340032 | tf_op jit(solution)/shard_map/concatenate | solution.py:831
  477.6 14.2 %convolution_convert_fusion.refs_2_ = bf16[2304,896]{1,0:T(8,128)(2,1)} fusion(bf16[2048,896]{1,0:T(8,128)(2,1)S(1)} %copy-done.7, bf16[512,2304]{1,0:T(8,128)(2,1)} %collective-permute-done.15, bf16[512,2304]{1,0:T(8,128)(2,1)} %collective-permute-done.14, bf16[512,2304]{1,0:T(8,128)(2,1)} %collective-permute-done.13, bf16[512,2304]{1,0:T(8,128)(2,1)} %bitcast.28), kind=kOutput, calls=%fused_computation.21 | convolution fusion | flops 8495529984 | bytes 17235968 | tf_op jit(solution)/shard_map/dot_general | solution.py:768
  491.8 14.0 %convolution_convert_fusion.1.refs_1_ = bf16[2304,896]{1,0:T(8,128)(2,1)} fusion(bf16[512,896]{1,0:T(8,128)(2,1)S(1)} %slice-done.5, bf16[512,896]{1,0:T(8,128)(2,1)S(1)} %slice-done.6, bf16[512,896]{1,0:T(8,128)(2,1)S(1)} %slice.156, bf16[512,896]{1,0:T(8,128)(2,1)S(1)} %copy-done.13, bf16[512,2304]{1,0:T(8,128)(2,1)} %collective-permute-done.15, ...), kind=kOutput, calls=%fused_computation.22 | convolution fusion | flops 8510210048 | bytes 17235968 | tf_op jit(solution)/shard_map/dot_general | solution.py:768
  505.8 466.6 %spread.1 = (bf16[4,6912,896]{2,1,0:T(8,128)(2,1)}, f32[6,1152]{1,0:T(8,128)}) custom-call(bf16[2304,896]{1,0:T(8,128)(2,1)} %fusion.21.refs_0_, bf16[2304,896]{1,0:T(8,128)(2,1)} %convolution_convert_fusion.1.refs_1_, bf16[2304,896]{1,0:T(8,128)(2,1)} %convolution_convert_fusion.refs_2_, f32[6,1152]{1,0:T(8,128)} %pad_maximum_fusion.7.refs_3_), custom_call_target="tpu_custom_call" | custom-call | bytes 99090432 | tf_op jit(solution)/shard_map/spread/pallas_call | solution.py:672
  972.4 21.0 %widen.3 = f32[1,3,2304,1152]{3,2,1,0:T(8,128)} custom-call(bf16[4,6912,896]{2,1,0:T(8,128)(2,1)} %get-tuple-element.30.given), custom_call_target="tpu_custom_call" | custom-call | tf_op jit(solution)/shard_map/widen/pallas_call | solution.py:717
  993.4 39.0 %widen.2 = f32[2,3,2304,1152]{3,2,1,0:T(8,128)} custom-call(bf16[4,6912,896]{2,1,0:T(8,128)(2,1)} %get-tuple-element.30.given), custom_call_target="tpu_custom_call" | custom-call | tf_op jit(solution)/shard_map/widen/pallas_call | solution.py:717
  1033.0 3.5 select_add_fusion
  (119 shorter events, 40.3 us)
Async XLA Ops:
  0.6 8.4 collective-permute-start
  1.9 5.8 collective-permute-start.1
  7.8 1.2 collective-permute-start.2
  56.8 3.1 collective-permute-start.3
  61.4 15.5 %copy-start.3 = (bf16[512,1152]{1,0:T(8,128)(2,1)}, bf16[512,1152]{1,0:T(8,128)(2,1)S(1)}, u32[]{:S(2)}) copy-start(bf16[512,1152]{1,0:T(8,128)(2,1)S(1)} %get-tuple-element.43) | copy-start | bytes 3538948
  61.4 15.4 %copy-start.5 = (bf16[512,1152]{1,0:T(8,128)(2,1)}, bf16[512,1152]{1,0:T(8,128)(2,1)S(1)}, u32[]{:S(2)}) copy-start(bf16[512,1152]{1,0:T(8,128)(2,1)S(1)} %get-tuple-element.44) | copy-start | bytes 3538948
  126.3 12.4 %collective-permute-start.4 = (f32[512,1152]{1,0:T(8,128)S(1)}, f32[512,1152]{1,0:T(8,128)}, u32[]{:S(2)}, u32[]{:S(2)}) collective-permute-start(f32[512,1152]{1,0:T(8,128)S(1)} %slice_select_fusion.1), channel_id=1, source_target_pairs={{0,1},{1,0},{2,3},{3,2},{4,5},{5,4},{6,7},{7,6},{8,9},{9,8},{10,11... | collective-permute-start | bytes 7077896 | tf_op jit(solution)/shard_map/ppermute | solution.py:763
  130.5 47.0 %collective-permute-start.12 = (bf16[512,896]{1,0:T(8,128)(2,1)}, bf16[512,896]{1,0:T(8,128)(2,1)}, u32[]{:S(2)}, u32[]{:S(2)}) collective-permute-start(bf16[512,896]{1,0:T(8,128)(2,1)} %get-tuple-element.40), channel_id=1, source_target_pairs={{0,24},{8,16},{16,8},{24,0},{1,25},{9,17},{17,9},{25,1},{2,26},{10... | collective-permute-start | bytes 2752520 | tf_op jit(solution)/shard_map/ppermute | solution.py:729
  134.5 143.7 %collective-permute-start.8 = (bf16[512,2304]{1,0:T(8,128)(2,1)}, bf16[512,2304]{1,0:T(8,128)(2,1)}, u32[]{:S(2)}, u32[]{:S(2)}) collective-permute-start(bf16[512,2304]{1,0:T(8,128)(2,1)} %pad_maximum_fusion.4), channel_id=1, source_target_pairs={{0,16},{8,24},{16,0},{24,8},{1,17},{9,25},{17,1},{25,9},{2,18},{10... | collective-permute-start | bytes 7077896 | tf_op jit(solution)/shard_map/ppermute | solution.py:729
  135.0 143.7 %collective-permute-start.7 = (bf16[512,2304]{1,0:T(8,128)(2,1)}, bf16[512,2304]{1,0:T(8,128)(2,1)}, u32[]{:S(2)}, u32[]{:S(2)}) collective-permute-start(bf16[512,2304]{1,0:T(8,128)(2,1)} %pad_maximum_fusion.4), channel_id=1, source_target_pairs={{0,8},{8,0},{16,24},{24,16},{1,9},{9,1},{17,25},{25,17},{2,10},{10... | collective-permute-start | bytes 7077896 | tf_op jit(solution)/shard_map/ppermute | solution.py:729
  135.6 144.6 %collective-permute-start.9 = (bf16[512,2304]{1,0:T(8,128)(2,1)}, bf16[512,2304]{1,0:T(8,128)(2,1)}, u32[]{:S(2)}, u32[]{:S(2)}) collective-permute-start(bf16[512,2304]{1,0:T(8,128)(2,1)} %pad_maximum_fusion.4), channel_id=1, source_target_pairs={{0,24},{8,16},{16,8},{24,0},{1,25},{9,17},{17,9},{25,1},{2,26},{10... | collective-permute-start | bytes 7077896 | tf_op jit(solution)/shard_map/ppermute | solution.py:729
  138.7 136.6 %collective-permute-start.11 = (bf16[512,896]{1,0:T(8,128)(2,1)}, bf16[512,896]{1,0:T(8,128)(2,1)}, u32[]{:S(2)}, u32[]{:S(2)}) collective-permute-start(bf16[512,896]{1,0:T(8,128)(2,1)} %get-tuple-element.41), channel_id=1, source_target_pairs={{0,16},{8,24},{16,0},{24,8},{1,17},{9,25},{17,1},{25,9},{2,18},{10... | collective-permute-start | bytes 2752520 | tf_op jit(solution)/shard_map/ppermute | solution.py:729
  177.5 100.1 %collective-permute-start.10 = (bf16[512,896]{1,0:T(8,128)(2,1)}, bf16[512,896]{1,0:T(8,128)(2,1)}, u32[]{:S(2)}, u32[]{:S(2)}) collective-permute-start(bf16[512,896]{1,0:T(8,128)(2,1)} %get-tuple-element.42), channel_id=1, source_target_pairs={{0,8},{8,0},{16,24},{24,16},{1,9},{9,1},{17,25},{25,17},{2,10},{10... | collective-permute-start | bytes 2752520 | tf_op jit(solution)/shard_map/ppermute | solution.py:729
  178.1 24.4 %copy-start.15 = (f32[3,8,1152]{2,1,0:T(8,128)S(1)}, f32[3,8,1152]{2,1,0:T(8,128)}, u32[]{:S(2)}) copy-start(f32[3,8,1152]{2,1,0:T(8,128)} %get-tuple-element.28) | copy-start | bytes 331780
  275.2 201.6 %collective-permute-start.15 = (bf16[512,2304]{1,0:T(8,128)(2,1)}, bf16[512,2304]{1,0:T(8,128)(2,1)}, u32[]{:S(2)}, u32[]{:S(2)}) collective-permute-start(bf16[512,2304]{1,0:T(8,128)(2,1)} %bitcast.28), channel_id=1, source_target_pairs={{0,24},{8,16},{16,8},{24,0},{1,25},{9,17},{17,9},{25,1},{2,26},{10... | collective-permute-start | bytes 7077896 | tf_op jit(solution)/shard_map/ppermute | solution.py:729
  277.7 199.1 %collective-permute-start.14 = (bf16[512,2304]{1,0:T(8,128)(2,1)}, bf16[512,2304]{1,0:T(8,128)(2,1)}, u32[]{:S(2)}, u32[]{:S(2)}) collective-permute-start(bf16[512,2304]{1,0:T(8,128)(2,1)} %bitcast.28), channel_id=1, source_target_pairs={{0,16},{8,24},{16,0},{24,8},{1,17},{9,25},{17,1},{25,9},{2,18},{10... | collective-permute-start | bytes 7077896 | tf_op jit(solution)/shard_map/ppermute | solution.py:729
  278.2 198.6 %collective-permute-start.13 = (bf16[512,2304]{1,0:T(8,128)(2,1)}, bf16[512,2304]{1,0:T(8,128)(2,1)}, u32[]{:S(2)}, u32[]{:S(2)}) collective-permute-start(bf16[512,2304]{1,0:T(8,128)(2,1)} %bitcast.28), channel_id=1, source_target_pairs={{0,8},{8,0},{16,24},{24,16},{1,9},{9,1},{17,25},{25,17},{2,10},{10... | collective-permute-start | bytes 7077896 | tf_op jit(solution)/shard_map/ppermute | solution.py:729
  278.7 122.8 %collective-permute-start.16 = (bf16[528,896]{1,0:T(8,128)(2,1)}, bf16[528,896]{1,0:T(8,128)(2,1)}, u32[]{:S(2)}, u32[]{:S(2)}) collective-permute-start(bf16[528,896]{1,0:T(8,128)(2,1)} %get-tuple-element.36), channel_id=1, source_target_pairs={{0,8},{8,0},{16,24},{24,16},{1,9},{9,1},{17,25},{25,17},{2,10},{10... | collective-permute-start | bytes 2838536 | tf_op jit(solution)/shard_map/ppermute | solution.py:729
  280.2 18.1 %collective-permute-start.5 = (f32[2,2304]{1,0:T(2,128)S(1)}, f32[2,2304]{1,0:T(2,128)S(1)}, u32[]{:S(2)}, u32[]{:S(2)}) collective-permute-start(f32[2,2304]{1,0:T(2,128)S(1)} %bitcast.95), channel_id=1, source_target_pairs={{2,0},{4,2},{6,4},{3,1},{5,3},{7,5},{10,8},{12,10},{14,12},{11,9},... | collective-permute-start | bytes 55304 | tf_op jit(solution)/shard_map/ppermute | solution.py:744
  299.2 121.6 %collective-permute-start.18 = (bf16[528,896]{1,0:T(8,128)(2,1)S(1)}, bf16[528,896]{1,0:T(8,128)(2,1)S(1)}, u32[]{:S(2)}, u32[]{:S(2)}) collective-permute-start(bf16[528,896]{1,0:T(8,128)(2,1)S(1)} %copy-done.12), channel_id=1, source_target_pairs={{0,24},{8,16},{16,8},{24,0},{1,25},{9,17},{17,9},{25,1},{2,26},{10... | collective-permute-start | bytes 2838536 | tf_op jit(solution)/shard_map/ppermute | solution.py:729
  302.2 99.3 %copy-start.11 = (bf16[528,896]{1,0:T(8,128)(2,1)S(1)}, bf16[528,896]{1,0:T(8,128)(2,1)}, u32[]{:S(2)}) copy-start(bf16[528,896]{1,0:T(8,128)(2,1)} %get-tuple-element.38) | copy-start | bytes 2838532
  302.7 140.0 %copy-start = (f32[512,2304]{1,0:T(8,128)}, f32[512,2304]{1,0:T(8,128)S(1)}, u32[]{:S(2)}) copy-start(f32[512,2304]{1,0:T(8,128)S(1)} %fusion.33) | copy-start | bytes 14155780
  401.5 39.5 %collective-permute-start.17 = (bf16[528,896]{1,0:T(8,128)(2,1)S(1)}, bf16[528,896]{1,0:T(8,128)(2,1)S(1)}, u32[]{:S(2)}, u32[]{:S(2)}) collective-permute-start(bf16[528,896]{1,0:T(8,128)(2,1)S(1)} %copy-done.11), channel_id=1, source_target_pairs={{0,16},{8,24},{16,0},{24,8},{1,17},{9,25},{17,1},{25,9},{2,18},{10... | collective-permute-start | bytes 2838536 | tf_op jit(solution)/shard_map/ppermute | solution.py:729
  420.8 56.0 %copy-start.8 = (bf16[528,896]{1,0:T(8,128)(2,1)}, bf16[528,896]{1,0:T(8,128)(2,1)S(1)}, u32[]{:S(2)}) copy-start(bf16[528,896]{1,0:T(8,128)(2,1)S(1)} %collective-permute-done.18) | copy-start | bytes 2838532
  420.8 612.2 %collective-permute-start.6 = (f32[512,1152]{1,0:T(8,128)}, f32[512,1152]{1,0:T(8,128)}, u32[]{:S(2)}, u32[]{:S(2)}) collective-permute-start(f32[512,1152]{1,0:T(8,128)} %slice_select_fusion), channel_id=1, source_target_pairs={{0,1},{1,0},{2,3},{3,2},{4,5},{5,4},{6,7},{7,6},{8,9},{9,8},{10,11... | collective-permute-start | bytes 7077896 | tf_op jit(solution)/shard_map/ppermute | solution.py:763
  441.0 35.8 %copy-start.9 = (bf16[528,896]{1,0:T(8,128)(2,1)}, bf16[528,896]{1,0:T(8,128)(2,1)S(1)}, u32[]{:S(2)}) copy-start(bf16[528,896]{1,0:T(8,128)(2,1)S(1)} %collective-permute-done.17) | copy-start | bytes 2838532
  476.8 15.0 %slice-start.5 = ((bf16[528,896]{1,0:T(8,128)(2,1)}), bf16[512,896]{1,0:T(8,128)(2,1)S(1)}, s32[]{:S(2)}) async-start(bf16[528,896]{1,0:T(8,128)(2,1)} %copy-done.8), calls=%async_computation.5 | async-start | bytes 1835008 | tf_op jit(solution)/shard_map/slice | solution.py:823
  476.8 15.0 %slice-start.6 = ((bf16[528,896]{1,0:T(8,128)(2,1)}), bf16[512,896]{1,0:T(8,128)(2,1)S(1)}, s32[]{:S(2)}) async-start(bf16[528,896]{1,0:T(8,128)(2,1)} %copy-done.9), calls=%async_computation.6 | async-start | bytes 1835008 | tf_op jit(solution)/shard_map/slice | solution.py:823
  476.8 15.0 %copy-start.13 = (bf16[512,896]{1,0:T(8,128)(2,1)S(1)}, bf16[512,896]{1,0:T(8,128)(2,1)}, u32[]{:S(2)}) copy-start(bf16[512,896]{1,0:T(8,128)(2,1)} %constant_dynamic-slice_fusion) | copy-start | bytes 2752516
  972.4 60.6 %slice-start = ((s8[4718592]{0:T(1024)(128)(4,1)}), s8[4194304]{0:T(1024)(128)(4,1)S(1)}, s32[]{:S(2)}) async-start(s8[4718592]{0:T(1024)(128)(4,1)} %bitcast.82), calls=%async_computation | async-start | bytes 8388608
  993.4 39.0 %copy-start.17 = (f32[6,1152]{1,0:T(8,128)S(1)}, f32[6,1152]{1,0:T(8,128)}, u32[]{:S(2)}) copy-start(f32[6,1152]{1,0:T(8,128)} %get-tuple-element.31) | copy-start | bytes 82948
  993.4 39.6 %slice-start.1 = ((s8[4718592]{0:T(1024)(128)(4,1)}), s8[524288]{0:T(1024)(128)(4,1)S(1)}, s32[]{:S(2)}) async-start(s8[4718592]{0:T(1024)(128)(4,1)} %bitcast.82), calls=%async_computation.1 | async-start | bytes 1048576
  (12 other events, 44.6 us)

commit v2 on v1

--- a/solution.py
+++ b/solution.py
@@ -191,7 +191,7 @@
     lax.fori_loop(0, tokens // STEP, body, 0)
 
 
-def grads_pass(seqs, tokens, channels, message, entering, upstream, keep, upd, fgt, out, state, scale, shift, grads, sums):
+def grads_pass(seqs, tokens, channels, message, entering, upstream, keep, upd, fgt, out, state, scale, shift, grads, planes, sums):
     steps = tokens // STEP
     sums[...] = jnp.zeros_like(sums)
     if grads.shape[1] > 3 * channels:
@@ -222,6 +222,7 @@
                 for gate, value in enumerate(given):
                     value = value.astype(BF16)
                     grads[whole, gate * channels + lanes.start : gate * channels + lanes.stop] = value
+                    planes[gate, whole, lanes] = value
                     value = value.astype(F32)
                     total = value[:SUB]
                     for half in range(1, STEP // SUB):
@@ -242,7 +243,7 @@
     states_pass(seqs, tokens, channels, entering, out, scale, shift, state, hidden)
 
 
-def top_kernel(seqs, tokens, channels, gates, bias, keep, initial, cotangent, pooled, grads, sums, upd, fgt, out, state, entering, message, scale, shift, back_scale, back_shift, summary, slots, send_sems, recv_sems):
+def top_kernel(seqs, tokens, channels, gates, bias, keep, initial, cotangent, pooled, grads, planes, sums, upd, fgt, out, state, entering, message, scale, shift, back_scale, back_shift, summary, slots, send_sems, recv_sems):
     greet("seq")
     first_pass(seqs, tokens, channels, gates, bias, keep, upd, fgt, out, scale, shift, summary)
     back_pass(seqs, tokens, channels, cotangent, keep, fgt, out, back_scale, back_shift, summary, 2 * seqs)
@@ -254,7 +255,7 @@
         slots, (seqs, channels), slice(2 * seqs, 3 * seqs), slice(3 * seqs, 4 * seqs), "seq"
     )
     states_pass(seqs, tokens, channels, entering, out, scale, shift, state, pooled)
-    grads_pass(seqs, tokens, channels, message, entering, cotangent, keep, upd, fgt, out, state, back_scale, back_shift, grads, sums)
+    grads_pass(seqs, tokens, channels, message, entering, cotangent, keep, upd, fgt, out, state, back_scale, back_shift, grads, planes, sums)
 
 
 def pass_edges(seqs, tokens, grads, edges, arrived, edge_sems):
@@ -294,14 +295,14 @@
         copy.wait_send()
 
 
-def backward_kernel(seqs, tokens, channels, upstream, keep, upd, fgt, out, state, entering, grads, sums, message, scale, shift, summary, slots, send_sems, recv_sems, edges, arrived, edge_sems):
+def backward_kernel(seqs, tokens, channels, upstream, keep, upd, fgt, out, state, entering, grads, planes, sums, message, scale, shift, summary, slots, send_sems, recv_sems, edges, arrived, edge_sems):
     greet("seq")
     back_pass(seqs, tokens, channels, upstream, keep, fgt, out, scale, shift, summary, 0)
     copies = to_all(summary, slots, send_sems, recv_sems, "seq")
     for copy in copies:
         copy.wait()
     message[...] = from_later(slots, (seqs, channels), slice(0, seqs), slice(seqs, 2 * seqs), "seq")
-    grads_pass(seqs, tokens, channels, message, entering, upstream, keep, upd, fgt, out, state, scale, shift, grads, sums)
+    grads_pass(seqs, tokens, channels, message, entering, upstream, keep, upd, fgt, out, state, scale, shift, grads, planes, sums)
     pass_edges(seqs, tokens, grads, edges, arrived, edge_sems)
 
 
@@ -356,10 +357,11 @@
         out_shape=(
             jax.ShapeDtypeStruct((rows, channels), BF16),
             jax.ShapeDtypeStruct((rows, lanes), BF16),
+            jax.ShapeDtypeStruct((3, rows, channels), BF16),
             jax.ShapeDtypeStruct((3, SUB, channels), F32),
         ),
         in_specs=[VMEM] * 5,
-        out_specs=[VMEM] * 3,
+        out_specs=[VMEM] * 4,
         scratch_shapes=[whole] * 4 + [edge] * 2 + [whole] * 4 + exchange_scratch(4 * seqs, channels),
         compiler_params=params(2),
         cost_estimate=cost(rows * channels, 120, rows * channels * 22),
@@ -374,10 +376,11 @@
         functools.partial(backward_kernel, seqs, tokens, channels),
         out_shape=(
             jax.ShapeDtypeStruct((rows + EDGE, lanes), BF16),
+            jax.ShapeDtypeStruct((3, rows, channels), BF16),
             jax.ShapeDtypeStruct((3, SUB, channels), F32),
         ),
         in_specs=[VMEM] * 7,
-        out_specs=[VMEM] * 2,
+        out_specs=[VMEM] * 3,
         scratch_shapes=[pltpu.VMEM((seqs, channels), F32)]
         + [whole] * 2
         + exchange_scratch(2 * seqs, channels)
@@ -389,12 +392,39 @@
     )(upstream, keep, upd, fgt, out, state, entering)
 
 
-def spread_kernel(layers, parts, loads, sums, out, sums_out, own, ups, downs, acc, across, around, load_sems, up_sems, down_sems, line_send, line_recv, kept_sems, plane_send, plane_recv, sums_sems):
+def shift_up(seqs, tokens, value, edges, result):
+    width = value.shape[1]
+    steps = tokens // STEP
+
+    def body(index, none):
+        sequence, at = index // steps, lax.rem(index, steps)
+        row = lax.broadcasted_iota(jnp.int32, (STEP, width), 0)
+        rows = pl.ds(pl.multiple_of(index * STEP, STEP), STEP)
+        after = jnp.minimum(index + 1, value.shape[0] // STEP - 1)
+        first = value[pl.ds(pl.multiple_of(after * STEP, STEP), STEP), :].astype(F32)[0:1]
+        edge = edges[sequence // seqs].astype(F32)
+        edge = jnp.where(lax.rem(sequence, seqs) == 0, edge[0:1], edge[1:2])
+        moved = pltpu.roll(value[rows, :].astype(F32), STEP - 1, 0)
+        moved = jnp.where(row == STEP - 1, jnp.where(at == steps - 1, edge, first), moved)
+        result[rows, :] = moved.astype(BF16)
+        return none
+
+    lax.fori_loop(0, value.shape[0] // STEP, body, 0)
+
+
+def spread_kernel(seqs, tokens, parts, hidden_own, hidden_other, full_own, full_other, *refs):
+    blocks_two, (grads_one, sums, out, sums_out, rows_full, grads, grads_edge, moved, *rest) = refs[:4], refs[4:]
+    _spread(seqs, tokens, parts, (hidden_own, hidden_other), (full_own, full_other), blocks_two, grads_one, sums, out, sums_out, rows_full, grads, grads_edge, moved, *rest)
+
+
+def _spread(seqs, tokens, parts, hidden, full, blocks_two, grads_one, sums, out, sums_out, rows_full, grads, grads_edge, moved, own, ups, downs, acc, across, around, load_sems, swap_sems, up_sems, down_sems, line_send, line_recv, kept_sems, plane_send, plane_recv, sums_sems):
     line, plane = lax.axis_size("seq"), lax.axis_size("dp")
     at, here = lax.axis_index("seq"), lax.axis_index("dp")
     unit = line * parts
-    depth = own.shape[0] // layers
     units = own.shape[0] // unit
+    blocks = units // 3
+    width = own.shape[1]
+    block_rows = seqs * tokens
     half = unit // 2
     beside = here + 1 - 2 * lax.rem(here, 2)
     below = lax.rem(here + 2, plane)
@@ -418,8 +448,48 @@
             device_id_type=pl.DeviceIdType.MESH,
         )
 
-    def load(layer):
-        return pltpu.make_async_copy(loads[layer], own.at[pl.ds(layer * depth, depth)], load_sems.at[layer])
+    mine = lax.axis_index("mp")
+    wide = rows_full.shape[1] // 2
+
+    def load_rows(pair, number):
+        return [
+            pltpu.make_async_copy(
+                pair[way],
+                rows_full.at[:, pl.ds(pl.multiple_of((mine if way == 0 else 1 - mine) * wide, 128), wide)],
+                load_sems.at[number + way],
+            )
+            for way in range(2)
+        ]
+
+    def plane_rows(owner):
+        return pl.ds(pl.multiple_of(owner * block_rows, 16), block_rows)
+
+    def peer(steps):
+        return (here, beside, below, across_from)[steps]
+
+    def load_two(steps):
+        return pltpu.make_async_copy(blocks_two[steps], moved.at[plane_rows(peer(steps))], load_sems.at[4 + steps])
+
+    def swap(steps, edge, arriving=False):
+        columns = pl.ds(pl.multiple_of(peer(steps) * width, 128), width)
+        source = peer(steps) if arriving else here
+        if edge:
+            src, dst = grads_one.at[block_rows : block_rows + EDGE, columns], grads_edge.at[source]
+        else:
+            src, dst = grads_one.at[0:block_rows, columns], grads.at[plane_rows(source)]
+        number = steps * 2 + edge
+        if steps == 0:
+            return pltpu.make_async_copy(src, dst, swap_sems.at[0, number])
+        return remote(src, dst, swap_sems.at[0, number], swap_sems.at[1, number], "dp", peer(steps))
+
+    def product(block, right):
+        columns = pl.ds(pl.multiple_of(block * unit, 128), unit)
+        return lax.dot_general(
+            rows_full[:, columns], right[...], (((0,), (0,)), ((), ())), preferred_element_type=F32
+        ).astype(BF16)
+
+    def whole(u):
+        return pl.ds(pl.multiple_of(u * unit, unit), unit)
 
     def chunk(u, j):
         return pl.ds(pl.multiple_of(u * unit + j * parts, parts), parts)
@@ -478,18 +548,24 @@
         place = slots.at[lax.rem(me + count - step, count)]
         return remote(place, place, sums_sems.at[number, 0, step - 1], sums_sems.at[number, 1, step - 1], axis, lax.rem(me + step, count))
 
-    for layer in range(layers):
-        load(layer).start()
+    for steps in range(4):
+        load_two(steps).start()
+    for copy in load_rows(hidden, 0):
+        copy.start()
+    for steps in range(4):
+        for edge in range(2):
+            swap(steps, edge).start()
     across[at] = sums[...]
     for step in range(1, line):
         sums_copy(across, at, line, "seq", 0, step).start()
-    load(0).wait()
+    for steps in range(4):
+        load_two(steps).wait()
+    for copy in load_rows(hidden, 0):
+        copy.wait()
 
     def stage(index, none):
         @pl.when(index == 1)
         def _():
-            for layer in range(1, layers):
-                load(layer).wait()
             for step in range(1, line):
                 sums_arrival(across, at, line, "seq", 0, step).wait_recv()
             total = across[0]
@@ -508,6 +584,35 @@
                 total = total + around[other]
             sums_out[...] = total
 
+        @pl.when(index < blocks)
+        def _():
+            own[whole(index), :] = product(index, moved)
+
+        @pl.when(index == blocks - 1)
+        def _():
+            for copy in load_rows(full, 2):
+                copy.start()
+
+        @pl.when(index == blocks)
+        def _():
+            for steps in range(4):
+                for edge in range(2):
+                    if steps:
+                        swap(steps, edge, True).wait_recv()
+                    else:
+                        swap(steps, edge).wait()
+            shift_up(seqs, tokens, grads, grads_edge, moved)
+            for copy in load_rows(full, 2):
+                copy.wait()
+
+        @pl.when((index >= blocks) & (index < units) & (lax.rem(index - blocks, 2) == 0))
+        def _():
+            own[whole(index), :] = product((index - blocks) // 2, grads)
+
+        @pl.when((index >= blocks) & (index < units) & (lax.rem(index - blocks, 2) == 1))
+        def _():
+            own[whole(index), :] = product((index - blocks) // 2, moved)
+
         u = index - at
 
         @pl.when((u >= 0) & (u < units))
@@ -653,38 +758,43 @@
         return none
 
     lax.fori_loop(0, units, settle, 0)
+    for steps in range(1, 4):
+        for edge in range(2):
+            swap(steps, edge).wait_send()
     for step in range(1, line):
         sums_copy(across, at, line, "seq", 0, step).wait_send()
     for step in range(1, plane):
         sums_copy(around, here, plane, "dp", 1, step).wait_send()
 
 
-def spread(partials, sums):
+def spread(seqs, tokens, hidden, full, blocks_two, grads_one, sums):
     line, plane = lax.axis_size("seq"), lax.axis_size("dp")
-    layers = len(partials)
-    depth, width = partials[0].shape
-    units = layers * depth // (line * PART)
-
-    def kernel(*refs):
-        spread_kernel(layers, PART, refs[:layers], *refs[layers:])
-
+    rows, width = blocks_two[0].shape
+    depth = 2 * full[0].shape[1]
+    units = 3 * depth // (line * PART)
     dma = pltpu.SemaphoreType.DMA
+    hbm = pl.BlockSpec(memory_space=pl.ANY)
     return pl.pallas_call(
-        kernel,
+        functools.partial(spread_kernel, seqs, tokens, PART),
         out_shape=(
-            jax.ShapeDtypeStruct((plane, layers * depth, width), BF16),
+            jax.ShapeDtypeStruct((plane, 3 * depth, width), BF16),
             jax.ShapeDtypeStruct(sums.shape, F32),
         ),
-        in_specs=[pl.BlockSpec(memory_space=pl.ANY)] * layers + [VMEM],
-        out_specs=[pl.BlockSpec(memory_space=pl.ANY), VMEM],
+        in_specs=[hbm] * 9 + [VMEM],
+        out_specs=[hbm, VMEM],
         scratch_shapes=[
-            pltpu.VMEM((layers * depth, width), BF16),
+            pltpu.VMEM((plane * rows, depth), BF16),
+            pltpu.VMEM((plane * rows, width), BF16),
+            pltpu.VMEM((plane, EDGE, width), BF16),
+            pltpu.VMEM((plane * rows, width), BF16),
+            pltpu.VMEM((3 * depth, width), BF16),
             pltpu.VMEM((units, line - 1, PART, width), BF16),
             pltpu.VMEM((units, line - 1, PART, width), BF16),
             pltpu.VMEM((PART, width), F32),
             pltpu.VMEM((line,) + sums.shape, F32),
             pltpu.VMEM((plane,) + sums.shape, F32),
-            dma((layers,)),
+            dma((8,)),
+            dma((2, 8)),
             dma((2, units * (line - 1))),
             dma((2, units * (line - 1))),
             dma((units * 2 * (line - 1),)),
@@ -695,9 +805,11 @@
             dma((2, 2, max(line, plane) - 1)),
         ],
         compiler_params=params(4),
-        cost_estimate=pl.CostEstimate(flops=0, bytes_accessed=layers * depth * width * 16, transcendentals=0),
+        cost_estimate=pl.CostEstimate(
+            flops=6 * plane * rows * depth * width, bytes_accessed=depth * width * 48, transcendentals=0
+        ),
         name="spread",
-    )(*partials, sums)
+    )(*hidden, *full, *blocks_two, grads_one, sums)
 
 
 def widen_kernel(tiles, blocks, given, out):
@@ -710,19 +822,31 @@
         ].astype(F32)
 
 
-def widen(gathered, first, layers, depth, channels):
+def widen(gathered, layer_one, depth, channels, unit):
     plane, _, width = gathered.shape
     rows = 128
-    steps = depth // rows
+    steps, per = depth // rows, unit // rows
+    taps = 2 if layer_one else 1
+
+    def place(tap, step):
+        if not layer_one:
+            return (0, step, 0)
+        return (0, steps + (step // per * 2 + tap) * per + lax.rem(step, per), 0)
+
     return pl.pallas_call(
         functools.partial(widen_kernel, 3, channels // 128),
-        grid=(layers, steps),
-        out_shape=jax.ShapeDtypeStruct((layers, 3, depth, channels), F32),
-        in_specs=[pl.BlockSpec((plane, rows, width), lambda layer, step: (0, (first + layer) * steps + step, 0))],
-        out_specs=pl.BlockSpec((1, 3, rows, channels), lambda layer, step: (layer, 0, step, 0)),
+        grid=(taps, steps),
+        out_shape=jax.ShapeDtypeStruct((taps, 3, depth, channels), F32),
+        in_specs=[pl.BlockSpec((plane, rows, width), place)],
+        out_specs=pl.BlockSpec((1, 3, rows, channels), lambda tap, step: (tap, 0, step, 0)),
         compiler_params=pltpu.CompilerParams(vmem_limit_bytes=32 * 2**20),
         name="widen",
     )(gathered)
+
+
+def plane_tokens(value):
+    every = lax.all_gather(value, "dp", axis=0, tiled=True)
+    return every, lax.ppermute(every, "mp", [(0, 1), (1, 0)])
 
 
 def around_plane(value, steps):
@@ -794,44 +918,37 @@
     gates_two = jnp.einsum("td,gdc->gtc", full_hidden, mix, preferred_element_type=F32)
     line, plane = lax.axis_size("seq"), lax.axis_size("dp")
     tiles = 3 * channels // 128
-    spreads = plane == 4 and channels % 128 == 0 and width % (line * PART) == 0 and line > 1
+    spreads = plane == 4 and lax.axis_size("mp") == 2 and seqs == 2 and channels % 128 == 0 and width % (line * PART) == 0 and line > 1
     block = -(-tiles // plane) * 128
     lanes = plane * block if spreads else 3 * channels
-    pooled_two, grad_two, sums_two = pool_top(
+    pooled_two, grad_two, planes_two, sums_two = pool_top(
         seqs, tokens, lanes, gates_two, bias_two, keep, init_state[1], cotangent.reshape(rows, channels)
     )
     hidden_terms = jnp.einsum(
-        "tgc,gdc->td", grad_two[:, : 3 * channels].reshape(rows, 3, channels), mix, preferred_element_type=F32
+        "gtc,gdc->td", planes_two, mix, preferred_element_type=F32
     )
     hidden_grad = sum_channels(hidden_terms)
-    extended, sums_one = pool_backward(seqs, tokens, lanes, hidden_grad, keep, upd, fgt, out, state, entering)
+    extended, planes_one, sums_one = pool_backward(seqs, tokens, lanes, hidden_grad, keep, upd, fgt, out, state, entering)
     grad_one = extended[:rows, : 3 * channels]
     input_terms = jnp.einsum(
-        "tgc,kgdc->ktd", grad_one.reshape(rows, 3, channels), taps, preferred_element_type=F32
+        "gtc,kgdc->ktd", planes_one, taps, preferred_element_type=F32
     ).reshape(2, seqs, tokens, width)
     late = input_terms[1]
     late = jnp.concatenate([late[:, 1:], shifted(late[:, 0], "seq", -1)[:, None]], 1)
     input_grad = sum_channels((input_terms[0] + late).reshape(rows, width))
     sums = jnp.concatenate([jnp.sum(sums_one, 1), jnp.sum(sums_two, 1)])
     if spreads:
-        every = [full] + [around_plane(full, steps) for steps in range(1, 4)]
-        every_hidden = [full_hidden] + [around_plane(full_hidden, steps) for steps in range(1, 4)]
-        blocks_two = to_owners(grad_two, block)
-        blocks_one = to_owners(extended, block)
-        partial_two = dot(jnp.concatenate(every_hidden), jnp.concatenate(blocks_two), ((0,), (0,))).astype(BF16)
-        every = jnp.concatenate(every)
-        partial_one = dot(every, jnp.concatenate([given[:rows] for given in blocks_one]), ((0,), (0,))).astype(BF16)
-        following = []
-        for given in blocks_one:
-            for seq in range(seqs):
-                following += [
-                    given[seq * tokens + 1 : seq * tokens + tokens],
-                    given[rows + seq : rows + seq + 1],
-                ]
-        partial_late = dot(every, jnp.concatenate(following), ((0,), (0,))).astype(BF16)
-        gathered, sums = spread([partial_two, partial_one, partial_late], sums)
-        weight_two_grad = widen(gathered, 0, 1, width, channels)[0].transpose(1, 0, 2)
-        weight_one_grad = widen(gathered, 1, 2, width, channels).transpose(0, 2, 1, 3)
+        gathered, sums = spread(
+            seqs,
+            tokens,
+            plane_tokens(hidden),
+            plane_tokens(inputs.reshape(rows, channels)),
+            to_owners(grad_two, block),
+            extended,
+            sums,
+        )
+        weight_two_grad = widen(gathered, False, width, channels, line * PART)[0].transpose(1, 0, 2)
+        weight_one_grad = widen(gathered, True, width, channels, line * PART).transpose(0, 2, 1, 3)
     else:
         sums = lax.psum(sums, ("dp", "seq"))
         weight_two_grad = reduce_weights(dot(full_hidden, grad_two, ((0,), (0,)))).reshape(width, 3, channels)

time: 1050 us -> 806 us (0.77)
  waiting for transfers between devices: 203 us -> 45.9 us
  local copies, waits for them, and re-layouts: 70.7 us -> 14.1 us
  matrix products: 122 us -> 77.3 us
  Pallas kernels: 600 us -> 620 us
  between operations: 1.28 us -> 14.3 us
    ppermute x12 -> x3, waiting for transfers between devices: 200 us -> 29.2 us  [around_plane(): return lax.ppermute(value, 'dp', [(at, at ^ steps) for at in range(4)])]
    dot_general x5 -> x2, matrix products: 81.2 us -> 37.3 us  [the longest x1 24.5 us: local(): jnp.einsum('gtc,kgdc->ktd', planes_one, taps, preferred_element_type=F32)]
    concatenate x1 -> x0, local copies, waits for them, and re-layouts: 30.4 us -> none  [local(): jnp.concatenate(following)]
    slice x18 -> x0, local copies, waits for them, and re-layouts: 21.1 us -> none  [the longest x2 5.82 us: local(): grad_two[:, :3 * channels].reshape(rows, 3, channels)]
    pallas_call x1, Pallas kernels: 467 us -> 485 us  [spread(): pl.pallas_call(functools.partial(spread_kernel, seqs, tokens, PART), out_...]
  transfers between devices with their start and end apart: 19 -> 14, of which waited for: 6 -> 7; matrix products, arithmetic and copies ran while one was open for 13% -> 13% of each run, Pallas kernels for 53% -> 9%
where the time goes in v2:
time: 806 us; the launch traced here: 803 us
  Pallas kernels  620 us (77%)
  matrix products  77.3 us (10%)
  waiting for transfers between devices  45.9 us (6%)
  other arithmetic  19.3 us (2%)
  between operations  14.3 us (2%)
  local copies, waits for them, and re-layouts  14.1 us (2%)
  starting transfers between devices  11.9 us (1%)
    pallas_call x1, Pallas kernels, spread(): pl.pallas_call(functools.partial(spread_kernel, seqs, tokens, PART), out_...  485 us
    pallas_call x2, Pallas kernels, widen(): pl.pallas_call(functools.partial(widen_kernel, 3, channels // 128), grid=...  59.1 us
    ppermute x3, waiting for transfers between devices, around_plane(): return lax.ppermute(value, 'dp', [(at, at ^ steps) for at in range(4)])  29.2 us
    pallas_call x1, Pallas kernels, pool_top(): pl.pallas_call(functools.partial(top_kernel, seqs, tokens, channels), out...  29.2 us
    pallas_call x1, Pallas kernels, pool_backward(): pl.pallas_call(functools.partial(backward_kernel, seqs, tokens, channels)...  28.8 us
    dot_general x1, matrix products, local(): jnp.einsum('tkd,kgdc->gtc', both.reshape(rows, 2, width), taps, preferred...  25.5 us
    dot_general x1, matrix products, local(): jnp.einsum('gtc,kgdc->ktd', planes_one, taps, preferred_element_type=F32)  24.5 us
    pallas_call x1, Pallas kernels, pool_forward(): pl.pallas_call(functools.partial(forward_kernel, seqs, tokens, channels),...  18 us
  transfers between devices with their start and end apart: 14, of which 7 were waited for; matrix products, arithmetic and copies ran while one was open for 13% of the time, Pallas kernels for 9%

profile of v2, /device:TPU:0, one launch (start us, length us, event | category | flops | bytes accessed | tf_op | source)
XLA Modules:
  0.0 802.8 jit_solution(7538367315315205475)
XLA Ops:
  8.7 4.9 collective-permute-start.1
  13.7 1.3 slice_bitcast_fusion.1
  16.2 1.5 broadcast_select_fusion
  18.7 25.5 %fusion.11.gates = f32[3,512,1152]{2,1,0:T(8,128)} fusion(bf16[2,2304,3,1152]{3,1,2,0:T(8,128)(2,1)} %param.11, bf16[512,1,2304]{2,0,1:T(8,128)(2,1)S(1)} %bitcast.84, bf16[512,1,2304]{2,0,1:T(8,128)(2,1)S(1)} %bitcast.83), kind=kOutput, calls=%fused_computation.9 | convolution fusion | flops 16316891136 | bytes 43646976 | tf_op jit(solution)/shard_map/tkd,kgdc->gtc/dot_general | solution.py:913
  45.0 18.0 %pool_forward.1 = (bf16[512,1152]{1,0:T(8,128)(2,1)}, f32[512,1152]{1,0:T(8,128)}, f32[512,1152]{1,0:T(8,128)}, f32[512,1152]{1,0:T(8,128)}, f32[512,1152]{1,0:T(8,128)}, /*index=5*/f32[2,1152]{1,0:T(2,128)}) custom-call(f32[3,512,1152]{2,1,0:T(8,128)} %fusion.11.gates, f32[3,1152]{1,0:T(4,128)} %bias.2, f32[512,128]{1,0:T(8,128)} %broadcast_in_dim.15.keep, ...), custom_call_target="tpu_custom_call" | custom-call | flops 35389440 | bytes 17694720 | tf_op jit(solution)/shard_map/pool_forward/pallas_call | solution.py:331
  63.0 3.0 collective-permute-done.3
  66.0 1.5 broadcast_select_fusion.3
  67.5 14.6 %fusion.14.gates = f32[3,512,1152]{2,1,0:T(8,128)} fusion(bf16[2304,3,1152]{2,0,1:T(8,128)(2,1)} %param.13, bf16[512,1152]{1,0:T(8,128)(2,1)S(1)} %get-tuple-element.41, bf16[512,1152]{1,0:T(8,128)(2,1)S(1)} %get-tuple-element.40), kind=kOutput, calls=%fused_computation.10 | convolution fusion | flops 8158445568 | bytes 25362432 | tf_op jit(solution)/shard_map/td,gdc->gtc/dot_general | solution.py:918
  82.1 29.2 %pool_top.1 = (bf16[512,1152]{1,0:T(8,128)(2,1)}, bf16[512,3584]{1,0:T(8,128)(2,1)}, bf16[3,512,1152]{2,1,0:T(8,128)(2,1)}, f32[3,8,1152]{2,1,0:T(8,128)}) custom-call(f32[3,512,1152]{2,1,0:T(8,128)} %fusion.14.gates, f32[3,1152]{1,0:T(4,128)} %bias.3, f32[512,128]{1,0:T(8,128)} %broadcast_in_dim.15.keep, f32[2,1152]{1,0:T(2,128)} %get-tuple-element.46.initial, ...), custom_call_target="tpu_custom_call" | custom-call | flops 70778880 | bytes 12976128 | tf_op jit(solution)/shard_map/pool_top/pallas_call | solution.py:355
  111.4 12.7 %fusion.17 = f32[512,2304]{1,0:T(8,128)S(1)} fusion(bf16[3,512,1152]{2,1,0:T(8,128)(2,1)} %get-tuple-element.23, bf16[2304,3,1152]{2,0,1:T(8,128)(2,1)} %param.13), kind=kOutput, calls=%fused_computation.11 | convolution fusion | flops 8153726976 | bytes 24182784 | tf_op jit(solution)/shard_map/gtc,gdc->td/dot_general | solution.py:927
  124.4 4.5 collective-permute-done.4
  129.0 1.9 select_add_fusion.1.upstream
  130.9 28.8 %pool_backward.1 = (bf16[528,3584]{1,0:T(8,128)(2,1)}, bf16[3,512,1152]{2,1,0:T(8,128)(2,1)}, f32[3,8,1152]{2,1,0:T(8,128)}) custom-call(f32[512,1152]{1,0:T(8,128)} %select_add_fusion.1.upstream, f32[512,128]{1,0:T(8,128)} %broadcast_in_dim.15.keep, f32[512,1152]{1,0:T(8,128)} %get-tuple-element.24.upd, f32[512,1152]{1,0:T(8,128)} %get-tuple-element.25.fgt, ...), custom_call_target="tpu_custom_call" | custom-call | flops 35389440 | bytes 15335424 | tf_op jit(solution)/shard_map/pool_backward/pallas_call | solution.py:375
  159.7 24.5 %fusion.8 = f32[2,512,2304]{2,1,0:T(8,128)} fusion(bf16[2,2304,3,1152]{3,1,2,0:T(8,128)(2,1)} %param.11, bf16[3,512,1152]{2,1,0:T(8,128)(2,1)} %get-tuple-element.29), kind=kOutput, calls=%fused_computation.8 | convolution fusion | flops 16307453952 | bytes 44826624 | tf_op jit(solution)/shard_map/gtc,kgdc->ktd/dot_general | solution.py:933
  184.2 2.6 slice.63
  186.9 1.3 collective-permute-start.5
  188.5 4.0 collective-permute-done.5
  192.6 2.5 pad_maximum_fusion
  195.6 4.3 fusion.20
  200.2 1.9 copy-done
  202.1 3.7 constant_dynamic-slice_fusion
  205.8 2.4 collective-permute-start.11
  208.8 4.4 collective-permute-done.6
  213.3 1.5 collective-permute-start.9
  215.3 4.8 select_add_fusion
  220.2 10.0 %collective-permute-done.11.refs_3_ = bf16[512,896]{1,0:T(8,128)(2,1)} collective-permute-done((bf16[512,896]{1,0:T(8,128)(2,1)}, bf16[512,896]{1,0:T(8,128)(2,1)}, u32[]{:S(2)}, u32[]{:S(2)}) %collective-permute-start.11) | collective-permute-done | bytes 917536 | tf_op jit(solution)/shard_map/ppermute | solution.py:853
  230.2 19.2 %collective-permute-done.10.refs_2_ = bf16[512,896]{1,0:T(8,128)(2,1)} collective-permute-done((bf16[512,896]{1,0:T(8,128)(2,1)}, bf16[512,896]{1,0:T(8,128)(2,1)}, u32[]{:S(2)}, u32[]{:S(2)}) %collective-permute-start.10) | collective-permute-done | bytes 917536 | tf_op jit(solution)/shard_map/ppermute | solution.py:853
  249.4 0.9 copy-done.5
  250.3 484.8 %spread.1 = (bf16[4,6912,896]{2,1,0:T(8,128)(2,1)}, f32[6,1152]{1,0:T(8,128)}) custom-call(bf16[2048,1152]{1,0:T(8,128)(2,1)} %all-gather.3.cloned.1.call-done.hidden_own, bf16[2048,1152]{1,0:T(8,128)(2,1)} %collective-permute-done.7.hidden_other, bf16[2048,1152]{1,0:T(8,128)(2,1)} %all-gather.5.cloned.1.call-done.full_own, ...), custom_call_target="tpu_custom_call" | custom-call | flops 25367150592 | bytes 99090432 | tf_op jit(solution)/shard_map/spread/pallas_call | solution.py:777
  735.2 20.1 %widen.3 = f32[1,3,2304,1152]{3,2,1,0:T(8,128)} custom-call(bf16[4,6912,896]{2,1,0:T(8,128)(2,1)} %get-tuple-element.34.given), custom_call_target="tpu_custom_call" | custom-call | tf_op jit(solution)/shard_map/widen/pallas_call | solution.py:836
  755.3 39.0 %widen.2 = f32[2,3,2304,1152]{3,2,1,0:T(8,128)} custom-call(bf16[4,6912,896]{2,1,0:T(8,128)(2,1)} %get-tuple-element.34.given), custom_call_target="tpu_custom_call" | custom-call | tf_op jit(solution)/shard_map/widen/pallas_call | solution.py:836
  794.9 1.0 copy.33
  (51 shorter events, 7.9 us)
Async XLA Ops:
  7.2 187.9 %all-gather.5.cloned.1.call-start = ((), (), s32[]{:S(2)}) async-start(), calls=%async_computation.1 | async-start | bytes 5898240 | tf_op jit(solution)/shard_map/all_gather | solution.py:848
  7.2 9.0 %collective-permute-start = (bf16[2,256,1152]{2,1,0:T(8,128)(2,1)}, bf16[2,256,1152]{2,1,0:T(8,128)(2,1)S(1)}, u32[]{:S(2)}, u32[]{:S(2)}) collective-permute-start(bf16[2,256,1152]{2,1,0:T(8,128)(2,1)} %param.8), channel_id=1, source_target_pairs={{0,1},{1,0},{2,3},{3,2},{4,5},{5,4},{6,7},{7,6},{8,9},{9,8},{10,11... | collective-permute-start | bytes 3538952 | tf_op jit(solution)/shard_map/ppermute | solution.py:875
  7.9 187.2 %all-gather.3.cloned.1.call-start = ((), (), s32[]{:S(2)}) async-start(), calls=%async_computation | async-start | bytes 5898240 | tf_op jit(solution)/shard_map/all_gather | solution.py:848
  8.7 6.3 collective-permute-start.1
  15.0 1.2 collective-permute-start.2
  62.9 3.1 collective-permute-start.3
  124.4 4.6 collective-permute-start.4
  186.9 5.7 collective-permute-start.5
  195.1 54.3 %collective-permute-start.8 = (bf16[2048,1152]{1,0:T(8,128)(2,1)}, bf16[2048,1152]{1,0:T(8,128)(2,1)}, u32[]{:S(2)}, u32[]{:S(2)}) collective-permute-start(bf16[2048,1152]{1,0:T(8,128)(2,1)} %all-gather.5.cloned.1.call-done.full_own), channel_id=1, source_target_pairs={{0,1},{1,0},{2,3},{3,2},{4,5},{5,4},{6,7},{7,6},{8,9},{9,8},{10,11... | collective-permute-start | bytes 14155784 | tf_op jit(solution)/shard_map/ppermute | solution.py:849
  195.1 54.3 %collective-permute-start.7 = (bf16[2048,1152]{1,0:T(8,128)(2,1)}, bf16[2048,1152]{1,0:T(8,128)(2,1)}, u32[]{:S(2)}, u32[]{:S(2)}) collective-permute-start(bf16[2048,1152]{1,0:T(8,128)(2,1)} %all-gather.3.cloned.1.call-done.hidden_own), channel_id=1, source_target_pairs={{0,1},{1,0},{2,3},{3,2},{4,5},{5,4},{6,7},{7,6},{8,9},{9,8},{10,11... | collective-permute-start | bytes 14155784 | tf_op jit(solution)/shard_map/ppermute | solution.py:849
  199.9 2.2 copy-start
  202.1 11.1 %collective-permute-start.6 = (f32[512,1152]{1,0:T(8,128)S(1)}, f32[512,1152]{1,0:T(8,128)}, u32[]{:S(2)}, u32[]{:S(2)}) collective-permute-start(f32[512,1152]{1,0:T(8,128)S(1)} %slice_select_fusion), channel_id=1, source_target_pairs={{0,1},{1,0},{2,3},{3,2},{4,5},{5,4},{6,7},{7,6},{8,9},{9,8},{10,11... | collective-permute-start | bytes 7077896 | tf_op jit(solution)/shard_map/ppermute | solution.py:887
  202.1 6.6 copy-start.2
  202.1 6.7 copy-start.3
  205.8 24.4 %collective-permute-start.11 = (bf16[512,896]{1,0:T(8,128)(2,1)}, bf16[512,896]{1,0:T(8,128)(2,1)}, u32[]{:S(2)}, u32[]{:S(2)}) collective-permute-start(bf16[512,896]{1,0:T(8,128)(2,1)} %get-tuple-element.36), channel_id=1, source_target_pairs={{0,24},{8,16},{16,8},{24,0},{1,25},{9,17},{17,9},{25,1},{2,26},{10... | collective-permute-start | bytes 2752520 | tf_op jit(solution)/shard_map/ppermute | solution.py:853
  208.2 41.2 %collective-permute-start.10 = (bf16[512,896]{1,0:T(8,128)(2,1)}, bf16[512,896]{1,0:T(8,128)(2,1)}, u32[]{:S(2)}, u32[]{:S(2)}) collective-permute-start(bf16[512,896]{1,0:T(8,128)(2,1)} %get-tuple-element.37), channel_id=1, source_target_pairs={{0,16},{8,24},{16,0},{24,8},{1,17},{9,25},{17,1},{25,9},{2,18},{10... | collective-permute-start | bytes 2752520 | tf_op jit(solution)/shard_map/ppermute | solution.py:853
  213.3 36.2 %collective-permute-start.9 = (bf16[512,896]{1,0:T(8,128)(2,1)S(1)}, bf16[512,896]{1,0:T(8,128)(2,1)S(1)}, u32[]{:S(2)}, u32[]{:S(2)}) collective-permute-start(bf16[512,896]{1,0:T(8,128)(2,1)S(1)} %get-tuple-element.38), channel_id=1, source_target_pairs={{0,8},{8,0},{16,24},{24,16},{1,9},{9,1},{17,25},{25,17},{2,10},{10... | collective-permute-start | bytes 2752520 | tf_op jit(solution)/shard_map/ppermute | solution.py:853
  249.4 0.9 copy-start.5
  755.3 39.0 %copy-start.4 = (f32[6,1152]{1,0:T(8,128)S(1)}, f32[6,1152]{1,0:T(8,128)}, u32[]{:S(2)}) copy-start(f32[6,1152]{1,0:T(8,128)} %get-tuple-element.35) | copy-start | bytes 82948
  755.3 39.6 %copy-start.1 = (bf16[512,1152]{1,0:T(8,128)(2,1)S(1)}, bf16[512,1152]{1,0:T(8,128)(2,1)}, u32[]{:S(2)}) copy-start(bf16[512,1152]{1,0:T(8,128)(2,1)} %get-tuple-element.22) | copy-start | bytes 3538948
Sparse Core Ops, SparseCore 0:
  9.8 59.7 all-gather.4
  71.5 57.1 all-gather.2

commit v3 on v2

--- a/solution.py
+++ b/solution.py
@@ -13,7 +13,8 @@
 STEP = 16
 EDGE = 16
 PART = 64
-LAG = 1
+LAG = 2
+TURN = 6
 VMEM = pl.BlockSpec(memory_space=pltpu.VMEM)
 
 
@@ -48,15 +49,32 @@
     return scale, shift
 
 
-def greet(axis):
-    count = lax.axis_size(axis)
-    me = lax.axis_index(axis)
-    barrier = pltpu.get_barrier_semaphore()
-    for step in range(1, count):
-        pl.semaphore_signal(
-            barrier, inc=1, device_id={axis: lax.rem(me + step, count)}, device_id_type=pl.DeviceIdType.MESH
-        )
-    pl.semaphore_wait(barrier, count - 1)
+def greet(*axes):
+    for axis in axes:
+        count = lax.axis_size(axis)
+        me = lax.axis_index(axis)
+        for step in range(1, count):
+            pl.semaphore_signal(
+                pltpu.get_barrier_semaphore(),
+                inc=1,
+                device_id={axis: lax.rem(me + step, count)},
+                device_id_type=pl.DeviceIdType.MESH,
+            )
+
+
+def met(*axes):
+    pl.semaphore_wait(pltpu.get_barrier_semaphore(), sum(lax.axis_size(axis) - 1 for axis in axes))
+
+
+def remote(src, dst, send, recv, axis, target):
+    return pltpu.make_async_remote_copy(
+        src_ref=src,
+        dst_ref=dst,
+        send_sem=send,
+        recv_sem=recv,
+        device_id={axis: target},
+        device_id_type=pl.DeviceIdType.MESH,
+    )
 
 
 def to_all(src, slots, send_sems, recv_sems, axis):
@@ -178,14 +196,13 @@
             place += 2
 
 
-def states_pass(seqs, tokens, channels, entering, out, scale, shift, state, pooled):
+def states_pass(seq, tokens, channels, entering, out, scale, shift, state, pooled):
     def body(at, none):
-        for seq in range(seqs):
-            rows = pl.ds(pl.multiple_of(seq * tokens + at * STEP, STEP), STEP)
-            for lanes in lane_blocks(channels):
-                value = scale[rows, lanes] * entering[seq : seq + 1, lanes] + shift[rows, lanes]
-                state[rows, lanes] = value
-                pooled[rows, lanes] = (out[rows, lanes] * value).astype(BF16)
+        rows = pl.ds(pl.multiple_of(seq * tokens + at * STEP, STEP), STEP)
+        for lanes in lane_blocks(channels):
+            value = scale[rows, lanes] * entering[seq : seq + 1, lanes] + shift[rows, lanes]
+            state[rows, lanes] = value
+            pooled[rows, lanes] = (out[rows, lanes] * value).astype(BF16)
         return none
 
     lax.fori_loop(0, tokens // STEP, body, 0)
@@ -222,7 +239,8 @@
                 for gate, value in enumerate(given):
                     value = value.astype(BF16)
                     grads[whole, gate * channels + lanes.start : gate * channels + lanes.stop] = value
-                    planes[gate, whole, lanes] = value
+                    if planes is not None:
+                        planes[gate, whole, lanes] = value
                     value = value.astype(F32)
                     total = value[:SUB]
                     for half in range(1, STEP // SUB):
@@ -233,20 +251,46 @@
             lax.fori_loop(0, steps, body, message[seq : seq + 1, lanes])
 
 
-def forward_kernel(seqs, tokens, channels, gates, bias, keep, initial, hidden, upd, fgt, out, state, entering, scale, shift, summary, slots, send_sems, recv_sems):
-    greet("seq")
+def forward_kernel(seqs, tokens, channels, paired, gates, bias, keep, initial, *refs):
+    given, refs = refs[: 7 if paired else 6], refs[7 if paired else 6 :]
+    hidden_out, upd_out, fgt_out, out_out, state_out, entering = given[:6]
+    hidden, upd, fgt, out, state, scale, shift, summary, slots, send_sems, recv_sems, save_sems, pair_sems = refs
+    axes = ("seq", "mp") if paired else ("seq",)
+    greet(*axes)
     first_pass(seqs, tokens, channels, gates, bias, keep, upd, fgt, out, scale, shift, summary)
+    met(*axes)
     copies = to_all(summary, slots, send_sems, recv_sems, "seq")
+    saves = [
+        pltpu.make_async_copy(src, dst, save_sems.at[number])
+        for number, (src, dst) in enumerate(((upd, upd_out), (fgt, fgt_out), (out, out_out), (state, state_out), (hidden, hidden_out)))
+    ]
+    for copy in saves[:3]:
+        copy.start()
     for copy in copies:
         copy.wait()
     entering[...] = from_earlier(slots, initial[...], slice(0, seqs), slice(seqs, 2 * seqs), "seq")
-    states_pass(seqs, tokens, channels, entering, out, scale, shift, state, hidden)
+    sent = []
+    for seq in range(seqs):
+        states_pass(seq, tokens, channels, entering, out, scale, shift, state, hidden)
+        if paired:
+            mine = lax.axis_index("mp")
+            rows = pl.ds(seq * tokens, tokens)
+            place = given[6].at[rows, pl.ds(pl.multiple_of(mine * channels, 128), channels)]
+            sent.append(pltpu.make_async_copy(hidden.at[rows], place, pair_sems.at[2, seq]))
+            sent.append(remote(hidden.at[rows], place, pair_sems.at[0, seq], pair_sems.at[1, seq], "mp", 1 - mine))
+            for copy in sent[-2:]:
+                copy.start()
+    for copy in saves[3:]:
+        copy.start()
+    for copy in saves + sent:
+        copy.wait()
 
 
 def top_kernel(seqs, tokens, channels, gates, bias, keep, initial, cotangent, pooled, grads, planes, sums, upd, fgt, out, state, entering, message, scale, shift, back_scale, back_shift, summary, slots, send_sems, recv_sems):
     greet("seq")
     first_pass(seqs, tokens, channels, gates, bias, keep, upd, fgt, out, scale, shift, summary)
     back_pass(seqs, tokens, channels, cotangent, keep, fgt, out, back_scale, back_shift, summary, 2 * seqs)
+    met("seq")
     copies = to_all(summary, slots, send_sems, recv_sems, "seq")
     for copy in copies:
         copy.wait()
@@ -254,7 +298,8 @@
     message[...] = from_later(
         slots, (seqs, channels), slice(2 * seqs, 3 * seqs), slice(3 * seqs, 4 * seqs), "seq"
     )
-    states_pass(seqs, tokens, channels, entering, out, scale, shift, state, pooled)
+    for seq in range(seqs):
+        states_pass(seq, tokens, channels, entering, out, scale, shift, state, pooled)
     grads_pass(seqs, tokens, channels, message, entering, cotangent, keep, upd, fgt, out, state, back_scale, back_shift, grads, planes, sums)
 
 
@@ -295,15 +340,101 @@
         copy.wait_send()
 
 
-def backward_kernel(seqs, tokens, channels, upstream, keep, upd, fgt, out, state, entering, grads, planes, sums, message, scale, shift, summary, slots, send_sems, recv_sems, edges, arrived, edge_sems):
+def backward_kernel(seqs, tokens, channels, upstream, keep, upd, fgt, out, state, entering, grads, sums, message, scale, shift, summary, slots, send_sems, recv_sems, edges, arrived, edge_sems):
     greet("seq")
+    back_pass(seqs, tokens, channels, upstream, keep, fgt, out, scale, shift, summary, 0)
+    met("seq")
+    copies = to_all(summary, slots, send_sems, recv_sems, "seq")
+    for copy in copies:
+        copy.wait()
+    message[...] = from_later(slots, (seqs, channels), slice(0, seqs), slice(seqs, 2 * seqs), "seq")
+    grads_pass(seqs, tokens, channels, message, entering, upstream, keep, upd, fgt, out, state, scale, shift, grads, None, sums)
+    pass_edges(seqs, tokens, grads, edges, arrived, edge_sems)
+
+
+def neighbours():
+    here = lax.axis_index("dp")
+    beside = here + 1 - 2 * lax.rem(here, 2)
+    return here, beside, lax.rem(here + 2, 4), lax.rem(beside + 2, 4)
+
+
+def lower_kernel(seqs, tokens, channels, above, above_columns, mix, keep, upd_in, fgt_in, out_in, state_in, entering, grads, sums, swapped, weights, total, coming, upd, fgt, out, state, message, scale, shift, summary, slots, send_sems, recv_sems, edges, arrived, edge_sems, weight_sems, load_sems, pair_sems, swap_sems):
+    greet("seq", "dp", "mp")
+    mine = lax.axis_index("mp")
+    width = swapped.shape[2]
+
+    def load(step):
+        side = jnp.where(step < 3, 1 - mine, mine)
+        slot = lax.rem(step, 2)
+        return pltpu.make_async_copy(
+            mix.at[lax.rem(step, 3), pl.ds(pl.multiple_of(side * channels, 128), channels), :],
+            weights.at[slot],
+            weight_sems.at[slot],
+        )
+
+    load(0).start()
+    loads = [
+        pltpu.make_async_copy(src, dst, load_sems.at[number])
+        for number, (src, dst) in enumerate(((upd_in, upd), (fgt_in, fgt), (out_in, out), (state_in, state)))
+    ]
+    for copy in loads:
+        copy.start()
+    met("seq", "dp", "mp")
+    plane = neighbours()
+    swaps = []
+    for steps in (3, 1, 2, 0):
+        src = above_columns.at[:, pl.ds(pl.multiple_of(plane[steps] * width, 128), width)]
+        dst = swapped.at[plane[0]]
+        if steps:
+            swaps.append(remote(src, dst, swap_sems.at[0, steps], swap_sems.at[1, steps], "dp", plane[steps]))
+        else:
+            swaps.append(pltpu.make_async_copy(src, dst, swap_sems.at[0, steps]))
+        swaps[-1].start()
+    give = remote(total.at[0], coming, pair_sems.at[0], pair_sems.at[1], "mp", 1 - mine)
+
+    def body(step, none):
+        load(step).wait()
+
+        @pl.when(step < 5)
+        def _():
+            load(step + 1).start()
+
+        side, gate = step // 3, lax.rem(step, 3)
+        rows = above.shape[1] // 2
+        for half in range(2):
+            place = pl.ds(half * rows, rows)
+            term = lax.dot_general(
+                above[gate, place, :], weights[lax.rem(step, 2)], (((1,), (1,)), ((), ())), preferred_element_type=F32
+            )
+            total[side, place, :] = jnp.where(gate == 0, term, total[side, place, :] + term)
+
+        @pl.when(step == 2)
+        def _():
+            give.start()
+
+        return none
+
+    lax.fori_loop(0, 6, body, 0)
+    give.wait_recv()
+    total[1] += coming[...]
+    for copy in loads:
+        copy.wait()
+    upstream = total.at[1]
     back_pass(seqs, tokens, channels, upstream, keep, fgt, out, scale, shift, summary, 0)
     copies = to_all(summary, slots, send_sems, recv_sems, "seq")
     for copy in copies:
         copy.wait()
     message[...] = from_later(slots, (seqs, channels), slice(0, seqs), slice(seqs, 2 * seqs), "seq")
-    grads_pass(seqs, tokens, channels, message, entering, upstream, keep, upd, fgt, out, state, scale, shift, grads, planes, sums)
+    grads_pass(seqs, tokens, channels, message, entering, upstream, keep, upd, fgt, out, state, scale, shift, grads, None, sums)
     pass_edges(seqs, tokens, grads, edges, arrived, edge_sems)
+    give.wait_send()
+    for steps, copy in zip((3, 1, 2, 0), swaps):
+        if steps:
+            copy.wait_send()
+            place = swapped.at[plane[steps]]
+            remote(place, place, swap_sems.at[0, steps], swap_sems.at[1, steps], "dp", plane[steps]).wait_recv()
+        else:
+            copy.wait()
 
 
 def exchange_scratch(rows, channels):
@@ -324,23 +455,32 @@
     return pl.CostEstimate(flops=elements * ops, bytes_accessed=moved, transcendentals=elements * 3)
 
 
-def pool_forward(seqs, tokens, gates, bias, keep, initial):
+def pool_forward(seqs, tokens, paired, gates, bias, keep, initial):
     channels = gates.shape[2]
     rows = seqs * tokens
     whole = jax.ShapeDtypeStruct((rows, channels), F32)
+    shapes = [
+        jax.ShapeDtypeStruct((rows, channels), BF16),
+        whole,
+        whole,
+        whole,
+        whole,
+        jax.ShapeDtypeStruct((seqs, channels), F32),
+    ]
+    hbm = pl.BlockSpec(memory_space=pl.ANY)
+    specs = [hbm] * 5 + [VMEM]
+    if paired:
+        shapes.append(jax.ShapeDtypeStruct((rows, 2 * channels), BF16))
+        specs.append(hbm)
     return pl.pallas_call(
-        functools.partial(forward_kernel, seqs, tokens, channels),
-        out_shape=(
-            jax.ShapeDtypeStruct((rows, channels), BF16),
-            whole,
-            whole,
-            whole,
-            whole,
-            jax.ShapeDtypeStruct((seqs, channels), F32),
-        ),
+        functools.partial(forward_kernel, seqs, tokens, channels, paired),
+        out_shape=shapes,
         in_specs=[VMEM] * 4,
-        out_specs=[VMEM] * 6,
-        scratch_shapes=[pltpu.VMEM((rows, channels), F32)] * 2 + exchange_scratch(2 * seqs, channels),
+        out_specs=specs,
+        scratch_shapes=[pltpu.VMEM((rows, channels), BF16)]
+        + [pltpu.VMEM((rows, channels), F32)] * 6
+        + exchange_scratch(2 * seqs, channels)
+        + [pltpu.SemaphoreType.DMA((5,)), pltpu.SemaphoreType.DMA((3, seqs))],
         compiler_params=params(1),
         cost_estimate=cost(rows * channels, 60, rows * channels * 30),
         name="pool_forward",
@@ -376,11 +516,10 @@
         functools.partial(backward_kernel, seqs, tokens, channels),
         out_shape=(
             jax.ShapeDtypeStruct((rows + EDGE, lanes), BF16),
-            jax.ShapeDtypeStruct((3, rows, channels), BF16),
             jax.ShapeDtypeStruct((3, SUB, channels), F32),
         ),
         in_specs=[VMEM] * 7,
-        out_specs=[VMEM] * 3,
+        out_specs=[VMEM] * 2,
         scratch_shapes=[pltpu.VMEM((seqs, channels), F32)]
         + [whole] * 2
         + exchange_scratch(2 * seqs, channels)
@@ -390,6 +529,44 @@
         cost_estimate=cost(rows * channels, 60, rows * channels * 26),
         name="pool_backward",
     )(upstream, keep, upd, fgt, out, state, entering)
+
+
+def pool_lower(seqs, tokens, above, above_columns, mix, keep, upd, fgt, out, state, entering):
+    rows, channels = upd.shape
+    lanes = above_columns.shape[1]
+    whole = pltpu.VMEM((rows, channels), F32)
+    hbm = pl.BlockSpec(memory_space=pl.ANY)
+    dma = pltpu.SemaphoreType.DMA
+    return pl.pallas_call(
+        functools.partial(lower_kernel, seqs, tokens, channels),
+        out_shape=(
+            jax.ShapeDtypeStruct((rows + EDGE, lanes), BF16),
+            jax.ShapeDtypeStruct((3, SUB, channels), F32),
+            jax.ShapeDtypeStruct((4, rows, lanes // 4), BF16),
+        ),
+        in_specs=[VMEM, hbm, hbm, VMEM, hbm, hbm, hbm, hbm, VMEM],
+        out_specs=[VMEM, VMEM, hbm],
+        scratch_shapes=[
+            pltpu.VMEM((2, channels, channels), BF16),
+            pltpu.VMEM((2, rows, channels), F32),
+            whole,
+            whole,
+            whole,
+            whole,
+            whole,
+            pltpu.VMEM((seqs, channels), F32),
+            whole,
+            whole,
+        ]
+        + exchange_scratch(2 * seqs, channels)
+        + [pltpu.VMEM((EDGE, lanes), BF16)] * 2
+        + [dma((2,)), dma((2,)), dma((4,)), dma((2,)), dma((2, 4))],
+        compiler_params=params(5),
+        cost_estimate=pl.CostEstimate(
+            flops=12 * rows * channels * channels, bytes_accessed=rows * channels * 40, transcendentals=0
+        ),
+        name="pool_lower",
+    )(above, above_columns, mix, keep, upd, fgt, out, state, entering)
 
 
 def shift_up(seqs, tokens, value, edges, result):
@@ -412,12 +589,7 @@
     lax.fori_loop(0, value.shape[0] // STEP, body, 0)
 
 
-def spread_kernel(seqs, tokens, parts, hidden_own, hidden_other, full_own, full_other, *refs):
-    blocks_two, (grads_one, sums, out, sums_out, rows_full, grads, grads_edge, moved, *rest) = refs[:4], refs[4:]
-    _spread(seqs, tokens, parts, (hidden_own, hidden_other), (full_own, full_other), blocks_two, grads_one, sums, out, sums_out, rows_full, grads, grads_edge, moved, *rest)
-
-
-def _spread(seqs, tokens, parts, hidden, full, blocks_two, grads_one, sums, out, sums_out, rows_full, grads, grads_edge, moved, own, ups, downs, acc, across, around, load_sems, swap_sems, up_sems, down_sems, line_send, line_recv, kept_sems, plane_send, plane_recv, sums_sems):
+def spread_kernel(seqs, tokens, parts, turn, hidden, full, grads_two, grads_one, taps, sums, out, input_grad, sums_out, rows_full, grads, grads_edge, moved, own, ups, downs, acc, across, around, every, weights, leaving, coming, load_sems, swap_sems, up_sems, down_sems, line_send, line_recv, column_send, column_recv, kept_sems, plane_send, plane_recv, sums_sems, weight_sems, leaving_sems, coming_sems, result_sems, pair_sems, ready_sem):
     line, plane = lax.axis_size("seq"), lax.axis_size("dp")
     at, here = lax.axis_index("seq"), lax.axis_index("dp")
     unit = line * parts
@@ -426,40 +598,28 @@
     width = own.shape[1]
     block_rows = seqs * tokens
     half = unit // 2
-    beside = here + 1 - 2 * lax.rem(here, 2)
-    below = lax.rem(here + 2, plane)
-    across_from = lax.rem(beside + 2, plane)
-
-    barrier = pltpu.get_barrier_semaphore()
-    for axis, me, count in (("seq", at, line), ("dp", here, plane)):
-        for step in range(1, count):
-            pl.semaphore_signal(
-                barrier, inc=1, device_id={axis: lax.rem(me + step, count)}, device_id_type=pl.DeviceIdType.MESH
-            )
-    pl.semaphore_wait(barrier, line + plane - 2)
-
-    def remote(src, dst, send, recv, axis, target):
-        return pltpu.make_async_remote_copy(
-            src_ref=src,
-            dst_ref=dst,
-            send_sem=send,
-            recv_sem=recv,
-            device_id={axis: target},
-            device_id_type=pl.DeviceIdType.MESH,
-        )
-
+    here, beside, below, across_from = neighbours()
     mine = lax.axis_index("mp")
+    greet("seq", "dp", "mp")
+    met("seq", "dp", "mp")
+
+    def turned(u):
+        return lax.rem(u, turn) == turn - 1
+
+    def direct(u):
+        return lax.rem(u, turn) != turn - 1
+
     wide = rows_full.shape[1] // 2
 
-    def load_rows(pair, number):
-        return [
-            pltpu.make_async_copy(
-                pair[way],
-                rows_full.at[:, pl.ds(pl.multiple_of((mine if way == 0 else 1 - mine) * wide, 128), wide)],
-                load_sems.at[number + way],
-            )
-            for way in range(2)
-        ]
+    def own_rows(value, number, way):
+        place = rows_full.at[:, pl.ds(pl.multiple_of(mine * wide, 128), wide)]
+        if way == 0:
+            return pltpu.make_async_copy(value, place, load_sems.at[number])
+        return remote(value, place, pair_sems.at[0, number], pair_sems.at[1, number], "mp", 1 - mine)
+
+    def other_rows(number):
+        place = rows_full.at[:, pl.ds(pl.multiple_of((1 - mine) * wide, 128), wide)]
+        return remote(place, place, pair_sems.at[0, number], pair_sems.at[1, number], "mp", 1 - mine)
 
     def plane_rows(owner):
         return pl.ds(pl.multiple_of(owner * block_rows, 16), block_rows)
@@ -467,8 +627,8 @@
     def peer(steps):
         return (here, beside, below, across_from)[steps]
 
-    def load_two(steps):
-        return pltpu.make_async_copy(blocks_two[steps], moved.at[plane_rows(peer(steps))], load_sems.at[4 + steps])
+    def load_two():
+        return pltpu.make_async_copy(grads_two, moved, load_sems.at[2])
 
     def swap(steps, edge, arriving=False):
         columns = pl.ds(pl.multiple_of(peer(steps) * width, 128), width)
@@ -488,6 +648,50 @@
             rows_full[:, columns], right[...], (((0,), (0,)), ((), ())), preferred_element_type=F32
         ).astype(BF16)
 
+    narrow = leaving.shape[2]
+    pieces = wide // narrow
+
+    def load_weights(step):
+        first = jnp.where(step < pieces, (1 - mine) * pieces + step, mine * pieces + step - pieces) * narrow
+        slot = lax.rem(step, 2)
+        return pltpu.make_async_copy(
+            taps.at[:, :, pl.ds(pl.multiple_of(first, narrow), narrow), :], weights.at[slot], weight_sems.at[slot]
+        )
+
+    def load_every():
+        return pltpu.make_async_copy(grads_one, every, load_sems.at[3])
+
+    def leave(step):
+        slot = lax.rem(step, 2)
+        return remote(leaving.at[slot], coming.at[step], leaving_sems.at[slot], coming_sems.at[step], "mp", 1 - mine)
+
+    def result(step):
+        return pltpu.make_async_copy(
+            coming.at[step],
+            input_grad.at[:, pl.ds(pl.multiple_of(step * narrow, narrow), narrow)],
+            result_sems.at[step],
+        )
+
+    def input_terms(slot):
+        channels = taps.shape[3]
+        now = jnp.zeros((block_rows, narrow), F32)
+        late = jnp.zeros((block_rows + EDGE, narrow), F32)
+        for gate in range(3):
+            lanes = slice(gate * channels, gate * channels + channels)
+            now += lax.dot_general(
+                every[:block_rows, lanes], weights[slot, 0, gate], (((1,), (1,)), ((), ())), preferred_element_type=F32
+            )
+            late += lax.dot_general(
+                every[:, lanes], weights[slot, 1, gate], (((1,), (1,)), ((), ())), preferred_element_type=F32
+            )
+        row = lax.broadcasted_iota(jnp.int32, now.shape, 0)
+        after = pltpu.roll(late[:block_rows], block_rows - 1, 0)
+        for seq in range(seqs):
+            after = jnp.where(
+                row == seq * tokens + tokens - 1, late[block_rows + seq : block_rows + seq + 1], after
+            )
+        return now + after
+
     def whole(u):
         return pl.ds(pl.multiple_of(u * unit, unit), unit)
 
@@ -514,6 +718,33 @@
             lax.rem(at + (1 if way == 0 else line - 1), line),
         )
 
+    def column(src, steps, u, j, way, hop):
+        number = u // turn * 4 + steps
+        return remote(
+            src,
+            out.at[peer(steps), chunk(u, j)],
+            column_send.at[(number * 2 + way) * (line - 1) + hop],
+            column_recv.at[number * line + j],
+            "seq",
+            lax.rem(at + (1 if way == 0 else line - 1), line),
+        )
+
+    def over_part(src, u, way):
+        return remote(
+            src,
+            out.at[here, chunk(u, at)],
+            plane_send.at[u * 4 + way],
+            plane_recv.at[u * 4 + way],
+            "dp",
+            (beside, below)[way],
+        )
+
+    def onward_part(owner, u, way):
+        place = out.at[owner, pl.ds(pl.multiple_of(u * unit + at * parts + way * (parts // 2), 16), parts // 2)]
+        return remote(
+            place, place, plane_send.at[u * 4 + 2 + way], plane_recv.at[u * 4 + 2 + way], "dp", (below, beside)[way]
+        )
+
     def keep(u):
         return pltpu.make_async_copy(own.at[chunk(u, at)], out.at[here, chunk(u, at)], kept_sems.at[u])
 
@@ -548,20 +779,20 @@
         place = slots.at[lax.rem(me + count - step, count)]
         return remote(place, place, sums_sems.at[number, 0, step - 1], sums_sems.at[number, 1, step - 1], axis, lax.rem(me + step, count))
 
-    for steps in range(4):
-        load_two(steps).start()
-    for copy in load_rows(hidden, 0):
-        copy.start()
+    for way in range(2):
+        own_rows(hidden, 0, way).start()
+    load_two().start()
     for steps in range(4):
         for edge in range(2):
             swap(steps, edge).start()
+    load_every().start()
+    load_weights(0).start()
     across[at] = sums[...]
     for step in range(1, line):
         sums_copy(across, at, line, "seq", 0, step).start()
-    for steps in range(4):
-        load_two(steps).wait()
-    for copy in load_rows(hidden, 0):
-        copy.wait()
+    load_two().wait()
+    own_rows(hidden, 0, 0).wait()
+    other_rows(0).wait_recv()
 
     def stage(index, none):
         @pl.when(index == 1)
@@ -590,8 +821,11 @@
 
         @pl.when(index == blocks - 1)
         def _():
-            for copy in load_rows(full, 2):
-                copy.start()
+            own_rows(hidden, 0, 1).wait_send()
+            own_rows(full, 1, 0).start()
+            pl.semaphore_signal(ready_sem, inc=1, device_id={"mp": 1 - mine}, device_id_type=pl.DeviceIdType.MESH)
+            pl.semaphore_wait(ready_sem, 1)
+            own_rows(full, 1, 1).start()
 
         @pl.when(index == blocks)
         def _():
@@ -602,8 +836,9 @@
                     else:
                         swap(steps, edge).wait()
             shift_up(seqs, tokens, grads, grads_edge, moved)
-            for copy in load_rows(full, 2):
-                copy.wait()
+            own_rows(full, 1, 0).wait()
+            other_rows(1).wait_recv()
+            load_every().wait()
 
         @pl.when((index >= blocks) & (index < units) & (lax.rem(index - blocks, 2) == 0))
         def _():
@@ -612,6 +847,33 @@
         @pl.when((index >= blocks) & (index < units) & (lax.rem(index - blocks, 2) == 1))
         def _():
             own[whole(index), :] = product((index - blocks) // 2, moved)
+
+        k = index - blocks
+
+        @pl.when((k >= 0) & (k < 2 * pieces))
+        def _():
+            load_weights(k).wait()
+
+            @pl.when(k + 1 < 2 * pieces)
+            def _():
+                load_weights(k + 1).start()
+
+            terms = input_terms(lax.rem(k, 2))
+
+            @pl.when(k < pieces)
+            def _():
+                @pl.when(k >= 2)
+                def _():
+                    leave(k - 2).wait_send()
+
+                leaving[lax.rem(k, 2)] = terms
+                leave(k).start()
+
+            @pl.when(k >= pieces)
+            def _():
+                leave(k - pieces).wait_recv()
+                coming[k - pieces] += terms
+                result(k - pieces).start()
 
         u = index - at
 
@@ -668,18 +930,67 @@
             own[chunk(w, at)] = acc[...].astype(BF16)
             keep(w).start()
 
-            @pl.when(at < line - 1)
+            @pl.when(direct(w) & (at < line - 1))
             def _():
                 along(own.at[chunk(w, at)], w, at, 0, 0).start()
 
-            @pl.when(at > 0)
+            @pl.when(direct(w) & (at > 0))
             def _():
                 along(own.at[chunk(w, at)], w, at, 1, 0).start()
 
+            @pl.when(turned(w))
+            def _():
+                for way in range(2):
+                    over_part(own.at[chunk(w, at)], w, way).start()
+
+        c = index - line
+
+        @pl.when((c >= 0) & (c < units) & turned(c))
+        def _():
+            keep(c).wait()
+            for way in range(2):
+                over_part(out.at[(beside, below)[way], chunk(c, at)], c, way).wait_recv()
+                onward_part((beside, below)[way], c, way).start()
+
+        d = index - line - 1
+
+        @pl.when((d >= 0) & (d < units) & turned(d))
+        def _():
+            for way in range(2):
+                onward_part(across_from, d, way).wait_recv()
+
+        for steps in range(4):
+            for hop in range(line):
+                e = index - line - 1 - steps - hop
+
+                @pl.when((e >= 0) & (e < units) & turned(e))
+                def _(e=e, steps=steps, hop=hop):
+                    @pl.when(at >= hop)
+                    def _():
+                        src = out.at[peer(steps), chunk(e, at - hop)]
+                        if hop:
+                            column(src, steps, e, at - hop, 0, 0).wait_recv()
+                        if hop < line - 1:
+
+                            @pl.when(at < line - 1)
+                            def _():
+                                column(src, steps, e, at - hop, 0, hop).start()
+
+                    @pl.when(at + hop < line)
+                    def _():
+                        src = out.at[peer(steps), chunk(e, at + hop)]
+                        if hop:
+                            column(src, steps, e, at + hop, 1, 0).wait_recv()
+                        if hop < line - 1:
+
+                            @pl.when(at > 0)
+                            def _():
+                                column(src, steps, e, at + hop, 1, hop).start()
+
         for hop in range(1, line):
             x = index - (line - 1) - hop
 
-            @pl.when((x >= 0) & (x < units))
+            @pl.when((x >= 0) & (x < units) & direct(x))
             def _(x=x, hop=hop):
                 @pl.when(at >= hop)
                 def _():
@@ -703,7 +1014,7 @@
 
         y = index - 2 * (line - 1)
 
-        @pl.when((y >= 0) & (y < units))
+        @pl.when((y >= 0) & (y < units) & direct(y))
         def _():
             keep(y).wait()
             over(y, 0).start()
@@ -711,7 +1022,7 @@
 
         z = y - LAG
 
-        @pl.when((z >= 0) & (z < units))
+        @pl.when((z >= 0) & (z < units) & direct(z))
         def _():
             for way in range(2):
                 place = out.at[(beside, below)[way], rows(z, 0, unit)]
@@ -720,14 +1031,15 @@
 
         t = z - LAG
 
-        @pl.when((t >= 0) & (t < units))
+        @pl.when((t >= 0) & (t < units) & direct(t))
         def _():
             for way in range(2):
                 corner(t, way).wait_recv()
 
         return none
 
-    lax.fori_loop(0, units + 2 * (line - 1) + 2 * LAG, stage, 0)
+    last_turned = units // turn * turn - 1
+    lax.fori_loop(0, max(units + 2 * (line - 1) + 2 * LAG, last_turned + 2 * line + 4), stage, 0)
 
     def settle(u, none):
         for j in range(1, line):
@@ -744,44 +1056,74 @@
 
         for hop in range(line - 1):
 
-            @pl.when((at >= hop) & (at < line - 1))
+            @pl.when(direct(u) & (at >= hop) & (at < line - 1))
             def _(hop=hop):
                 along(out.at[here, chunk(u, at - hop)], u, at - hop, 0, hop).wait_send()
 
-            @pl.when((at + hop < line) & (at > 0))
+            @pl.when(direct(u) & (at + hop < line) & (at > 0))
             def _(hop=hop):
                 along(out.at[here, chunk(u, at + hop)], u, at + hop, 1, hop).wait_send()
 
-        for way in range(2):
-            over(u, way).wait_send()
-            onward(u, way).wait_send()
+            @pl.when(turned(u) & (at >= hop) & (at < line - 1))
+            def _(hop=hop):
+                for steps in range(4):
+                    column(out.at[here, chunk(u, at - hop)], steps, u, at - hop, 0, hop).wait_send()
+
+            @pl.when(turned(u) & (at + hop < line) & (at > 0))
+            def _(hop=hop):
+                for steps in range(4):
+                    column(out.at[here, chunk(u, at + hop)], steps, u, at + hop, 1, hop).wait_send()
+
+        @pl.when(direct(u))
+        def _():
+            for way in range(2):
+                over(u, way).wait_send()
+                onward(u, way).wait_send()
+
+        @pl.when(turned(u))
+        def _():
+            for way in range(2):
+                over_part(out.at[here, chunk(u, at)], u, way).wait_send()
+                onward_part(here, u, way).wait_send()
+
         return none
 
     lax.fori_loop(0, units, settle, 0)
     for steps in range(1, 4):
         for edge in range(2):
             swap(steps, edge).wait_send()
+    own_rows(full, 1, 1).wait_send()
+    for step in range(pieces - 2, pieces):
+        leave(step).wait_send()
+    for step in range(pieces):
+        result(step).wait()
     for step in range(1, line):
         sums_copy(across, at, line, "seq", 0, step).wait_send()
     for step in range(1, plane):
         sums_copy(around, here, plane, "dp", 1, step).wait_send()
 
 
-def spread(seqs, tokens, hidden, full, blocks_two, grads_one, sums):
+def spread(seqs, tokens, hidden, full, grads_two, grads_one, taps, sums):
     line, plane = lax.axis_size("seq"), lax.axis_size("dp")
-    rows, width = blocks_two[0].shape
-    depth = 2 * full[0].shape[1]
+    width = grads_two.shape[1]
+    rows = grads_two.shape[0] // plane
+    depth = 2 * full.shape[1]
     units = 3 * depth // (line * PART)
+    channels = taps.shape[3]
+    narrow = depth // (units - units // 3)
+    pieces = channels // narrow
+    turns = units // TURN
     dma = pltpu.SemaphoreType.DMA
     hbm = pl.BlockSpec(memory_space=pl.ANY)
     return pl.pallas_call(
-        functools.partial(spread_kernel, seqs, tokens, PART),
+        functools.partial(spread_kernel, seqs, tokens, PART, TURN),
         out_shape=(
             jax.ShapeDtypeStruct((plane, 3 * depth, width), BF16),
+            jax.ShapeDtypeStruct((rows, channels), F32),
             jax.ShapeDtypeStruct(sums.shape, F32),
         ),
-        in_specs=[hbm] * 9 + [VMEM],
-        out_specs=[hbm, VMEM],
+        in_specs=[hbm] * 5 + [VMEM],
+        out_specs=[hbm, hbm, VMEM],
         scratch_shapes=[
             pltpu.VMEM((plane * rows, depth), BF16),
             pltpu.VMEM((plane * rows, width), BF16),
@@ -793,23 +1135,37 @@
             pltpu.VMEM((PART, width), F32),
             pltpu.VMEM((line,) + sums.shape, F32),
             pltpu.VMEM((plane,) + sums.shape, F32),
-            dma((8,)),
+            pltpu.VMEM(grads_one.shape, BF16),
+            pltpu.VMEM((2, 2, 3, narrow, channels), BF16),
+            pltpu.VMEM((2, rows, narrow), F32),
+            pltpu.VMEM((pieces, rows, narrow), F32),
+            dma((4,)),
             dma((2, 8)),
             dma((2, units * (line - 1))),
             dma((2, units * (line - 1))),
             dma((units * 2 * (line - 1),)),
             dma((units * line,)),
+            dma((turns * 4 * 2 * (line - 1),)),
+            dma((turns * 4 * line,)),
             dma((units,)),
             dma((units * 4,)),
             dma((units * 4,)),
             dma((2, 2, max(line, plane) - 1)),
+            dma((2,)),
+            dma((2,)),
+            dma((pieces,)),
+            dma((pieces,)),
+            dma((2, 2)),
+            pltpu.SemaphoreType.REGULAR,
         ],
-        compiler_params=params(4),
+        compiler_params=pltpu.CompilerParams(
+            collective_id=4, has_side_effects=True, vmem_limit_bytes=62 * 2**20
+        ),
         cost_estimate=pl.CostEstimate(
             flops=6 * plane * rows * depth * width, bytes_accessed=depth * width * 48, transcendentals=0
         ),
         name="spread",
-    )(*hidden, *full, *blocks_two, grads_one, sums)
+    )(hidden, full, grads_two, grads_one, taps, sums)
 
 
 def widen_kernel(tiles, blocks, given, out):
@@ -824,7 +1180,7 @@
 
 def widen(gathered, layer_one, depth, channels, unit):
     plane, _, width = gathered.shape
-    rows = 128
+    rows = unit
     steps, per = depth // rows, unit // rows
     taps = 2 if layer_one else 1
 
@@ -844,24 +1200,6 @@
     )(gathered)
 
 
-def plane_tokens(value):
-    every = lax.all_gather(value, "dp", axis=0, tiled=True)
-    return every, lax.ppermute(every, "mp", [(0, 1), (1, 0)])
-
-
-def around_plane(value, steps):
-    return lax.ppermute(value, "dp", [(at, at ^ steps) for at in range(4)])
-
-
-def to_owners(grads, width):
-    here = lax.axis_index("dp")
-    blocks = []
-    for steps, owner in enumerate((here, here + 1 - 2 * lax.rem(here, 2), lax.rem(here + 2, 4), 3 - here)):
-        block = lax.dynamic_slice(grads, (0, owner * width), (grads.shape[0], width))
-        blocks.append(around_plane(block, steps) if steps else block)
-    return blocks
-
-
 def shifted(value, axis, steps):
     count = lax.axis_size(axis)
     initial, last = (max(0, -steps), min(count, count - steps))
@@ -913,43 +1251,49 @@
     gates_one = jnp.einsum(
         "tkd,kgdc->gtc", both.reshape(rows, 2, width), taps, preferred_element_type=F32
     )
-    hidden, upd, fgt, out, state, entering = pool_forward(seqs, tokens, gates_one, bias_one, keep, init_state[0])
-    full_hidden = gather_channels(hidden)
-    gates_two = jnp.einsum("td,gdc->gtc", full_hidden, mix, preferred_element_type=F32)
     line, plane = lax.axis_size("seq"), lax.axis_size("dp")
     tiles = 3 * channels // 128
-    spreads = plane == 4 and lax.axis_size("mp") == 2 and seqs == 2 and channels % 128 == 0 and width % (line * PART) == 0 and line > 1
+    spreads = plane == 4 and lax.axis_size("mp") == 2 and seqs == 2 and channels % 128 == 0
+    spreads = spreads and width % (line * PART) == 0 and line > 1
     block = -(-tiles // plane) * 128
     lanes = plane * block if spreads else 3 * channels
+    hidden, upd, fgt, out, state, entering, *both_cores = pool_forward(
+        seqs, tokens, spreads, gates_one, bias_one, keep, init_state[0]
+    )
+    full_hidden = both_cores[0] if spreads else gather_channels(hidden)
+    gates_two = jnp.einsum("td,gdc->gtc", full_hidden, mix, preferred_element_type=F32)
     pooled_two, grad_two, planes_two, sums_two = pool_top(
         seqs, tokens, lanes, gates_two, bias_two, keep, init_state[1], cotangent.reshape(rows, channels)
     )
-    hidden_terms = jnp.einsum(
-        "gtc,gdc->td", planes_two, mix, preferred_element_type=F32
-    )
-    hidden_grad = sum_channels(hidden_terms)
-    extended, planes_one, sums_one = pool_backward(seqs, tokens, lanes, hidden_grad, keep, upd, fgt, out, state, entering)
-    grad_one = extended[:rows, : 3 * channels]
-    input_terms = jnp.einsum(
-        "gtc,kgdc->ktd", planes_one, taps, preferred_element_type=F32
-    ).reshape(2, seqs, tokens, width)
-    late = input_terms[1]
-    late = jnp.concatenate([late[:, 1:], shifted(late[:, 0], "seq", -1)[:, None]], 1)
-    input_grad = sum_channels((input_terms[0] + late).reshape(rows, width))
-    sums = jnp.concatenate([jnp.sum(sums_one, 1), jnp.sum(sums_two, 1)])
     if spreads:
-        gathered, sums = spread(
+        extended, sums_one, swapped = pool_lower(
+            seqs, tokens, planes_two, grad_two, mix, keep, upd, fgt, out, state, entering
+        )
+        sums = jnp.concatenate([jnp.sum(sums_one, 1), jnp.sum(sums_two, 1)])
+        gathered, input_grad, sums = spread(
             seqs,
             tokens,
-            plane_tokens(hidden),
-            plane_tokens(inputs.reshape(rows, channels)),
-            to_owners(grad_two, block),
+            lax.all_gather(hidden, "dp", axis=0, tiled=True),
+            lax.all_gather(inputs.reshape(rows, channels), "dp", axis=0, tiled=True),
+            swapped.reshape(plane * rows, block),
             extended,
+            taps,
             sums,
         )
         weight_two_grad = widen(gathered, False, width, channels, line * PART)[0].transpose(1, 0, 2)
         weight_one_grad = widen(gathered, True, width, channels, line * PART).transpose(0, 2, 1, 3)
     else:
+        hidden_terms = jnp.einsum("gtc,gdc->td", planes_two, mix, preferred_element_type=F32)
+        hidden_grad = sum_channels(hidden_terms)
+        extended, sums_one = pool_backward(seqs, tokens, lanes, hidden_grad, keep, upd, fgt, out, state, entering)
+        grad_one = extended[:rows]
+        input_terms = jnp.einsum(
+            "tgc,kgdc->ktd", grad_one.reshape(rows, 3, channels), taps, preferred_element_type=F32
+        ).reshape(2, seqs, tokens, width)
+        late = input_terms[1]
+        late = jnp.concatenate([late[:, 1:], shifted(late[:, 0], "seq", -1)[:, None]], 1)
+        input_grad = sum_channels((input_terms[0] + late).reshape(rows, width))
+        sums = jnp.concatenate([jnp.sum(sums_one, 1), jnp.sum(sums_two, 1)])
         sums = lax.psum(sums, ("dp", "seq"))
         weight_two_grad = reduce_weights(dot(full_hidden, grad_two, ((0,), (0,)))).reshape(width, 3, channels)
         weight_one_grad = jnp.stack(

time: 806 us -> 685 us (0.85)
  waiting for transfers between devices: 45.9 us -> 0.97 us
  matrix products: 77.3 us -> 42 us
  other arithmetic: 19.3 us -> 4.7 us
  Pallas kernels: 620 us -> 611 us
    ppermute x7 -> x0, waiting for transfers between devices: 38.2 us -> none  [the longest x3 29.2 us: around_plane(): return lax.ppermute(value, 'dp', [(at, at ^ steps) for at in range(4)])]
    dot_general x2 -> x0, matrix products: 37.3 us -> none  [the longest x1 24.5 us: local(): jnp.einsum('gtc,kgdc->ktd', planes_one, taps, preferred_element_type=F32)]
    add x3 -> x0, other arithmetic: 11.1 us -> none  [the longest x2 6.77 us: sum_channels(): return jnp.where(second, high, low) + other]
  transfers between devices with their start and end apart: 14 -> 5, of which waited for: 7 -> 1; matrix products, arithmetic and copies ran while one was open for 13% -> 7% of each run, Pallas kernels for 9% -> 16%
where the time goes in v3:
time: 685 us; the launch traced here: 684 us
  Pallas kernels  611 us (89%)
  matrix products  42 us (6%)
  between operations  14.2 us (2%)
    pallas_call x1, Pallas kernels, spread(): pl.pallas_call(functools.partial(spread_kernel, seqs, tokens, PART, TURN)...  450 us
    pallas_call x1, Pallas kernels, pool_lower(): pl.pallas_call(functools.partial(lower_kernel, seqs, tokens, channels), o...  64.8 us
    pallas_call x2, Pallas kernels, widen(): pl.pallas_call(functools.partial(widen_kernel, 3, channels // 128), grid=...  52.5 us
    pallas_call x1, Pallas kernels, pool_top(): pl.pallas_call(functools.partial(top_kernel, seqs, tokens, channels), out...  27.1 us
    dot_general x1, matrix products, local(): jnp.einsum('tkd,kgdc->gtc', both.reshape(rows, 2, width), taps, preferred...  25.4 us
    dot_general x1, matrix products, local(): jnp.einsum('td,gdc->gtc', full_hidden, mix, preferred_element_type=F32)  16.6 us
    pallas_call x1, Pallas kernels, pool_forward(): pl.pallas_call(functools.partial(forward_kernel, seqs, tokens, channels,...  16.3 us
  transfers between devices with their start and end apart: 5, of which 1 were waited for; matrix products, arithmetic and copies ran while one was open for 7% of the time, Pallas kernels for 16%

profile of v3, /device:TPU:0, one launch (start us, length us, event | category | flops | bytes accessed | tf_op | source)
XLA Modules:
  0.0 684.0 jit_solution(9785090892096760252)
XLA Ops:
  7.2 0.0 all-gather.5.cloned.1.call-start
  7.2 0.7 all-gather.5.cloned.1.call-update
  7.9 0.0 all-gather.3.cloned.1.call-start
  7.9 0.5 collective-permute-start
  8.5 0.8 slice.18
  9.3 4.5 collective-permute-start.1
  13.8 1.3 slice_bitcast_fusion
  15.1 0.0 collective-permute-done.1
  15.1 0.2 collective-permute-start.2
  15.3 0.7 convert_bitcast_fusion
  16.0 0.3 collective-permute-done.2
  16.3 0.0 collective-permute-done
  16.3 1.5 broadcast_select_fusion
  17.8 0.2 fusion.4
  18.0 0.2 pad_maximum_fusion
  18.2 0.6 pad_maximum_fusion.1
  18.7 25.4 %convolution_bitcast_fusion.gates = f32[3,512,1152]{2,1,0:T(8,128)} fusion(bf16[512,1,2304]{2,0,1:T(8,128)(2,1)S(1)} %bitcast.52, bf16[512,1,2304]{2,0,1:T(8,128)(2,1)S(1)} %bitcast.51, bf16[2,2304,3,1152]{3,1,2,0:T(8,128)(2,1)} %param.11), kind=kOutput, calls=%fused_computation | convolution fusion | flops 16316891136 | bytes 43646976 | tf_op jit(solution)/shard_map/tkd,kgdc->gtc/dot_general | solution.py:1251
  44.2 0.8 broadcast_in_dim.12.keep
  45.0 16.3 %pool_forward.1 = (bf16[512,1152]{1,0:T(8,128)(2,1)}, f32[512,1152]{1,0:T(8,128)}, f32[512,1152]{1,0:T(8,128)}, f32[512,1152]{1,0:T(8,128)}, f32[512,1152]{1,0:T...) custom-call(f32[3,512,1152]{2,1,0:T(8,128)} %convolution_bitcast_fusion.gates, f32[3,1152]{1,0:T(4,128)} %bias.2, ...), custom_call_target="tpu_custom_call" | custom-call | flops 35389440 | bytes 17694720 | tf_op jit(solution)/shard_map/pool_forward/pallas_call | solution.py:475
  61.3 0.0 all-gather.3.cloned.1.call-update
  61.3 16.6 %convolution_bitcast_fusion.1.gates = f32[3,512,1152]{2,1,0:T(8,128)} fusion(bf16[512,2304]{1,0:T(8,128)(2,1)} %get-tuple-element.23, bf16[2304,3,1152]{2,0,1:T(8,128)(2,1)} %param.13), kind=kOutput, calls=%fused_computation.1 | convolution fusion | flops 8153726976 | bytes 25362432 | tf_op jit(solution)/shard_map/td,gdc->gtc/dot_general | solution.py:1264
  77.9 27.1 %pool_top.1 = (bf16[512,1152]{1,0:T(8,128)(2,1)}, bf16[512,3584]{1,0:T(8,128)(2,1)}, bf16[3,512,1152]{2,1,0:T(8,128)(2,1)}, f32[3,8,1152]{2,1,0:T(8,128)}) custom-call(f32[3,512,1152]{2,1,0:T(8,128)} %convolution_bitcast_fusion.1.gates, f32[3,1152]{1,0:T(4,128)} %bias.3, f32[512,128]{1,0:T(8,128)} %broadcast_in_dim.12.keep, ...), custom_call_target="tpu_custom_call" | custom-call | flops 70778880 | bytes 12976128 | tf_op jit(solution)/shard_map/pool_top/pallas_call | solution.py:495
  105.0 64.8 %pool_lower.1 = (bf16[528,3584]{1,0:T(8,128)(2,1)}, f32[3,8,1152]{2,1,0:T(8,128)}, bf16[4,512,896]{2,1,0:T(8,128)(2,1)}) custom-call(bf16[3,512,1152]{2,1,0:T(8,128)(2,1)} %get-tuple-element.26.above, bf16[512,3584]{1,0:T(8,128)(2,1)} %get-tuple-element.27.above_columns, bf16[3,2304,1152]{2,1,0:T(8,128)(2,1)} %bitcast.48, f32[512,128]{1,0:T(8,128)} %broadcast_in_dim.12.keep, ...), custom_call_target="tpu_custom_call" | custom-call | flops 8153726976 | bytes 23592960 | tf_op jit(solution)/shard_map/pool_lower/pallas_call | solution.py:540
  169.8 0.9 reduce_sum.18
  170.8 0.6 pad_maximum_fusion.2.sums
  171.5 449.9 %spread.1 = (bf16[4,6912,896]{2,1,0:T(8,128)(2,1)}, f32[512,1152]{1,0:T(8,128)}, f32[6,1152]{1,0:T(8,128)}) custom-call(bf16[2048,1152]{1,0:T(8,128)(2,1)} %all-gather.3.cloned.1.call-done.hidden, bf16[2048,1152]{1,0:T(8,128)(2,1)} %all-gather.5.cloned.1.call-done.full, bf16[2048,896]{1,0:T(8,128)(2,1)} %bitcast.58, ...), custom_call_target="tpu_custom_call" | custom-call | flops 25367150592 | bytes 99090432 | tf_op jit(solution)/shard_map/spread/pallas_call | solution.py:1118
  621.4 18.1 %widen.3 = f32[1,3,2304,1152]{3,2,1,0:T(8,128)} custom-call(bf16[4,6912,896]{2,1,0:T(8,128)(2,1)} %get-tuple-element.38.given), custom_call_target="tpu_custom_call" | custom-call | tf_op jit(solution)/shard_map/widen/pallas_call | solution.py:1192
  639.4 34.4 %widen.2 = f32[2,3,2304,1152]{3,2,1,0:T(8,128)} custom-call(bf16[4,6912,896]{2,1,0:T(8,128)(2,1)} %get-tuple-element.38.given), custom_call_target="tpu_custom_call" | custom-call | tf_op jit(solution)/shard_map/widen/pallas_call | solution.py:1192
  673.9 0.6 fusion.9
  674.5 1.0 copy.27
  675.5 0.2 copy-done
  675.7 1.4 copy.28
  (15 shorter events, 0.1 us)
Async XLA Ops:
  7.2 164.3 %all-gather.5.cloned.1.call-start = ((), (), s32[]{:S(2)}) async-start(), calls=%async_computation.1 | async-start | bytes 5898240 | tf_op jit(solution)/shard_map/all_gather | solution.py:1277
  7.9 163.6 %all-gather.3.cloned.1.call-start = ((), (), s32[]{:S(2)}) async-start(), calls=%async_computation | async-start | bytes 5898240 | tf_op jit(solution)/shard_map/all_gather | solution.py:1276
  7.9 8.4 %collective-permute-start = (bf16[2,256,1152]{2,1,0:T(8,128)(2,1)}, bf16[2,256,1152]{2,1,0:T(8,128)(2,1)S(1)}, u32[]{:S(2)}, u32[]{:S(2)}) collective-permute-start(bf16[2,256,1152]{2,1,0:T(8,128)(2,1)} %param.8), channel_id=1, source_target_pairs={{0,1},{1,0},{2,3},{3,2},{4,5},{5,4},{6,7},{7,6},{8,9},{9,8},{10,11... | collective-permute-start | bytes 3538952 | tf_op jit(solution)/shard_map/ppermute | solution.py:1213
  9.3 5.8 collective-permute-start.1
  15.1 1.2 collective-permute-start.2
  105.0 65.8 %copy-start.2 = (f32[3,8,1152]{2,1,0:T(8,128)S(1)}, f32[3,8,1152]{2,1,0:T(8,128)}, u32[]{:S(2)}) copy-start(f32[3,8,1152]{2,1,0:T(8,128)} %get-tuple-element.36) | copy-start | bytes 331780
  639.4 34.4 %copy-start.3 = (f32[6,1152]{1,0:T(8,128)S(1)}, f32[6,1152]{1,0:T(8,128)}, u32[]{:S(2)}) copy-start(f32[6,1152]{1,0:T(8,128)} %get-tuple-element.39) | copy-start | bytes 82948
  639.4 35.1 %copy-start.1 = (bf16[512,1152]{1,0:T(8,128)(2,1)S(1)}, bf16[512,1152]{1,0:T(8,128)(2,1)}, u32[]{:S(2)}) copy-start(bf16[512,1152]{1,0:T(8,128)(2,1)} %get-tuple-element.24) | copy-start | bytes 3538948
  673.9 1.9 copy-start
Sparse Core Ops, SparseCore 0:
  9.8 59.7 all-gather.4
  71.5 92.0 all-gather.2

commit v4 on v3

--- a/solution.py
+++ b/solution.py
@@ -15,6 +15,7 @@
 PART = 64
 LAG = 2
 TURN = 6
+TAIL = 2
 VMEM = pl.BlockSpec(memory_space=pltpu.VMEM)
 
 
@@ -358,6 +359,75 @@
     return here, beside, lax.rem(here + 2, 4), lax.rem(beside + 2, 4)
 
 
+def upper_kernel(seqs, tokens, channels, full_hidden, hidden, mix, bias, keep, initial, cotangent, pooled, grads, planes, sums, every, weights, gates, state, entering, message, scale, shift, back_scale, back_shift, summary, slots, send_sems, recv_sems, weight_sems, plane_sems, kept_sem):
+    greet("seq", "dp")
+    here, beside, below, corner = neighbours()
+    rows = seqs * tokens
+    half = rows // 2
+
+    def load(step):
+        slot = lax.rem(step, 2)
+        return pltpu.make_async_copy(
+            mix.at[step // 2, pl.ds(pl.multiple_of(lax.rem(step, 2) * channels, 128), channels), :],
+            weights.at[slot],
+            weight_sems.at[slot],
+        )
+
+    def over(src, owner, way):
+        place = every.at[owner]
+        return remote(src, place, plane_sems.at[0, way], plane_sems.at[1, way], "dp", (beside, below)[way])
+
+    def onward(owner, way):
+        place = every.at[owner, pl.ds(way * half, half)]
+        return remote(place, place, plane_sems.at[0, 2 + way], plane_sems.at[1, 2 + way], "dp", (below, beside)[way])
+
+    load(0).start()
+    kept = pltpu.make_async_copy(hidden, every.at[here], kept_sem)
+    kept.start()
+    met("seq", "dp")
+    for way in range(2):
+        over(hidden, here, way).start()
+
+    def body(step, none):
+        load(step).wait()
+
+        @pl.when(step < 5)
+        def _():
+            load(step + 1).start()
+
+        gate, part = step // 2, lax.rem(step, 2)
+        columns = pl.ds(pl.multiple_of(part * channels, 128), channels)
+        for side in range(2):
+            place = pl.ds(side * half, half)
+            term = jnp.dot(full_hidden[place, columns], weights[part], preferred_element_type=F32)
+            gates[gate, place, :] = jnp.where(part == 0, term, gates[gate, place, :] + term)
+        return none
+
+    lax.fori_loop(0, 6, body, 0)
+    upd, fgt, out = gates.at[0], gates.at[1], gates.at[2]
+    first_pass(seqs, tokens, channels, gates, bias, keep, upd, fgt, out, scale, shift, summary)
+    back_pass(seqs, tokens, channels, cotangent, keep, fgt, out, back_scale, back_shift, summary, 2 * seqs)
+    copies = to_all(summary, slots, send_sems, recv_sems, "seq")
+    for way in range(2):
+        owner = (beside, below)[way]
+        over(every.at[owner], owner, way).wait_recv()
+        onward(owner, way).start()
+    for copy in copies:
+        copy.wait()
+    entering[...] = from_earlier(slots, initial[...], slice(0, seqs), slice(seqs, 2 * seqs), "seq")
+    message[...] = from_later(
+        slots, (seqs, channels), slice(2 * seqs, 3 * seqs), slice(3 * seqs, 4 * seqs), "seq"
+    )
+    for seq in range(seqs):
+        states_pass(seq, tokens, channels, entering, out, scale, shift, state, pooled)
+    grads_pass(seqs, tokens, channels, message, entering, cotangent, keep, upd, fgt, out, state, back_scale, back_shift, grads, planes, sums)
+    for way in range(2):
+        over(hidden, here, way).wait_send()
+        onward((beside, below)[way], way).wait_send()
+        onward(corner, way).wait_recv()
+    kept.wait()
+
+
 def lower_kernel(seqs, tokens, channels, above, above_columns, mix, keep, upd_in, fgt_in, out_in, state_in, entering, grads, sums, swapped, weights, total, coming, upd, fgt, out, state, message, scale, shift, summary, slots, send_sems, recv_sems, edges, arrived, edge_sems, weight_sems, load_sems, pair_sems, swap_sems):
     greet("seq", "dp", "mp")
     mine = lax.axis_index("mp")
@@ -507,6 +577,35 @@
         cost_estimate=cost(rows * channels, 120, rows * channels * 22),
         name="pool_top",
     )(gates, bias, keep, initial, cotangent)
+
+
+def pool_upper(seqs, tokens, lanes, full_hidden, hidden, mix, bias, keep, initial, cotangent):
+    rows, channels = hidden.shape
+    whole = pltpu.VMEM((rows, channels), F32)
+    edge = pltpu.VMEM((seqs, channels), F32)
+    hbm = pl.BlockSpec(memory_space=pl.ANY)
+    dma = pltpu.SemaphoreType.DMA
+    return pl.pallas_call(
+        functools.partial(upper_kernel, seqs, tokens, channels),
+        out_shape=(
+            jax.ShapeDtypeStruct((rows, channels), BF16),
+            jax.ShapeDtypeStruct((rows, lanes), BF16),
+            jax.ShapeDtypeStruct((3, rows, channels), BF16),
+            jax.ShapeDtypeStruct((3, SUB, channels), F32),
+            jax.ShapeDtypeStruct((4, rows, channels), BF16),
+        ),
+        in_specs=[VMEM, hbm, hbm, VMEM, VMEM, VMEM, VMEM],
+        out_specs=[VMEM] * 4 + [hbm],
+        scratch_shapes=[pltpu.VMEM((2, channels, channels), BF16), pltpu.VMEM((3, rows, channels), F32), whole, edge, edge]
+        + [whole] * 4
+        + exchange_scratch(4 * seqs, channels)
+        + [dma((2,)), dma((2, 4)), dma],
+        compiler_params=params(6),
+        cost_estimate=pl.CostEstimate(
+            flops=12 * rows * channels * channels, bytes_accessed=rows * channels * 40, transcendentals=0
+        ),
+        name="pool_upper",
+    )(full_hidden, hidden, mix, bias, keep, initial, cotangent)
 
 
 def pool_backward(seqs, tokens, lanes, upstream, keep, upd, fgt, out, state, entering):
@@ -589,7 +688,7 @@
     lax.fori_loop(0, value.shape[0] // STEP, body, 0)
 
 
-def spread_kernel(seqs, tokens, parts, turn, hidden, full, grads_two, grads_one, taps, sums, out, input_grad, sums_out, rows_full, grads, grads_edge, moved, own, ups, downs, acc, across, around, every, weights, leaving, coming, load_sems, swap_sems, up_sems, down_sems, line_send, line_recv, column_send, column_recv, kept_sems, plane_send, plane_recv, sums_sems, weight_sems, leaving_sems, coming_sems, result_sems, pair_sems, ready_sem):
+def spread_kernel(seqs, tokens, parts, turn, tail, hidden, full, grads_two, grads_one, taps, sums, out, input_grad, sums_out, rows_full, grads, grads_edge, moved, own, ups, downs, acc, across, around, every, weights, leaving, coming, load_sems, swap_sems, up_sems, down_sems, line_send, line_recv, column_send, column_recv, kept_sems, plane_send, plane_recv, sums_sems, weight_sems, leaving_sems, coming_sems, result_sems, pair_sems, ready_sem):
     line, plane = lax.axis_size("seq"), lax.axis_size("dp")
     at, here = lax.axis_index("seq"), lax.axis_index("dp")
     unit = line * parts
@@ -643,7 +742,7 @@
         return remote(src, dst, swap_sems.at[0, number], swap_sems.at[1, number], "dp", peer(steps))
 
     def product(block, right):
-        columns = pl.ds(pl.multiple_of(block * unit, 128), unit)
+        columns = pl.ds(pl.multiple_of(jnp.where(mine == 0, block, blocks - 1 - block) * unit, 128), unit)
         return lax.dot_general(
             rows_full[:, columns], right[...], (((0,), (0,)), ((), ())), preferred_element_type=F32
         ).astype(BF16)
@@ -792,7 +891,6 @@
         sums_copy(across, at, line, "seq", 0, step).start()
     load_two().wait()
     own_rows(hidden, 0, 0).wait()
-    other_rows(0).wait_recv()
 
     def stage(index, none):
         @pl.when(index == 1)
@@ -815,6 +913,14 @@
                 total = total + around[other]
             sums_out[...] = total
 
+        @pl.when(index == wide // unit)
+        def _():
+            other_rows(0).wait_recv()
+
+        @pl.when(index == blocks + 2 * (wide // unit))
+        def _():
+            other_rows(1).wait_recv()
+
         @pl.when(index < blocks)
         def _():
             own[whole(index), :] = product(index, moved)
@@ -837,7 +943,6 @@
                         swap(steps, edge).wait()
             shift_up(seqs, tokens, grads, grads_edge, moved)
             own_rows(full, 1, 0).wait()
-            other_rows(1).wait_recv()
             load_every().wait()
 
         @pl.when((index >= blocks) & (index < units) & (lax.rem(index - blocks, 2) == 0))
@@ -879,7 +984,7 @@
 
         @pl.when((u >= 0) & (u < units))
         def _():
-            for j in range(1, line):
+            for j in range(line - 1, 0, -1):
 
                 @pl.when(at == 0)
                 def _(j=j):
@@ -1017,12 +1122,15 @@
         @pl.when((y >= 0) & (y < units) & direct(y))
         def _():
             keep(y).wait()
+
+        @pl.when((y >= 0) & (y < units - tail) & direct(y))
+        def _():
             over(y, 0).start()
             over(y, 1).start()
 
         z = y - LAG
 
-        @pl.when((z >= 0) & (z < units) & direct(z))
+        @pl.when((z >= 0) & (z < units - tail) & direct(z))
         def _():
             for way in range(2):
                 place = out.at[(beside, below)[way], rows(z, 0, unit)]
@@ -1031,7 +1139,7 @@
 
         t = z - LAG
 
-        @pl.when((t >= 0) & (t < units) & direct(t))
+        @pl.when((t >= 0) & (t < units - tail) & direct(t))
         def _():
             for way in range(2):
                 corner(t, way).wait_recv()
@@ -1039,7 +1147,9 @@
         return none
 
     last_turned = units // turn * turn - 1
-    lax.fori_loop(0, max(units + 2 * (line - 1) + 2 * LAG, last_turned + 2 * line + 4), stage, 0)
+    lax.fori_loop(
+        0, max(units + 2 * (line - 1), units - tail + 2 * (line - 1) + 2 * LAG, last_turned + 2 * line + 4), stage, 0
+    )
 
     def settle(u, none):
         for j in range(1, line):
@@ -1074,7 +1184,7 @@
                 for steps in range(4):
                     column(out.at[here, chunk(u, at + hop)], steps, u, at + hop, 1, hop).wait_send()
 
-        @pl.when(direct(u))
+        @pl.when(direct(u) & (u < units - tail))
         def _():
             for way in range(2):
                 over(u, way).wait_send()
@@ -1116,7 +1226,7 @@
     dma = pltpu.SemaphoreType.DMA
     hbm = pl.BlockSpec(memory_space=pl.ANY)
     return pl.pallas_call(
-        functools.partial(spread_kernel, seqs, tokens, PART, TURN),
+        functools.partial(spread_kernel, seqs, tokens, PART, TURN, TAIL),
         out_shape=(
             jax.ShapeDtypeStruct((plane, 3 * depth, width), BF16),
             jax.ShapeDtypeStruct((rows, channels), F32),
@@ -1168,9 +1278,10 @@
     )(hidden, full, grads_two, grads_one, taps, sums)
 
 
-def widen_kernel(tiles, blocks, given, out):
+def widen_kernel(blocks, core, given, *refs):
+    out = refs[-1]
     per = given.shape[2] // 128
-    for tile in range(tiles * blocks):
+    for tile in range(3 * blocks):
         source, place = divmod(tile, per)
         gate, column = divmod(tile, blocks)
         out[0, gate, :, column * 128 : column * 128 + 128] = given[
@@ -1178,26 +1289,34 @@
         ].astype(F32)
 
 
-def widen(gathered, layer_one, depth, channels, unit):
+def widen(gathered, first, taps, start, count, depth, channels, unit, core, into=None):
     plane, _, width = gathered.shape
-    rows = unit
-    steps, per = depth // rows, unit // rows
-    taps = 2 if layer_one else 1
-
-    def place(tap, step):
-        if not layer_one:
-            return (0, step, 0)
-        return (0, steps + (step // per * 2 + tap) * per + lax.rem(step, per), 0)
-
+    last = depth // unit - 1
+
+    def source(tap, step, core):
+        return (0, first + step * taps + tap, 0)
+
+    def target(tap, step, core):
+        block = start + step
+        return (tap, 0, jnp.where(core[0] == 0, block, last - block), 0)
+
+    given = (core, gathered) if into is None else (core, gathered, into)
     return pl.pallas_call(
-        functools.partial(widen_kernel, 3, channels // 128),
-        grid=(taps, steps),
+        functools.partial(widen_kernel, channels // 128),
+        grid_spec=pltpu.PrefetchScalarGridSpec(
+            num_scalar_prefetch=1,
+            grid=(taps, count),
+            in_specs=[pl.BlockSpec((plane, unit, width), source)] + [pl.BlockSpec(memory_space=pl.ANY)] * (len(given) - 2),
+            out_specs=pl.BlockSpec((1, 3, unit, channels), target),
+        ),
         out_shape=jax.ShapeDtypeStruct((taps, 3, depth, channels), F32),
-        in_specs=[pl.BlockSpec((plane, rows, width), place)],
-        out_specs=pl.BlockSpec((1, 3, rows, channels), lambda tap, step: (tap, 0, step, 0)),
-        compiler_params=pltpu.CompilerParams(vmem_limit_bytes=32 * 2**20),
+        input_output_aliases={} if into is None else {2: 0},
+        compiler_params=pltpu.CompilerParams(vmem_limit_bytes=40 * 2**20),
+        cost_estimate=pl.CostEstimate(
+            flops=0, bytes_accessed=taps * count * unit * (plane * width * 2 + channels * 12), transcendentals=0
+        ),
         name="widen",
-    )(gathered)
+    )(*given)
 
 
 def shifted(value, axis, steps):
@@ -1261,11 +1380,11 @@
         seqs, tokens, spreads, gates_one, bias_one, keep, init_state[0]
     )
     full_hidden = both_cores[0] if spreads else gather_channels(hidden)
-    gates_two = jnp.einsum("td,gdc->gtc", full_hidden, mix, preferred_element_type=F32)
-    pooled_two, grad_two, planes_two, sums_two = pool_top(
-        seqs, tokens, lanes, gates_two, bias_two, keep, init_state[1], cotangent.reshape(rows, channels)
-    )
+    upstream = cotangent.reshape(rows, channels)
     if spreads:
+        pooled_two, grad_two, planes_two, sums_two, every_hidden = pool_upper(
+            seqs, tokens, lanes, full_hidden, hidden, mix, bias_two, keep, init_state[1], upstream
+        )
         extended, sums_one, swapped = pool_lower(
             seqs, tokens, planes_two, grad_two, mix, keep, upd, fgt, out, state, entering
         )
@@ -1273,16 +1392,33 @@
         gathered, input_grad, sums = spread(
             seqs,
             tokens,
-            lax.all_gather(hidden, "dp", axis=0, tiled=True),
+            every_hidden.reshape(plane * rows, channels),
             lax.all_gather(inputs.reshape(rows, channels), "dp", axis=0, tiled=True),
             swapped.reshape(plane * rows, block),
             extended,
             taps,
             sums,
         )
-        weight_two_grad = widen(gathered, False, width, channels, line * PART)[0].transpose(1, 0, 2)
-        weight_one_grad = widen(gathered, True, width, channels, line * PART).transpose(0, 2, 1, 3)
+        unit = line * PART
+        blocks = width // unit
+        core = lax.axis_index("mp").reshape(1)
+        behind = TAIL // 2
+        kept = lax.dynamic_slice(
+            gathered, (lax.axis_index("dp"), (3 * blocks - TAIL) * unit, 0), (1, TAIL * unit, block)
+        )
+        tail = lax.all_gather(kept, "dp", axis=0, tiled=True)
+        weight_two_grad = widen(gathered, 0, 1, 0, blocks, width, channels, unit, core)
+        weight_one_grad = widen(gathered, blocks, 2, 0, blocks - behind, width, channels, unit, core)
+        weight_one_grad = widen(
+            tail, 0, 2, blocks - behind, behind, width, channels, unit, core, weight_one_grad
+        )
+        weight_two_grad = weight_two_grad[0].transpose(1, 0, 2)
+        weight_one_grad = weight_one_grad.transpose(0, 2, 1, 3)
     else:
+        gates_two = jnp.einsum("td,gdc->gtc", full_hidden, mix, preferred_element_type=F32)
+        pooled_two, grad_two, planes_two, sums_two = pool_top(
+            seqs, tokens, lanes, gates_two, bias_two, keep, init_state[1], upstream
+        )
         hidden_terms = jnp.einsum("gtc,gdc->td", planes_two, mix, preferred_element_type=F32)
         hidden_grad = sum_channels(hidden_terms)
         extended, sums_one = pool_backward(seqs, tokens, lanes, hidden_grad, keep, upd, fgt, out, state, entering)

time: 685 us -> 655 us (0.956)
  Pallas kernels: 611 us -> 592 us
  matrix products: 42 us -> 25.5 us
    pallas_call x1, Pallas kernels: 64.8 us -> 47.7 us  [pool_lower(): pl.pallas_call(functools.partial(lower_kernel, seqs, tokens, channels), o...]
    dot_general x1 -> x0, matrix products: 16.6 us -> none  [local(): jnp.einsum('td,gdc->gtc', full_hidden, mix, preferred_element_type=F32)]
    pallas_call x4 -> x5, Pallas kernels: 529 us -> 528 us  [the longest x1 423 us: spread(): pl.pallas_call(functools.partial(spread_kernel, seqs, tokens, PART, TURN,...]
  transfers between devices with their start and end apart: 5 -> 5, of which waited for: 1 -> 1; matrix products, arithmetic and copies ran while one was open for 7% -> 5% of each run, Pallas kernels for 16% -> 25%
where the time goes in v4:
time: 655 us; the launch traced here: 654 us
  Pallas kernels  592 us (90%)
  matrix products  25.5 us (4%)
  between operations  14.2 us (2%)
  local copies, waits for them, and re-layouts  11.3 us (2%)
    pallas_call x1, Pallas kernels, spread(): pl.pallas_call(functools.partial(spread_kernel, seqs, tokens, PART, TURN,...  423 us
    pallas_call x3, Pallas kernels, widen(): pl.pallas_call(functools.partial(widen_kernel, channels // 128), grid_spe...  52.5 us
    pallas_call x1, Pallas kernels, pool_upper(): pl.pallas_call(functools.partial(upper_kernel, seqs, tokens, channels), o...  52.1 us
    pallas_call x1, Pallas kernels, pool_lower(): pl.pallas_call(functools.partial(lower_kernel, seqs, tokens, channels), o...  47.7 us
    dot_general x1, matrix products, local(): jnp.einsum('tkd,kgdc->gtc', both.reshape(rows, 2, width), taps, preferred...  25.5 us
    pallas_call x1, Pallas kernels, pool_forward(): pl.pallas_call(functools.partial(forward_kernel, seqs, tokens, channels,...  16.2 us
  transfers between devices with their start and end apart: 5, of which 1 were waited for; matrix products, arithmetic and copies ran while one was open for 5% of the time, Pallas kernels for 25%

profile of v4, /device:TPU:0, one launch (start us, length us, event | category | flops | bytes accessed | tf_op | source)
XLA Modules:
  0.0 653.8 jit_solution(4473016411065748010)
XLA Ops:
  7.2 0.0 all-gather.3.cloned.1.call-start
  7.2 0.5 collective-permute-start
  7.7 0.2 all-gather.3.cloned.1.call-update
  7.9 0.0 all-gather.5.cloned.1.call-start
  7.9 0.8 slice.18
  8.7 4.9 collective-permute-start.1
  13.7 1.3 slice_bitcast_fusion
  15.0 0.0 collective-permute-done.1
  15.0 0.7 convert_bitcast_fusion
  15.7 0.5 collective-permute-done.2
  16.2 1.5 broadcast_select_fusion
  17.7 0.2 fusion.4
  17.9 0.2 pad_maximum_fusion
  18.1 0.6 pad_maximum_fusion.1
  18.7 25.5 %convolution_bitcast_fusion.gates = f32[3,512,1152]{2,1,0:T(8,128)} fusion(bf16[512,1,2304]{2,0,1:T(8,128)(2,1)S(1)} %bitcast.48, bf16[512,1,2304]{2,0,1:T(8,128)(2,1)S(1)} %bitcast.47, bf16[2,2304,3,1152]{3,1,2,0:T(8,128)(2,1)} %param.11), kind=kOutput, calls=%fused_computation | convolution fusion | flops 16316891136 | bytes 43646976 | tf_op jit(solution)/shard_map/tkd,kgdc->gtc/dot_general | solution.py:1370
  44.1 0.8 broadcast_in_dim.12.keep
  45.0 16.2 %pool_forward.1 = (bf16[512,1152]{1,0:T(8,128)(2,1)}, f32[512,1152]{1,0:T(8,128)}, f32[512,1152]{1,0:T(8,128)}, f32[512,1152]{1,0:T(8,128)}, f32[512,1152]{1,0:T...) custom-call(f32[3,512,1152]{2,1,0:T(8,128)} %convolution_bitcast_fusion.gates, f32[3,1152]{1,0:T(4,128)} %bias.2, ...), custom_call_target="tpu_custom_call" | custom-call | flops 35389440 | bytes 17694720 | tf_op jit(solution)/shard_map/pool_forward/pallas_call | solution.py:545
  61.2 52.1 %pool_upper.1 = (bf16[512,1152]{1,0:T(8,128)(2,1)}, bf16[512,3584]{1,0:T(8,128)(2,1)}, bf16[3,512,1152]{2,1,0:T(8,128)(2,1)}, f32[3,8,1152]{2,1,0:T(8,128)}, bf16[4,512,1152]{2,1,0:T(8,128)(2,1)}) custom-call(bf16[512,2304]{1,0:T(8,128)(2,1)} %get-tuple-element.24.full_hidden, bf16[512,1152]{1,0:T(8,128)(2,1)} %get-tuple-element.25.hidden, ...), custom_call_target="tpu_custom_call" | custom-call | flops 8153726976 | bytes 23592960 | tf_op jit(solution)/shard_map/pool_upper/pallas_call | solution.py:588
  113.4 47.7 %pool_lower.1 = (bf16[528,3584]{1,0:T(8,128)(2,1)}, f32[3,8,1152]{2,1,0:T(8,128)}, bf16[4,512,896]{2,1,0:T(8,128)(2,1)}) custom-call(bf16[3,512,1152]{2,1,0:T(8,128)(2,1)} %get-tuple-element.28.above, bf16[512,3584]{1,0:T(8,128)(2,1)} %get-tuple-element.29.above_columns, bf16[3,2304,1152]{2,1,0:T(8,128)(2,1)} %bitcast.44, f32[512,128]{1,0:T(8,128)} %broadcast_in_dim.12.keep, ...), custom_call_target="tpu_custom_call" | custom-call | flops 8153726976 | bytes 23592960 | tf_op jit(solution)/shard_map/pool_lower/pallas_call | solution.py:639
  161.1 0.9 reduce_sum.18
  162.1 0.6 pad_maximum_fusion.2.sums
  162.7 423.4 %spread.1 = (bf16[4,6912,896]{2,1,0:T(8,128)(2,1)}, f32[512,1152]{1,0:T(8,128)}, f32[6,1152]{1,0:T(8,128)}) custom-call(bf16[2048,1152]{1,0:T(8,128)(2,1)} %bitcast.55, bf16[2048,1152]{1,0:T(8,128)(2,1)} %all-gather.3.cloned.1.call-done.full, bf16[2048,896]{1,0:T(8,128)(2,1)} %bitcast.53, bf16[528,3584]{1,0:T(8,128)(2,1)} %get-tuple-element.36.grads_one, ...), custom_call_target="tpu_custom_call" | custom-call | flops 25367150592 | bytes 99090432 | tf_op jit(solution)/shard_map/spread/pallas_call | solution.py:1228
  586.1 2.2 constant_dynamic-slice_fusion
  588.3 0.0 all-gather.5.cloned.1.call-update
  588.3 18.1 %widen.5 = f32[1,3,2304,1152]{3,2,1,0:T(8,128)} custom-call(s32[1]{0:T(128)} %bitcast.17.core, bf16[4,6912,896]{2,1,0:T(8,128)(2,1)} %get-tuple-element.40.given), custom_call_target="tpu_custom_call" | custom-call | bytes 48365568 | tf_op jit(solution)/shard_map/widen/pallas_call | solution.py:1304
  606.4 30.9 %widen.3.refs_0_ = f32[2,3,2304,1152]{3,2,1,0:T(8,128)} custom-call(s32[1]{0:T(128)} %bitcast.17.core, bf16[4,6912,896]{2,1,0:T(8,128)(2,1)} %get-tuple-element.40.given), custom_call_target="tpu_custom_call" | custom-call | bytes 85983232 | tf_op jit(solution)/shard_map/widen/pallas_call | solution.py:1304
  637.3 0.6 fusion.7
  637.9 2.0 copy-done
  639.9 3.5 widen.4
  643.5 1.0 copy.31
  644.5 1.1 copy-done.1
  645.5 1.4 copy.32
  (18 shorter events, 0.1 us)
Async XLA Ops:
  7.2 155.6 %all-gather.3.cloned.1.call-start = ((), (), s32[]{:S(2)}) async-start(), calls=%async_computation | async-start | bytes 5898240 | tf_op jit(solution)/shard_map/all_gather | solution.py:1396
  7.2 9.0 %collective-permute-start = (bf16[2,256,1152]{2,1,0:T(8,128)(2,1)}, bf16[2,256,1152]{2,1,0:T(8,128)(2,1)S(1)}, u32[]{:S(2)}, u32[]{:S(2)}) collective-permute-start(bf16[2,256,1152]{2,1,0:T(8,128)(2,1)} %param.8), channel_id=1, source_target_pairs={{0,1},{1,0},{2,3},{3,2},{4,5},{5,4},{6,7},{7,6},{8,9},{9,8},{10,11... | collective-permute-start | bytes 3538952 | tf_op jit(solution)/shard_map/ppermute | solution.py:1332
  7.9 630.0 %all-gather.5.cloned.1.call-start = ((), (), s32[]{:S(2)}) async-start(), calls=%async_computation.1 | async-start | bytes 4587520 | tf_op jit(solution)/shard_map/all_gather | solution.py:1409
  8.7 6.3 collective-permute-start.1
  15.0 1.2 collective-permute-start.2
  113.4 48.7 %copy-start.3 = (f32[3,8,1152]{2,1,0:T(8,128)S(1)}, f32[3,8,1152]{2,1,0:T(8,128)}, u32[]{:S(2)}) copy-start(f32[3,8,1152]{2,1,0:T(8,128)} %get-tuple-element.38) | copy-start | bytes 331780
  606.4 30.9 %copy-start.4 = (f32[6,1152]{1,0:T(8,128)S(1)}, f32[6,1152]{1,0:T(8,128)}, u32[]{:S(2)}) copy-start(f32[6,1152]{1,0:T(8,128)} %get-tuple-element.41) | copy-start | bytes 82948
  637.9 2.0 copy-start
  639.9 3.5 copy-start.2
  643.5 2.1 copy-start.1
Sparse Core Ops, SparseCore 0:
  9.8 61.6 all-gather.2
  588.4 46.6 all-gather.4

commit v5 on v4

--- a/solution.py
+++ b/solution.py
@@ -252,39 +252,16 @@
             lax.fori_loop(0, steps, body, message[seq : seq + 1, lanes])
 
 
-def forward_kernel(seqs, tokens, channels, paired, gates, bias, keep, initial, *refs):
-    given, refs = refs[: 7 if paired else 6], refs[7 if paired else 6 :]
-    hidden_out, upd_out, fgt_out, out_out, state_out, entering = given[:6]
-    hidden, upd, fgt, out, state, scale, shift, summary, slots, send_sems, recv_sems, save_sems, pair_sems = refs
-    axes = ("seq", "mp") if paired else ("seq",)
-    greet(*axes)
+def forward_kernel(seqs, tokens, channels, gates, bias, keep, initial, hidden, upd, fgt, out, state, entering, scale, shift, summary, slots, send_sems, recv_sems):
+    greet("seq")
     first_pass(seqs, tokens, channels, gates, bias, keep, upd, fgt, out, scale, shift, summary)
-    met(*axes)
+    met("seq")
     copies = to_all(summary, slots, send_sems, recv_sems, "seq")
-    saves = [
-        pltpu.make_async_copy(src, dst, save_sems.at[number])
-        for number, (src, dst) in enumerate(((upd, upd_out), (fgt, fgt_out), (out, out_out), (state, state_out), (hidden, hidden_out)))
-    ]
-    for copy in saves[:3]:
-        copy.start()
     for copy in copies:
         copy.wait()
     entering[...] = from_earlier(slots, initial[...], slice(0, seqs), slice(seqs, 2 * seqs), "seq")
-    sent = []
     for seq in range(seqs):
         states_pass(seq, tokens, channels, entering, out, scale, shift, state, hidden)
-        if paired:
-            mine = lax.axis_index("mp")
-            rows = pl.ds(seq * tokens, tokens)
-            place = given[6].at[rows, pl.ds(pl.multiple_of(mine * channels, 128), channels)]
-            sent.append(pltpu.make_async_copy(hidden.at[rows], place, pair_sems.at[2, seq]))
-            sent.append(remote(hidden.at[rows], place, pair_sems.at[0, seq], pair_sems.at[1, seq], "mp", 1 - mine))
-            for copy in sent[-2:]:
-                copy.start()
-    for copy in saves[3:]:
-        copy.start()
-    for copy in saves + sent:
-        copy.wait()
 
 
 def top_kernel(seqs, tokens, channels, gates, bias, keep, initial, cotangent, pooled, grads, planes, sums, upd, fgt, out, state, entering, message, scale, shift, back_scale, back_shift, summary, slots, send_sems, recv_sems):
@@ -359,11 +336,192 @@
     return here, beside, lax.rem(here + 2, 4), lax.rem(beside + 2, 4)
 
 
+def relay(value, every, plane_sems, kept_sem):
+    here, beside, below, corner = neighbours()
+    near = (beside, below)
+    half = value.shape[0] // 2
+
+    def over(src, owner, way):
+        place = every.at[owner]
+        return remote(src, place, plane_sems.at[0, way], plane_sems.at[1, way], "dp", near[way])
+
+    def onward(owner, way):
+        place = every.at[owner, pl.ds(way * half, half)]
+        return remote(place, place, plane_sems.at[0, 2 + way], plane_sems.at[1, 2 + way], "dp", near[1 - way])
+
+    def keep():
+        return pltpu.make_async_copy(value, every.at[here], kept_sem)
+
+    def start():
+        for way in range(2):
+            over(value, here, way).start()
+        keep().start()
+
+    def forward():
+        for way in range(2):
+            over(every.at[near[way]], near[way], way).wait_recv()
+            onward(near[way], way).start()
+
+    def finish():
+        for way in range(2):
+            over(value, here, way).wait_send()
+            onward(near[way], way).wait_send()
+            onward(corner, way).wait_recv()
+        keep().wait()
+
+    return start, forward, finish
+
+
+def first_kernel(seqs, tokens, channels, inputs, taps, bias, keep, initial, hidden_out, upd_out, fgt_out, out_out, state_out, entering, both_out, every, both, edges, weights, gates, hidden, state, scale, shift, summary, slots, send_sems, recv_sems, weight_sems, plane_sems, kept_sem, pair_sems, edge_sems, save_sems):
+    axes = ("seq", "dp", "mp")
+    line, at, mine = lax.axis_size("seq"), lax.axis_index("seq"), lax.axis_index("mp")
+    after, before = lax.rem(at + 1, line), lax.rem(at + line - 1, line)
+    greet(*axes)
+    pl.semaphore_signal(
+        pltpu.get_barrier_semaphore(),
+        inc=1,
+        device_id={"seq": before, "mp": 1 - mine},
+        device_id_type=pl.DeviceIdType.MESH,
+    )
+    rows = seqs * tokens
+    half = rows // 2
+    gather_start, gather_forward, gather_finish = relay(inputs, every, plane_sems, kept_sem)
+
+    def load(step):
+        slot = lax.rem(step, 2)
+        side = jnp.where(lax.rem(step // 3, 2) == 0, mine, 1 - mine)
+        return pltpu.make_async_copy(
+            taps.at[step // 6, lax.rem(step, 3), pl.ds(pl.multiple_of(side * channels, 128), channels), :],
+            weights.at[slot],
+            weight_sems.at[slot],
+        )
+
+    def lanes_of(core):
+        return pl.ds(pl.multiple_of(core * channels, 128), channels)
+
+    own = pltpu.make_async_copy(inputs, both.at[0, :, lanes_of(mine)], pair_sems.at[0])
+    give = remote(inputs, both.at[0, :, lanes_of(mine)], pair_sems.at[1], pair_sems.at[2], "mp", 1 - mine)
+    take = remote(inputs, both.at[0, :, lanes_of(1 - mine)], pair_sems.at[1], pair_sems.at[2], "mp", 1 - mine)
+
+    def edge(seq, other, arriving=False):
+        core = jnp.where(other, 1 - mine, mine)
+        return pltpu.make_async_remote_copy(
+            src_ref=inputs.at[seq * tokens + tokens - EDGE : seq * tokens + tokens],
+            dst_ref=edges.at[core if arriving else mine, seq],
+            send_sem=edge_sems.at[0, other, seq],
+            recv_sem=edge_sems.at[1, other, seq],
+            device_id={"seq": after, "mp": core},
+            device_id_type=pl.DeviceIdType.MESH,
+        )
+
+    load(0).start()
+    own.start()
+    pl.semaphore_wait(pltpu.get_barrier_semaphore(), sum(lax.axis_size(axis) - 1 for axis in axes) + 1)
+    give.start()
+
+    @pl.when(at < line - 1)
+    def _():
+        for seq in range(seqs):
+            for other in range(2):
+                edge(seq, other).start()
+
+    @pl.when(at == 0)
+    def _():
+        edges[...] = jnp.zeros(edges.shape, BF16)
+
+    gather_start()
+    own.wait()
+
+    def shift_down():
+        width = 2 * channels
+        steps = tokens // STEP
+
+        def body(index, none):
+            seq, tile = index // steps, lax.rem(index, steps)
+            row = lax.broadcasted_iota(jnp.int32, (STEP, width), 0)
+            place = pl.ds(pl.multiple_of(index * STEP, STEP), STEP)
+            ahead = pl.ds(pl.multiple_of(jnp.maximum(index - 1, 0) * STEP, STEP), STEP)
+            last = both[0, ahead, :].astype(F32)[STEP - 1 : STEP]
+            outer = jnp.concatenate([edges[0, seq], edges[1, seq]], 1).astype(F32)[EDGE - 1 : EDGE]
+            moved = pltpu.roll(both[0, place, :].astype(F32), 1, 0)
+            both[1, place, :] = jnp.where(row == 0, jnp.where(tile == 0, outer, last), moved).astype(BF16)
+            return none
+
+        lax.fori_loop(0, rows // STEP, body, 0)
+
+    def body(step, none):
+        @pl.when(step == 3)
+        def _():
+            take.wait_recv()
+
+        @pl.when(step == 6)
+        def _():
+            @pl.when(at > 0)
+            def _():
+                for seq in range(seqs):
+                    for other in range(2):
+                        edge(seq, other, True).wait_recv()
+
+            shift_down()
+
+        load(step).wait()
+
+        @pl.when(step < 11)
+        def _():
+            load(step + 1).start()
+
+        gate, part = lax.rem(step, 3), lax.rem(step // 3, 2)
+        columns = lanes_of(jnp.where(part == 0, mine, 1 - mine))
+        for side in range(2):
+            place = pl.ds(side * half, half)
+            term = jnp.dot(
+                both[step // 6, place, columns], weights[lax.rem(step, 2)], preferred_element_type=F32
+            )
+            gates[gate, place, :] = jnp.where(step < 3, term, gates[gate, place, :] + term)
+        return none
+
+    lax.fori_loop(0, 12, body, 0)
+    upd, fgt, out = gates.at[0], gates.at[1], gates.at[2]
+    first_pass(seqs, tokens, channels, gates, bias, keep, upd, fgt, out, scale, shift, summary)
+    copies = to_all(summary, slots, send_sems, recv_sems, "seq")
+    gather_forward()
+    saves = [
+        pltpu.make_async_copy(src, dst, save_sems.at[number])
+        for number, (src, dst) in enumerate(((upd, upd_out), (fgt, fgt_out), (out, out_out), (state, state_out), (hidden, hidden_out)))
+    ]
+    for copy in saves[:3]:
+        copy.start()
+    for copy in copies:
+        copy.wait()
+    entering[...] = from_earlier(slots, initial[...], slice(0, seqs), slice(seqs, 2 * seqs), "seq")
+    sent = []
+    for seq in range(seqs):
+        states_pass(seq, tokens, channels, entering, out, scale, shift, state, hidden)
+        part = pl.ds(seq * tokens, tokens)
+        place = both_out.at[part, lanes_of(mine)]
+        sent.append(pltpu.make_async_copy(hidden.at[part], place, pair_sems.at[3 + 3 * seq]))
+        sent.append(remote(hidden.at[part], place, pair_sems.at[4 + 3 * seq], pair_sems.at[5 + 3 * seq], "mp", 1 - mine))
+        for copy in sent[-2:]:
+            copy.start()
+    for copy in saves[3:]:
+        copy.start()
+    for copy in saves + sent:
+        copy.wait()
+    give.wait_send()
+
+    @pl.when(at < line - 1)
+    def _():
+        for seq in range(seqs):
+            for other in range(2):
+                edge(seq, other).wait_send()
+
+    gather_finish()
+
+
 def upper_kernel(seqs, tokens, channels, full_hidden, hidden, mix, bias, keep, initial, cotangent, pooled, grads, planes, sums, every, weights, gates, state, entering, message, scale, shift, back_scale, back_shift, summary, slots, send_sems, recv_sems, weight_sems, plane_sems, kept_sem):
     greet("seq", "dp")
-    here, beside, below, corner = neighbours()
-    rows = seqs * tokens
-    half = rows // 2
+    half = seqs * tokens // 2
+    gather_start, gather_forward, gather_finish = relay(hidden, every, plane_sems, kept_sem)
 
     def load(step):
         slot = lax.rem(step, 2)
@@ -373,20 +531,9 @@
             weight_sems.at[slot],
         )
 
-    def over(src, owner, way):
-        place = every.at[owner]
-        return remote(src, place, plane_sems.at[0, way], plane_sems.at[1, way], "dp", (beside, below)[way])
-
-    def onward(owner, way):
-        place = every.at[owner, pl.ds(way * half, half)]
-        return remote(place, place, plane_sems.at[0, 2 + way], plane_sems.at[1, 2 + way], "dp", (below, beside)[way])
-
     load(0).start()
-    kept = pltpu.make_async_copy(hidden, every.at[here], kept_sem)
-    kept.start()
     met("seq", "dp")
-    for way in range(2):
-        over(hidden, here, way).start()
+    gather_start()
 
     def body(step, none):
         load(step).wait()
@@ -408,10 +555,7 @@
     first_pass(seqs, tokens, channels, gates, bias, keep, upd, fgt, out, scale, shift, summary)
     back_pass(seqs, tokens, channels, cotangent, keep, fgt, out, back_scale, back_shift, summary, 2 * seqs)
     copies = to_all(summary, slots, send_sems, recv_sems, "seq")
-    for way in range(2):
-        owner = (beside, below)[way]
-        over(every.at[owner], owner, way).wait_recv()
-        onward(owner, way).start()
+    gather_forward()
     for copy in copies:
         copy.wait()
     entering[...] = from_earlier(slots, initial[...], slice(0, seqs), slice(seqs, 2 * seqs), "seq")
@@ -421,11 +565,7 @@
     for seq in range(seqs):
         states_pass(seq, tokens, channels, entering, out, scale, shift, state, pooled)
     grads_pass(seqs, tokens, channels, message, entering, cotangent, keep, upd, fgt, out, state, back_scale, back_shift, grads, planes, sums)
-    for way in range(2):
-        over(hidden, here, way).wait_send()
-        onward((beside, below)[way], way).wait_send()
-        onward(corner, way).wait_recv()
-    kept.wait()
+    gather_finish()
 
 
 def lower_kernel(seqs, tokens, channels, above, above_columns, mix, keep, upd_in, fgt_in, out_in, state_in, entering, grads, sums, swapped, weights, total, coming, upd, fgt, out, state, message, scale, shift, summary, slots, send_sems, recv_sems, edges, arrived, edge_sems, weight_sems, load_sems, pair_sems, swap_sems):
@@ -525,32 +665,23 @@
     return pl.CostEstimate(flops=elements * ops, bytes_accessed=moved, transcendentals=elements * 3)
 
 
-def pool_forward(seqs, tokens, paired, gates, bias, keep, initial):
+def pool_forward(seqs, tokens, gates, bias, keep, initial):
     channels = gates.shape[2]
     rows = seqs * tokens
     whole = jax.ShapeDtypeStruct((rows, channels), F32)
-    shapes = [
-        jax.ShapeDtypeStruct((rows, channels), BF16),
-        whole,
-        whole,
-        whole,
-        whole,
-        jax.ShapeDtypeStruct((seqs, channels), F32),
-    ]
-    hbm = pl.BlockSpec(memory_space=pl.ANY)
-    specs = [hbm] * 5 + [VMEM]
-    if paired:
-        shapes.append(jax.ShapeDtypeStruct((rows, 2 * channels), BF16))
-        specs.append(hbm)
     return pl.pallas_call(
-        functools.partial(forward_kernel, seqs, tokens, channels, paired),
-        out_shape=shapes,
+        functools.partial(forward_kernel, seqs, tokens, channels),
+        out_shape=(
+            jax.ShapeDtypeStruct((rows, channels), BF16),
+            whole,
+            whole,
+            whole,
+            whole,
+            jax.ShapeDtypeStruct((seqs, channels), F32),
+        ),
         in_specs=[VMEM] * 4,
-        out_specs=specs,
-        scratch_shapes=[pltpu.VMEM((rows, channels), BF16)]
-        + [pltpu.VMEM((rows, channels), F32)] * 6
-        + exchange_scratch(2 * seqs, channels)
-        + [pltpu.SemaphoreType.DMA((5,)), pltpu.SemaphoreType.DMA((3, seqs))],
+        out_specs=[VMEM] * 6,
+        scratch_shapes=[pltpu.VMEM((rows, channels), F32)] * 2 + exchange_scratch(2 * seqs, channels),
         compiler_params=params(1),
         cost_estimate=cost(rows * channels, 60, rows * channels * 30),
         name="pool_forward",
@@ -577,6 +708,43 @@
         cost_estimate=cost(rows * channels, 120, rows * channels * 22),
         name="pool_top",
     )(gates, bias, keep, initial, cotangent)
+
+
+def pool_first(seqs, tokens, inputs, taps, bias, keep, initial):
+    rows, channels = inputs.shape
+    whole = jax.ShapeDtypeStruct((rows, channels), F32)
+    hbm = pl.BlockSpec(memory_space=pl.ANY)
+    dma = pltpu.SemaphoreType.DMA
+    return pl.pallas_call(
+        functools.partial(first_kernel, seqs, tokens, channels),
+        out_shape=(
+            jax.ShapeDtypeStruct((rows, channels), BF16),
+            whole,
+            whole,
+            whole,
+            whole,
+            jax.ShapeDtypeStruct((seqs, channels), F32),
+            jax.ShapeDtypeStruct((rows, 2 * channels), BF16),
+            jax.ShapeDtypeStruct((4, rows, channels), BF16),
+        ),
+        in_specs=[hbm, hbm, VMEM, VMEM, VMEM],
+        out_specs=[hbm] * 5 + [VMEM, hbm, hbm],
+        scratch_shapes=[
+            pltpu.VMEM((2, rows, 2 * channels), BF16),
+            pltpu.VMEM((2, seqs, EDGE, channels), BF16),
+            pltpu.VMEM((2, channels, channels), BF16),
+            pltpu.VMEM((3, rows, channels), F32),
+            pltpu.VMEM((rows, channels), BF16),
+        ]
+        + [pltpu.VMEM((rows, channels), F32)] * 3
+        + exchange_scratch(2 * seqs, channels)
+        + [dma((2,)), dma((2, 4)), dma, dma((3 + 3 * seqs,)), dma((2, 2, seqs)), dma((5,))],
+        compiler_params=params(7),
+        cost_estimate=pl.CostEstimate(
+            flops=24 * rows * channels * channels, bytes_accessed=rows * channels * 80, transcendentals=0
+        ),
+        name="pool_first",
+    )(inputs, taps, bias, keep, initial)
 
 
 def pool_upper(seqs, tokens, lanes, full_hidden, hidden, mix, bias, keep, initial, cotangent):
@@ -1362,26 +1530,17 @@
     taps = weight_one.transpose(0, 2, 1, 3)
     mix = weight_two.transpose(1, 0, 2)
 
-    edge = gather_channels(shifted(inputs[:, -1], "seq", 1))
-    full = gather_channels(inputs)
-    previous = jnp.concatenate([edge[:, None], full[:, :-1]], 1).reshape(rows, width)
-    full = full.reshape(rows, width)
-    both = jnp.concatenate([full, previous], 1)
-    gates_one = jnp.einsum(
-        "tkd,kgdc->gtc", both.reshape(rows, 2, width), taps, preferred_element_type=F32
-    )
     line, plane = lax.axis_size("seq"), lax.axis_size("dp")
     tiles = 3 * channels // 128
     spreads = plane == 4 and lax.axis_size("mp") == 2 and seqs == 2 and channels % 128 == 0
     spreads = spreads and width % (line * PART) == 0 and line > 1
     block = -(-tiles // plane) * 128
     lanes = plane * block if spreads else 3 * channels
-    hidden, upd, fgt, out, state, entering, *both_cores = pool_forward(
-        seqs, tokens, spreads, gates_one, bias_one, keep, init_state[0]
-    )
-    full_hidden = both_cores[0] if spreads else gather_channels(hidden)
     upstream = cotangent.reshape(rows, channels)
     if spreads:
+        hidden, upd, fgt, out, state, entering, full_hidden, every = pool_first(
+            seqs, tokens, inputs.reshape(rows, channels), taps, bias_one, keep, init_state[0]
+        )
         pooled_two, grad_two, planes_two, sums_two, every_hidden = pool_upper(
             seqs, tokens, lanes, full_hidden, hidden, mix, bias_two, keep, init_state[1], upstream
         )
@@ -1393,7 +1552,7 @@
             seqs,
             tokens,
             every_hidden.reshape(plane * rows, channels),
-            lax.all_gather(inputs.reshape(rows, channels), "dp", axis=0, tiled=True),
+            every.reshape(plane * rows, channels),
             swapped.reshape(plane * rows, block),
             extended,
             taps,
@@ -1415,6 +1574,16 @@
         weight_two_grad = weight_two_grad[0].transpose(1, 0, 2)
         weight_one_grad = weight_one_grad.transpose(0, 2, 1, 3)
     else:
+        edge = gather_channels(shifted(inputs[:, -1], "seq", 1))
+        full = gather_channels(inputs)
+        previous = jnp.concatenate([edge[:, None], full[:, :-1]], 1).reshape(rows, width)
+        full = full.reshape(rows, width)
+        both = jnp.concatenate([full, previous], 1)
+        gates_one = jnp.einsum(
+            "tkd,kgdc->gtc", both.reshape(rows, 2, width), taps, preferred_element_type=F32
+        )
+        hidden, upd, fgt, out, state, entering = pool_forward(seqs, tokens, gates_one, bias_one, keep, init_state[0])
+        full_hidden = gather_channels(hidden)
         gates_two = jnp.einsum("td,gdc->gtc", full_hidden, mix, preferred_element_type=F32)
         pooled_two, grad_two, planes_two, sums_two = pool_top(
             seqs, tokens, lanes, gates_two, bias_two, keep, init_state[1], upstream

time: 655 us -> 647 us (0.988)
  Pallas kernels: 592 us -> 619 us
  matrix products: 25.5 us -> 0 us
    pallas_call x1, Pallas kernels: 16.2 us -> 49.7 us  [pool_first(): pl.pallas_call(functools.partial(first_kernel, seqs, tokens, channels), o...]
    dot_general x1 -> x0, matrix products: 25.5 us -> none  [local(): jnp.einsum('tkd,kgdc->gtc', both.reshape(rows, 2, width), taps, preferred...]
  transfers between devices with their start and end apart: 5 -> 1, of which waited for: 1 -> 0; matrix products, arithmetic and copies ran while one was open for 5% -> 0% of each run, Pallas kernels for 25% -> 8%
where the time goes in v5:
time: 647 us; the launch traced here: 646 us
  Pallas kernels  619 us (96%)
  between operations  14.1 us (2%)
  local copies, waits for them, and re-layouts  10.5 us (2%)
    pallas_call x1, Pallas kernels, spread(): pl.pallas_call(functools.partial(spread_kernel, seqs, tokens, PART, TURN,...  423 us
    pallas_call x3, Pallas kernels, widen(): pl.pallas_call(functools.partial(widen_kernel, channels // 128), grid_spe...  52.5 us
    pallas_call x1, Pallas kernels, pool_first(): pl.pallas_call(functools.partial(first_kernel, seqs, tokens, channels), o...  49.7 us
    pallas_call x1, Pallas kernels, pool_upper(): pl.pallas_call(functools.partial(upper_kernel, seqs, tokens, channels), o...  47.6 us
    pallas_call x1, Pallas kernels, pool_lower(): pl.pallas_call(functools.partial(lower_kernel, seqs, tokens, channels), o...  46.7 us
  transfers between devices with their start and end apart: 1, of which 0 were waited for; matrix products, arithmetic and copies ran while one was open for 0% of the time, Pallas kernels for 8%

profile of v5, /device:TPU:0, one launch (start us, length us, event | category | flops | bytes accessed | tf_op | source)
XLA Modules:
  0.0 646.2 jit_solution(2582392544073225267)
XLA Ops:
  7.2 0.0 all-gather.2.cloned.1.call-start
  7.2 0.7 convert_bitcast_fusion
  7.9 1.3 slice_bitcast_fusion
  9.2 0.8 broadcast_in_dim.8.keep
  10.1 49.7 %pool_first.1 = (bf16[512,1152]{1,0:T(8,128)(2,1)}, f32[512,1152]{1,0:T(8,128)}, f32[512,1152]{1,0:T(8,128)}, f32[512,1152]{1,0:T(8,128)}, f32[512,1152]{1,0:T(8...) custom-call(bf16[512,1152]{1,0:T(8,128)(2,1)} %bitcast.31, ...), custom_call_target="tpu_custom_call" | custom-call | flops 16307453952 | bytes 47185920 | tf_op jit(solution)/shard_map/pool_first/pallas_call | solution.py:718
  59.8 47.6 %pool_upper.1 = (bf16[512,1152]{1,0:T(8,128)(2,1)}, bf16[512,3584]{1,0:T(8,128)(2,1)}, bf16[3,512,1152]{2,1,0:T(8,128)(2,1)}, f32[3,8,1152]{2,1,0:T(8,128)}, bf16[4,512,1152]{2,1,0:T(8,128)(2,1)}) custom-call(bf16[512,2304]{1,0:T(8,128)(2,1)} %get-tuple-element.25.full_hidden, bf16[512,1152]{1,0:T(8,128)(2,1)} %get-tuple-element.26.hidden, ...), custom_call_target="tpu_custom_call" | custom-call | flops 8153726976 | bytes 23592960 | tf_op jit(solution)/shard_map/pool_upper/pallas_call | solution.py:756
  107.3 0.0 copy-start.3
  107.3 46.7 %pool_lower.1 = (bf16[528,3584]{1,0:T(8,128)(2,1)}, f32[3,8,1152]{2,1,0:T(8,128)}, bf16[4,512,896]{2,1,0:T(8,128)(2,1)}) custom-call(bf16[3,512,1152]{2,1,0:T(8,128)(2,1)} %get-tuple-element.30.above, bf16[512,3584]{1,0:T(8,128)(2,1)} %get-tuple-element.31.above_columns, bf16[3,2304,1152]{2,1,0:T(8,128)(2,1)} %bitcast.24, f32[512,128]{1,0:T(8,128)} %broadcast_in_dim.8.keep, ...), custom_call_target="tpu_custom_call" | custom-call | flops 8153726976 | bytes 23592960 | tf_op jit(solution)/shard_map/pool_lower/pallas_call | solution.py:807
  154.1 0.9 reduce_sum.18
  155.0 0.0 copy-done.3
  155.1 0.6 pad_maximum_fusion.sums
  155.7 422.8 %spread.1 = (bf16[4,6912,896]{2,1,0:T(8,128)(2,1)}, f32[512,1152]{1,0:T(8,128)}, f32[6,1152]{1,0:T(8,128)}) custom-call(bf16[2048,1152]{1,0:T(8,128)(2,1)} %bitcast.34, bf16[2048,1152]{1,0:T(8,128)(2,1)} %bitcast.33, bf16[2048,896]{1,0:T(8,128)(2,1)} %bitcast.30, bf16[528,3584]{1,0:T(8,128)(2,1)} %get-tuple-element.38.grads_one, ...), custom_call_target="tpu_custom_call" | custom-call | flops 25367150592 | bytes 99090432 | tf_op jit(solution)/shard_map/spread/pallas_call | solution.py:1396
  578.5 2.2 constant_dynamic-slice_fusion
  580.6 0.0 all-gather.2.cloned.1.call-update
  580.7 18.1 %widen.5 = f32[1,3,2304,1152]{3,2,1,0:T(8,128)} custom-call(s32[1]{0:T(128)} %bitcast.11.core, bf16[4,6912,896]{2,1,0:T(8,128)(2,1)} %get-tuple-element.42.given), custom_call_target="tpu_custom_call" | custom-call | bytes 48365568 | tf_op jit(solution)/shard_map/widen/pallas_call | solution.py:1472
  598.8 0.0 copy-start.4
  598.8 30.9 %widen.3.refs_0_ = f32[2,3,2304,1152]{3,2,1,0:T(8,128)} custom-call(s32[1]{0:T(128)} %bitcast.11.core, bf16[4,6912,896]{2,1,0:T(8,128)(2,1)} %get-tuple-element.42.given), custom_call_target="tpu_custom_call" | custom-call | bytes 85983232 | tf_op jit(solution)/shard_map/widen/pallas_call | solution.py:1472
  629.6 0.0 copy-done.4
  629.6 0.6 fusion
  630.3 0.0 all-gather.2.cloned.1.call-done.given
  630.3 0.0 copy-start
  630.3 2.0 copy-done
  632.3 0.0 copy-start.2
  632.3 3.5 widen.4
  635.8 0.0 copy-start.1
  635.8 0.0 copy-done.2
  635.8 1.0 copy.19
  636.8 1.1 copy-done.1
  637.9 1.4 copy.20
  (2 shorter events, 0.0 us)
Async XLA Ops:
  7.2 623.1 %all-gather.2.cloned.1.call-start = ((), (), s32[]{:S(2)}) async-start(), calls=%async_computation | async-start | bytes 4587520 | tf_op jit(solution)/shard_map/all_gather | solution.py:1568
  107.3 47.7 %copy-start.3 = (f32[3,8,1152]{2,1,0:T(8,128)S(1)}, f32[3,8,1152]{2,1,0:T(8,128)}, u32[]{:S(2)}) copy-start(f32[3,8,1152]{2,1,0:T(8,128)} %get-tuple-element.40) | copy-start | bytes 331780
  598.8 30.9 %copy-start.4 = (f32[6,1152]{1,0:T(8,128)S(1)}, f32[6,1152]{1,0:T(8,128)}, u32[]{:S(2)}) copy-start(f32[6,1152]{1,0:T(8,128)} %get-tuple-element.43) | copy-start | bytes 82948
  630.3 2.0 copy-start
  632.3 3.5 copy-start.2
  635.8 2.1 copy-start.1
Sparse Core Ops, SparseCore 0:
  580.8 47.0 all-gather.1

commit v6 on v5

--- a/solution.py
+++ b/solution.py
@@ -14,7 +14,7 @@
 EDGE = 16
 PART = 64
 LAG = 2
-TURN = 6
+TURN = 4
 TAIL = 2
 VMEM = pl.BlockSpec(memory_space=pltpu.VMEM)
 
@@ -985,21 +985,35 @@
             lax.rem(at + (1 if way == 0 else line - 1), line),
         )
 
-    def column(src, steps, u, j, way, hop):
-        number = u // turn * 4 + steps
+    at_end = (at == 0) | (at == line - 1)
+    share = line // 2 * parts
+    begin = jnp.where(at == 0, 0, line // 2) * parts
+
+    def owner_of(u, j):
+        return jnp.where(turned(u), (line - 1) * (j >= line // 2), j)
+
+    def column(steps, u, way):
+        number = (u // turn * 4 + steps) * 2 + way
+        place = out.at[peer(steps), rows(u, way * share, share)]
         return remote(
-            src,
-            out.at[peer(steps), chunk(u, j)],
-            column_send.at[(number * 2 + way) * (line - 1) + hop],
-            column_recv.at[number * line + j],
+            place,
+            place,
+            column_send.at[number],
+            column_recv.at[number],
             "seq",
             lax.rem(at + (1 if way == 0 else line - 1), line),
         )
+
+    def end_rows(u):
+        return pl.ds(pl.multiple_of(u * unit + begin, parts), share)
+
+    def keep_part(u):
+        return pltpu.make_async_copy(own.at[end_rows(u)], out.at[here, end_rows(u)], kept_sems.at[u])
 
     def over_part(src, u, way):
         return remote(
             src,
-            out.at[here, chunk(u, at)],
+            out.at[here, end_rows(u)],
             plane_send.at[u * 4 + way],
             plane_recv.at[u * 4 + way],
             "dp",
@@ -1007,7 +1021,7 @@
         )
 
     def onward_part(owner, u, way):
-        place = out.at[owner, pl.ds(pl.multiple_of(u * unit + at * parts + way * (parts // 2), 16), parts // 2)]
+        place = out.at[owner, pl.ds(pl.multiple_of(u * unit + begin + way * (share // 2), 16), share // 2)]
         return remote(
             place, place, plane_send.at[u * 4 + 2 + way], plane_recv.at[u * 4 + 2 + way], "dp", (below, beside)[way]
         )
@@ -1154,15 +1168,17 @@
         def _():
             for j in range(line - 1, 0, -1):
 
-                @pl.when(at == 0)
+                owner = owner_of(u, j)
+
+                @pl.when((at == 0) & (at < owner))
                 def _(j=j):
                     up(own.at[chunk(u, j)], u, j).start()
 
-                @pl.when((at > 0) & (at <= j))
+                @pl.when((at > 0) & (at <= owner))
                 def _(j=j):
                     up(ups.at[u, j - 1], u, j).wait_recv()
 
-                @pl.when((at > 0) & (at < j))
+                @pl.when((at > 0) & (at < owner))
                 def _(j=j):
                     ups[u, j - 1] = (ups[u, j - 1].astype(F32) + own[chunk(u, j)].astype(F32)).astype(BF16)
                     up(ups.at[u, j - 1], u, j).start()
@@ -1173,22 +1189,24 @@
         def _():
             for j in range(line - 1):
 
-                @pl.when(at == line - 1)
+                owner = owner_of(v, j)
+
+                @pl.when((at == line - 1) & (at > owner))
                 def _(j=j):
                     down(own.at[chunk(v, j)], v, j).start()
 
-                @pl.when((at < line - 1) & (at >= j))
+                @pl.when((at < line - 1) & (at >= owner))
                 def _(j=j):
                     down(downs.at[v, j], v, j).wait_recv()
 
-                @pl.when((at < line - 1) & (at > j))
+                @pl.when((at < line - 1) & (at > owner))
                 def _(j=j):
                     downs[v, j] = (downs[v, j].astype(F32) + own[chunk(v, j)].astype(F32)).astype(BF16)
                     down(downs.at[v, j], v, j).start()
 
         w = index - (line - 1)
 
-        @pl.when((w >= 0) & (w < units))
+        @pl.when((w >= 0) & (w < units) & direct(w))
         def _():
             acc[...] = own[chunk(w, at)].astype(F32)
 
@@ -1203,62 +1221,62 @@
             own[chunk(w, at)] = acc[...].astype(BF16)
             keep(w).start()
 
-            @pl.when(direct(w) & (at < line - 1))
+            @pl.when(at < line - 1)
             def _():
                 along(own.at[chunk(w, at)], w, at, 0, 0).start()
 
-            @pl.when(direct(w) & (at > 0))
+            @pl.when(at > 0)
             def _():
                 along(own.at[chunk(w, at)], w, at, 1, 0).start()
 
-            @pl.when(turned(w))
+        @pl.when((w >= 0) & (w < units) & turned(w))
+        def _():
+            @pl.when(at == 0)
             def _():
+                for j in range(line // 2):
+                    own[chunk(w, j)] = (own[chunk(w, j)].astype(F32) + downs[w, j].astype(F32)).astype(BF16)
+
+            @pl.when(at == line - 1)
+            def _():
+                for j in range(line // 2, line):
+                    own[chunk(w, j)] = (own[chunk(w, j)].astype(F32) + ups[w, j - 1].astype(F32)).astype(BF16)
+
+            @pl.when(at_end)
+            def _():
+                keep_part(w).start()
                 for way in range(2):
-                    over_part(own.at[chunk(w, at)], w, way).start()
+                    over_part(own.at[end_rows(w)], w, way).start()
 
         c = index - line
 
-        @pl.when((c >= 0) & (c < units) & turned(c))
-        def _():
-            keep(c).wait()
+        @pl.when((c >= 0) & (c < units) & turned(c) & at_end)
+        def _():
+            keep_part(c).wait()
             for way in range(2):
-                over_part(out.at[(beside, below)[way], chunk(c, at)], c, way).wait_recv()
+                over_part(out.at[(beside, below)[way], end_rows(c)], c, way).wait_recv()
                 onward_part((beside, below)[way], c, way).start()
 
         d = index - line - 1
 
-        @pl.when((d >= 0) & (d < units) & turned(d))
+        @pl.when((d >= 0) & (d < units) & turned(d) & at_end)
         def _():
             for way in range(2):
                 onward_part(across_from, d, way).wait_recv()
 
         for steps in range(4):
-            for hop in range(line):
-                e = index - line - 1 - steps - hop
+            for way in range(2):
+                hops = at if way == 0 else line - 1 - at
+                e = d - steps - hops
 
                 @pl.when((e >= 0) & (e < units) & turned(e))
-                def _(e=e, steps=steps, hop=hop):
-                    @pl.when(at >= hop)
+                def _(e=e, steps=steps, way=way, hops=hops):
+                    @pl.when(hops > 0)
                     def _():
-                        src = out.at[peer(steps), chunk(e, at - hop)]
-                        if hop:
-                            column(src, steps, e, at - hop, 0, 0).wait_recv()
-                        if hop < line - 1:
-
-                            @pl.when(at < line - 1)
-                            def _():
-                                column(src, steps, e, at - hop, 0, hop).start()
-
-                    @pl.when(at + hop < line)
+                        column(steps, e, way).wait_recv()
+
+                    @pl.when(hops < line - 1)
                     def _():
-                        src = out.at[peer(steps), chunk(e, at + hop)]
-                        if hop:
-                            column(src, steps, e, at + hop, 1, 0).wait_recv()
-                        if hop < line - 1:
-
-                            @pl.when(at > 0)
-                            def _():
-                                column(src, steps, e, at + hop, 1, hop).start()
+                        column(steps, e, way).start()
 
         for hop in range(1, line):
             x = index - (line - 1) - hop
@@ -1322,13 +1340,13 @@
     def settle(u, none):
         for j in range(1, line):
 
-            @pl.when(at < j)
+            @pl.when(at < owner_of(u, j))
             def _(j=j):
                 up(ups.at[u, j - 1], u, j).wait_send()
 
         for j in range(line - 1):
 
-            @pl.when(at > j)
+            @pl.when(at > owner_of(u, j))
             def _(j=j):
                 down(downs.at[u, j], u, j).wait_send()
 
@@ -1342,15 +1360,17 @@
             def _(hop=hop):
                 along(out.at[here, chunk(u, at + hop)], u, at + hop, 1, hop).wait_send()
 
-            @pl.when(turned(u) & (at >= hop) & (at < line - 1))
-            def _(hop=hop):
-                for steps in range(4):
-                    column(out.at[here, chunk(u, at - hop)], steps, u, at - hop, 0, hop).wait_send()
-
-            @pl.when(turned(u) & (at + hop < line) & (at > 0))
-            def _(hop=hop):
-                for steps in range(4):
-                    column(out.at[here, chunk(u, at + hop)], steps, u, at + hop, 1, hop).wait_send()
+        @pl.when(turned(u))
+        def _():
+            for steps in range(4):
+
+                @pl.when(at < line - 1)
+                def _(steps=steps):
+                    column(steps, u, 0).wait_send()
+
+                @pl.when(at > 0)
+                def _(steps=steps):
+                    column(steps, u, 1).wait_send()
 
         @pl.when(direct(u) & (u < units - tail))
         def _():
@@ -1358,10 +1378,10 @@
                 over(u, way).wait_send()
                 onward(u, way).wait_send()
 
-        @pl.when(turned(u))
+        @pl.when(turned(u) & at_end)
         def _():
             for way in range(2):
-                over_part(out.at[here, chunk(u, at)], u, way).wait_send()
+                over_part(out.at[here, end_rows(u)], u, way).wait_send()
                 onward_part(here, u, way).wait_send()
 
         return none
@@ -1423,8 +1443,8 @@
             dma((2, units * (line - 1))),
             dma((units * 2 * (line - 1),)),
             dma((units * line,)),
-            dma((turns * 4 * 2 * (line - 1),)),
-            dma((turns * 4 * line,)),
+            dma((turns * 8,)),
+            dma((turns * 8,)),
             dma((units,)),
             dma((units * 4,)),
             dma((units * 4,)),
@@ -1532,7 +1552,7 @@
 
     line, plane = lax.axis_size("seq"), lax.axis_size("dp")
     tiles = 3 * channels // 128
-    spreads = plane == 4 and lax.axis_size("mp") == 2 and seqs == 2 and channels % 128 == 0
+    spreads = plane == 4 and lax.axis_size("mp") == 2 and seqs == 2 and line % 2 == 0 and channels % 128 == 0
     spreads = spreads and width % (line * PART) == 0 and line > 1
     block = -(-tiles // plane) * 128
     lanes = plane * block if spreads else 3 * channels

time: 647 us -> 643 us (level)
  no operation moved by 1% of the time
where the time goes in v6:
time: 643 us
  Pallas kernels  616 us (96%)
  between operations  14.1 us (2%)
  local copies, waits for them, and re-layouts  10.5 us (2%)
    pallas_call x1, Pallas kernels, spread(): pl.pallas_call(functools.partial(spread_kernel, seqs, tokens, PART, TURN,...  419 us
    pallas_call x3, Pallas kernels, widen(): pl.pallas_call(functools.partial(widen_kernel, channels // 128), grid_spe...  52.5 us
    pallas_call x1, Pallas kernels, pool_first(): pl.pallas_call(functools.partial(first_kernel, seqs, tokens, channels), o...  49.7 us
    pallas_call x1, Pallas kernels, pool_upper(): pl.pallas_call(functools.partial(upper_kernel, seqs, tokens, channels), o...  47.6 us
    pallas_call x1, Pallas kernels, pool_lower(): pl.pallas_call(functools.partial(lower_kernel, seqs, tokens, channels), o...  46.7 us
  transfers between devices with their start and end apart: 1, of which 0 were waited for; matrix products, arithmetic and copies ran while one was open for 0% of the time, Pallas kernels for 8%

profile of v6, /device:TPU:0, one launch (start us, length us, event | category | flops | bytes accessed | tf_op | source)
XLA Modules:
  0.0 642.5 jit_solution(2009070090912637197)
XLA Ops:
  7.2 0.0 all-gather.2.cloned.1.call-start
  7.2 0.7 convert_bitcast_fusion
  7.9 1.3 slice_bitcast_fusion
  9.2 0.8 broadcast_in_dim.8.keep
  10.1 49.7 %pool_first.1 = (bf16[512,1152]{1,0:T(8,128)(2,1)}, f32[512,1152]{1,0:T(8,128)}, f32[512,1152]{1,0:T(8,128)}, f32[512,1152]{1,0:T(8,128)}, f32[512,1152]{1,0:T(8...) custom-call(bf16[512,1152]{1,0:T(8,128)(2,1)} %bitcast.31, ...), custom_call_target="tpu_custom_call" | custom-call | flops 16307453952 | bytes 47185920 | tf_op jit(solution)/shard_map/pool_first/pallas_call | solution.py:718
  59.8 47.6 %pool_upper.1 = (bf16[512,1152]{1,0:T(8,128)(2,1)}, bf16[512,3584]{1,0:T(8,128)(2,1)}, bf16[3,512,1152]{2,1,0:T(8,128)(2,1)}, f32[3,8,1152]{2,1,0:T(8,128)}, bf16[4,512,1152]{2,1,0:T(8,128)(2,1)}) custom-call(bf16[512,2304]{1,0:T(8,128)(2,1)} %get-tuple-element.25.full_hidden, bf16[512,1152]{1,0:T(8,128)(2,1)} %get-tuple-element.26.hidden, ...), custom_call_target="tpu_custom_call" | custom-call | flops 8153726976 | bytes 23592960 | tf_op jit(solution)/shard_map/pool_upper/pallas_call | solution.py:756
  107.3 0.0 copy-start.3
  107.3 46.7 %pool_lower.1 = (bf16[528,3584]{1,0:T(8,128)(2,1)}, f32[3,8,1152]{2,1,0:T(8,128)}, bf16[4,512,896]{2,1,0:T(8,128)(2,1)}) custom-call(bf16[3,512,1152]{2,1,0:T(8,128)(2,1)} %get-tuple-element.30.above, bf16[512,3584]{1,0:T(8,128)(2,1)} %get-tuple-element.31.above_columns, bf16[3,2304,1152]{2,1,0:T(8,128)(2,1)} %bitcast.24, f32[512,128]{1,0:T(8,128)} %broadcast_in_dim.8.keep, ...), custom_call_target="tpu_custom_call" | custom-call | flops 8153726976 | bytes 23592960 | tf_op jit(solution)/shard_map/pool_lower/pallas_call | solution.py:807
  154.1 0.9 reduce_sum.18
  155.0 0.0 copy-done.3
  155.1 0.6 pad_maximum_fusion.sums
  155.7 419.1 %spread.1 = (bf16[4,6912,896]{2,1,0:T(8,128)(2,1)}, f32[512,1152]{1,0:T(8,128)}, f32[6,1152]{1,0:T(8,128)}) custom-call(bf16[2048,1152]{1,0:T(8,128)(2,1)} %bitcast.34, bf16[2048,1152]{1,0:T(8,128)(2,1)} %bitcast.33, bf16[2048,896]{1,0:T(8,128)(2,1)} %bitcast.30, bf16[528,3584]{1,0:T(8,128)(2,1)} %get-tuple-element.38.grads_one, ...), custom_call_target="tpu_custom_call" | custom-call | flops 25367150592 | bytes 99090432 | tf_op jit(solution)/shard_map/spread/pallas_call | solution.py:1416
  574.8 2.2 constant_dynamic-slice_fusion
  577.0 0.0 all-gather.2.cloned.1.call-update
  577.0 18.2 %widen.5 = f32[1,3,2304,1152]{3,2,1,0:T(8,128)} custom-call(s32[1]{0:T(128)} %bitcast.11.core, bf16[4,6912,896]{2,1,0:T(8,128)(2,1)} %get-tuple-element.42.given), custom_call_target="tpu_custom_call" | custom-call | bytes 48365568 | tf_op jit(solution)/shard_map/widen/pallas_call | solution.py:1492
  595.1 0.0 copy-start.4
  595.2 30.9 %widen.3.refs_0_ = f32[2,3,2304,1152]{3,2,1,0:T(8,128)} custom-call(s32[1]{0:T(128)} %bitcast.11.core, bf16[4,6912,896]{2,1,0:T(8,128)(2,1)} %get-tuple-element.42.given), custom_call_target="tpu_custom_call" | custom-call | bytes 85983232 | tf_op jit(solution)/shard_map/widen/pallas_call | solution.py:1492
  626.0 0.0 copy-done.4
  626.0 0.6 fusion
  626.6 0.0 all-gather.2.cloned.1.call-done.given
  626.6 0.0 copy-start
  626.6 2.0 copy-done
  628.7 0.0 copy-start.2
  628.7 3.5 widen.4
  632.2 0.0 copy-start.1
  632.2 0.0 copy-done.2
  632.2 1.0 copy.19
  633.2 1.1 copy-done.1
  634.3 1.4 copy.20
  (2 shorter events, 0.0 us)
Async XLA Ops:
  7.2 619.5 %all-gather.2.cloned.1.call-start = ((), (), s32[]{:S(2)}) async-start(), calls=%async_computation | async-start | bytes 4587520 | tf_op jit(solution)/shard_map/all_gather | solution.py:1588
  107.3 47.7 %copy-start.3 = (f32[3,8,1152]{2,1,0:T(8,128)S(1)}, f32[3,8,1152]{2,1,0:T(8,128)}, u32[]{:S(2)}) copy-start(f32[3,8,1152]{2,1,0:T(8,128)} %get-tuple-element.40) | copy-start | bytes 331780
  595.1 30.9 %copy-start.4 = (f32[6,1152]{1,0:T(8,128)S(1)}, f32[6,1152]{1,0:T(8,128)}, u32[]{:S(2)}) copy-start(f32[6,1152]{1,0:T(8,128)} %get-tuple-element.43) | copy-start | bytes 82948
  626.6 2.0 copy-start
  628.7 3.5 copy-start.2
  632.2 2.1 copy-start.1
Sparse Core Ops, SparseCore 0:
  577.1 47.8 all-gather.1

commit v7 on v6

--- a/solution.py
+++ b/solution.py
@@ -372,7 +372,7 @@
     return start, forward, finish
 
 
-def first_kernel(seqs, tokens, channels, inputs, taps, bias, keep, initial, hidden_out, upd_out, fgt_out, out_out, state_out, entering, both_out, every, both, edges, weights, gates, hidden, state, scale, shift, summary, slots, send_sems, recv_sems, weight_sems, plane_sems, kept_sem, pair_sems, edge_sems, save_sems):
+def first_stage(seqs, tokens, channels, inputs, taps, bias, keep, initial, full_hidden, every, both, edges, weights, gates, hidden, state, entering, scale, shift, summary, slots, send_sems, recv_sems, weight_sems, plane_sems, kept_sem, pair_sems, edge_sems):
     axes = ("seq", "dp", "mp")
     line, at, mine = lax.axis_size("seq"), lax.axis_index("seq"), lax.axis_index("mp")
     after, before = lax.rem(at + 1, line), lax.rem(at + line - 1, line)
@@ -485,12 +485,6 @@
     first_pass(seqs, tokens, channels, gates, bias, keep, upd, fgt, out, scale, shift, summary)
     copies = to_all(summary, slots, send_sems, recv_sems, "seq")
     gather_forward()
-    saves = [
-        pltpu.make_async_copy(src, dst, save_sems.at[number])
-        for number, (src, dst) in enumerate(((upd, upd_out), (fgt, fgt_out), (out, out_out), (state, state_out), (hidden, hidden_out)))
-    ]
-    for copy in saves[:3]:
-        copy.start()
     for copy in copies:
         copy.wait()
     entering[...] = from_earlier(slots, initial[...], slice(0, seqs), slice(seqs, 2 * seqs), "seq")
@@ -498,28 +492,31 @@
     for seq in range(seqs):
         states_pass(seq, tokens, channels, entering, out, scale, shift, state, hidden)
         part = pl.ds(seq * tokens, tokens)
-        place = both_out.at[part, lanes_of(mine)]
+        place = full_hidden.at[part, lanes_of(mine)]
         sent.append(pltpu.make_async_copy(hidden.at[part], place, pair_sems.at[3 + 3 * seq]))
         sent.append(remote(hidden.at[part], place, pair_sems.at[4 + 3 * seq], pair_sems.at[5 + 3 * seq], "mp", 1 - mine))
         for copy in sent[-2:]:
             copy.start()
-    for copy in saves[3:]:
-        copy.start()
-    for copy in saves + sent:
-        copy.wait()
-    give.wait_send()
-
-    @pl.when(at < line - 1)
-    def _():
-        for seq in range(seqs):
-            for other in range(2):
-                edge(seq, other).wait_send()
-
-    gather_finish()
-
-
-def upper_kernel(seqs, tokens, channels, full_hidden, hidden, mix, bias, keep, initial, cotangent, pooled, grads, planes, sums, every, weights, gates, state, entering, message, scale, shift, back_scale, back_shift, summary, slots, send_sems, recv_sems, weight_sems, plane_sems, kept_sem):
-    greet("seq", "dp")
+
+    def finish():
+        give.wait_send()
+
+        @pl.when(at < line - 1)
+        def _():
+            for seq in range(seqs):
+                for other in range(2):
+                    edge(seq, other).wait_send()
+
+        gather_finish()
+
+    def hidden_here():
+        for copy in sent:
+            copy.wait()
+
+    return hidden_here, finish
+
+
+def upper_stage(seqs, tokens, channels, full_hidden, hidden_here, hidden, mix, bias, keep, initial, cotangent, pooled, grads, planes, sums, every, weights, gates, state, entering, message, scale, shift, back_scale, back_shift, summary, slots, send_sems, recv_sems, weight_sems, plane_sems, kept_sem):
     half = seqs * tokens // 2
     gather_start, gather_forward, gather_finish = relay(hidden, every, plane_sems, kept_sem)
 
@@ -532,8 +529,8 @@
         )
 
     load(0).start()
-    met("seq", "dp")
     gather_start()
+    hidden_here()
 
     def body(step, none):
         load(step).wait()
@@ -565,11 +562,10 @@
     for seq in range(seqs):
         states_pass(seq, tokens, channels, entering, out, scale, shift, state, pooled)
     grads_pass(seqs, tokens, channels, message, entering, cotangent, keep, upd, fgt, out, state, back_scale, back_shift, grads, planes, sums)
-    gather_finish()
-
-
-def lower_kernel(seqs, tokens, channels, above, above_columns, mix, keep, upd_in, fgt_in, out_in, state_in, entering, grads, sums, swapped, weights, total, coming, upd, fgt, out, state, message, scale, shift, summary, slots, send_sems, recv_sems, edges, arrived, edge_sems, weight_sems, load_sems, pair_sems, swap_sems):
-    greet("seq", "dp", "mp")
+    return gather_finish
+
+
+def lower_stage(seqs, tokens, channels, above, above_columns, mix, keep, upd, fgt, out, state, entering, grads, sums, swapped, weights, total, coming, message, scale, shift, summary, slots, send_sems, recv_sems, edges, arrived, edge_sems, weight_sems, pair_sems, swap_sems):
     mine = lax.axis_index("mp")
     width = swapped.shape[2]
 
@@ -583,13 +579,6 @@
         )
 
     load(0).start()
-    loads = [
-        pltpu.make_async_copy(src, dst, load_sems.at[number])
-        for number, (src, dst) in enumerate(((upd_in, upd), (fgt_in, fgt), (out_in, out), (state_in, state)))
-    ]
-    for copy in loads:
-        copy.start()
-    met("seq", "dp", "mp")
     plane = neighbours()
     swaps = []
     for steps in (3, 1, 2, 0):
@@ -627,8 +616,6 @@
     lax.fori_loop(0, 6, body, 0)
     give.wait_recv()
     total[1] += coming[...]
-    for copy in loads:
-        copy.wait()
     upstream = total.at[1]
     back_pass(seqs, tokens, channels, upstream, keep, fgt, out, scale, shift, summary, 0)
     copies = to_all(summary, slots, send_sems, recv_sems, "seq")
@@ -645,6 +632,28 @@
             remote(place, place, swap_sems.at[0, steps], swap_sems.at[1, steps], "dp", plane[steps]).wait_recv()
         else:
             copy.wait()
+
+
+def front_kernel(seqs, tokens, channels, inputs, taps, mix, bias_one, bias_two, keep, initial_one, initial_two, cotangent, pooled, sums_one, sums_two, extended, every, every_hidden, swapped, both, edges, weights, gates_one, gates_two, hidden, full_hidden, planes, grads_two, coming, state_one, state_two, scale, shift, back_scale, back_shift, entering_one, entering_two, message, edge_out, edge_in, *refs):
+    one, two, three = refs[:4], refs[4:8], refs[8:12]
+    weight_sems, inputs_sems, inputs_kept, pair_sems, edge_sems, hidden_sems, hidden_kept, first_sems, give_sems, swap_sems = refs[12:]
+    hidden_here, inputs_end = first_stage(
+        seqs, tokens, channels, inputs, taps, bias_one, keep, initial_one, full_hidden, every, both, edges, weights,
+        gates_one, hidden, state_one, entering_one, scale, shift, *one, weight_sems, inputs_sems, inputs_kept, pair_sems,
+        edge_sems,
+    )
+    hidden_end = upper_stage(
+        seqs, tokens, channels, full_hidden, hidden_here, hidden, mix, bias_two, keep, initial_two, cotangent, pooled,
+        grads_two, planes, sums_two, every_hidden, weights, gates_two, state_two, entering_two, message, scale, shift,
+        back_scale, back_shift, *two, weight_sems, hidden_sems, hidden_kept,
+    )
+    lower_stage(
+        seqs, tokens, channels, planes, grads_two, mix, keep, gates_one.at[0], gates_one.at[1], gates_one.at[2],
+        state_one, entering_one, extended, sums_one, swapped, weights, gates_two, coming, message, scale, shift, *three,
+        edge_out, edge_in, first_sems, weight_sems, give_sems, swap_sems,
+    )
+    inputs_end()
+    hidden_end()
 
 
 def exchange_scratch(rows, channels):
@@ -710,70 +719,52 @@
     )(gates, bias, keep, initial, cotangent)
 
 
-def pool_first(seqs, tokens, inputs, taps, bias, keep, initial):
+def front(seqs, tokens, lanes, inputs, taps, mix, bias_one, bias_two, keep, initial_one, initial_two, cotangent):
     rows, channels = inputs.shape
-    whole = jax.ShapeDtypeStruct((rows, channels), F32)
     hbm = pl.BlockSpec(memory_space=pl.ANY)
     dma = pltpu.SemaphoreType.DMA
+    whole = pltpu.VMEM((rows, channels), F32)
+    few = pltpu.VMEM((seqs, channels), F32)
     return pl.pallas_call(
-        functools.partial(first_kernel, seqs, tokens, channels),
+        functools.partial(front_kernel, seqs, tokens, channels),
         out_shape=(
             jax.ShapeDtypeStruct((rows, channels), BF16),
-            whole,
-            whole,
-            whole,
-            whole,
-            jax.ShapeDtypeStruct((seqs, channels), F32),
-            jax.ShapeDtypeStruct((rows, 2 * channels), BF16),
+            jax.ShapeDtypeStruct((3, SUB, channels), F32),
+            jax.ShapeDtypeStruct((3, SUB, channels), F32),
+            jax.ShapeDtypeStruct((rows + EDGE, lanes), BF16),
             jax.ShapeDtypeStruct((4, rows, channels), BF16),
+            jax.ShapeDtypeStruct((4, rows, channels), BF16),
+            jax.ShapeDtypeStruct((4, rows, lanes // 4), BF16),
         ),
-        in_specs=[hbm, hbm, VMEM, VMEM, VMEM],
-        out_specs=[hbm] * 5 + [VMEM, hbm, hbm],
+        in_specs=[hbm] * 3 + [VMEM] * 6,
+        out_specs=[VMEM] * 4 + [hbm] * 3,
         scratch_shapes=[
             pltpu.VMEM((2, rows, 2 * channels), BF16),
             pltpu.VMEM((2, seqs, EDGE, channels), BF16),
             pltpu.VMEM((2, channels, channels), BF16),
             pltpu.VMEM((3, rows, channels), F32),
+            pltpu.VMEM((3, rows, channels), F32),
             pltpu.VMEM((rows, channels), BF16),
+            pltpu.VMEM((rows, 2 * channels), BF16),
+            pltpu.VMEM((3, rows, channels), BF16),
+            pltpu.VMEM((rows, lanes), BF16),
         ]
-        + [pltpu.VMEM((rows, channels), F32)] * 3
+        + [whole] * 7
+        + [few] * 3
+        + [pltpu.VMEM((EDGE, lanes), BF16)] * 2
         + exchange_scratch(2 * seqs, channels)
-        + [dma((2,)), dma((2, 4)), dma, dma((3 + 3 * seqs,)), dma((2, 2, seqs)), dma((5,))],
-        compiler_params=params(7),
+        + exchange_scratch(4 * seqs, channels)
+        + exchange_scratch(2 * seqs, channels)
+        + [dma((2,)), dma((2, 4)), dma, dma((3 + 3 * seqs,)), dma((2, 2, seqs))]
+        + [dma((2, 4)), dma, dma((2,)), dma((2,)), dma((2, 4))],
+        compiler_params=pltpu.CompilerParams(
+            collective_id=7, has_side_effects=True, vmem_limit_bytes=62 * 2**20
+        ),
         cost_estimate=pl.CostEstimate(
-            flops=24 * rows * channels * channels, bytes_accessed=rows * channels * 80, transcendentals=0
+            flops=48 * rows * channels * channels, bytes_accessed=rows * channels * 160, transcendentals=0
         ),
-        name="pool_first",
-    )(inputs, taps, bias, keep, initial)
-
-
-def pool_upper(seqs, tokens, lanes, full_hidden, hidden, mix, bias, keep, initial, cotangent):
-    rows, channels = hidden.shape
-    whole = pltpu.VMEM((rows, channels), F32)
-    edge = pltpu.VMEM((seqs, channels), F32)
-    hbm = pl.BlockSpec(memory_space=pl.ANY)
-    dma = pltpu.SemaphoreType.DMA
-    return pl.pallas_call(
-        functools.partial(upper_kernel, seqs, tokens, channels),
-        out_shape=(
-            jax.ShapeDtypeStruct((rows, channels), BF16),
-            jax.ShapeDtypeStruct((rows, lanes), BF16),
-            jax.ShapeDtypeStruct((3, rows, channels), BF16),
-            jax.ShapeDtypeStruct((3, SUB, channels), F32),
-            jax.ShapeDtypeStruct((4, rows, channels), BF16),
-        ),
-        in_specs=[VMEM, hbm, hbm, VMEM, VMEM, VMEM, VMEM],
-        out_specs=[VMEM] * 4 + [hbm],
-        scratch_shapes=[pltpu.VMEM((2, channels, channels), BF16), pltpu.VMEM((3, rows, channels), F32), whole, edge, edge]
-        + [whole] * 4
-        + exchange_scratch(4 * seqs, channels)
-        + [dma((2,)), dma((2, 4)), dma],
-        compiler_params=params(6),
-        cost_estimate=pl.CostEstimate(
-            flops=12 * rows * channels * channels, bytes_accessed=rows * channels * 40, transcendentals=0
-        ),
-        name="pool_upper",
-    )(full_hidden, hidden, mix, bias, keep, initial, cotangent)
+        name="front",
+    )(inputs, taps, mix, bias_one, bias_two, keep, initial_one, initial_two, cotangent)
 
 
 def pool_backward(seqs, tokens, lanes, upstream, keep, upd, fgt, out, state, entering):
@@ -796,44 +787,6 @@
         cost_estimate=cost(rows * channels, 60, rows * channels * 26),
         name="pool_backward",
     )(upstream, keep, upd, fgt, out, state, entering)
-
-
-def pool_lower(seqs, tokens, above, above_columns, mix, keep, upd, fgt, out, state, entering):
-    rows, channels = upd.shape
-    lanes = above_columns.shape[1]
-    whole = pltpu.VMEM((rows, channels), F32)
-    hbm = pl.BlockSpec(memory_space=pl.ANY)
-    dma = pltpu.SemaphoreType.DMA
-    return pl.pallas_call(
-        functools.partial(lower_kernel, seqs, tokens, channels),
-        out_shape=(
-            jax.ShapeDtypeStruct((rows + EDGE, lanes), BF16),
-            jax.ShapeDtypeStruct((3, SUB, channels), F32),
-            jax.ShapeDtypeStruct((4, rows, lanes // 4), BF16),
-        ),
-        in_specs=[VMEM, hbm, hbm, VMEM, hbm, hbm, hbm, hbm, VMEM],
-        out_specs=[VMEM, VMEM, hbm],
-        scratch_shapes=[
-            pltpu.VMEM((2, channels, channels), BF16),
-            pltpu.VMEM((2, rows, channels), F32),
-            whole,
-            whole,
-            whole,
-            whole,
-            whole,
-            pltpu.VMEM((seqs, channels), F32),
-            whole,
-            whole,
-        ]
-        + exchange_scratch(2 * seqs, channels)
-        + [pltpu.VMEM((EDGE, lanes), BF16)] * 2
-        + [dma((2,)), dma((2,)), dma((4,)), dma((2,)), dma((2, 4))],
-        compiler_params=params(5),
-        cost_estimate=pl.CostEstimate(
-            flops=12 * rows * channels * channels, bytes_accessed=rows * channels * 40, transcendentals=0
-        ),
-        name="pool_lower",
-    )(above, above_columns, mix, keep, upd, fgt, out, state, entering)
 
 
 def shift_up(seqs, tokens, value, edges, result):
@@ -1558,14 +1511,19 @@
     lanes = plane * block if spreads else 3 * channels
     upstream = cotangent.reshape(rows, channels)
     if spreads:
-        hidden, upd, fgt, out, state, entering, full_hidden, every = pool_first(
-            seqs, tokens, inputs.reshape(rows, channels), taps, bias_one, keep, init_state[0]
-        )
-        pooled_two, grad_two, planes_two, sums_two, every_hidden = pool_upper(
-            seqs, tokens, lanes, full_hidden, hidden, mix, bias_two, keep, init_state[1], upstream
-        )
-        extended, sums_one, swapped = pool_lower(
-            seqs, tokens, planes_two, grad_two, mix, keep, upd, fgt, out, state, entering
+        pooled_two, sums_one, sums_two, extended, every, every_hidden, swapped = front(
+            seqs,
+            tokens,
+            lanes,
+            inputs.reshape(rows, channels),
+            taps,
+            mix,
+            bias_one,
+            bias_two,
+            keep,
+            init_state[0],
+            init_state[1],
+            upstream,
         )
         sums = jnp.concatenate([jnp.sum(sums_one, 1), jnp.sum(sums_two, 1)])
         gathered, input_grad, sums = spread(

time: 643 us -> 630 us (0.980)
  Pallas kernels: 616 us -> 602 us
    pallas_call x3 -> x1, Pallas kernels: 144 us -> 131 us  [front(): pl.pallas_call(functools.partial(front_kernel, seqs, tokens, channels), o...]
where the time goes in v7:
time: 630 us; the launch traced here: 629 us
  Pallas kernels  602 us (96%)
  between operations  14.1 us (2%)
  local copies, waits for them, and re-layouts  9.43 us (1%)
    pallas_call x1, Pallas kernels, spread(): pl.pallas_call(functools.partial(spread_kernel, seqs, tokens, PART, TURN,...  419 us
    pallas_call x1, Pallas kernels, front(): pl.pallas_call(functools.partial(front_kernel, seqs, tokens, channels), o...  131 us
    pallas_call x3, Pallas kernels, widen(): pl.pallas_call(functools.partial(widen_kernel, channels // 128), grid_spe...  52.5 us
  transfers between devices with their start and end apart: 1, of which 0 were waited for; matrix products, arithmetic and copies ran while one was open for 0% of the time, Pallas kernels for 8%

profile of v7, /device:TPU:0, one launch (start us, length us, event | category | flops | bytes accessed | tf_op | source)
XLA Modules:
  0.0 629.2 jit_solution(12095226698972201886)
XLA Ops:
  7.2 0.0 all-gather.2.cloned.1.call-start
  7.2 0.7 convert_bitcast_fusion
  7.9 1.3 slice_bitcast_fusion
  9.2 0.8 broadcast_in_dim.8.keep
  10.1 131.0 %front.1 = (bf16[512,1152]{1,0:T(8,128)(2,1)}, f32[3,8,1152]{2,1,0:T(8,128)}, f32[3,8,1152]{2,1,0:T(8,128)}, bf16[528,3584]{1,0:T(8,128)(2,1)}, bf16[4,512,1152]...) custom-call(bf16[512,1152]{1,0:T(8,128)(2,1)} %bitcast.29, ...), custom_call_target="tpu_custom_call" | custom-call | flops 32614907904 | bytes 94371840 | tf_op jit(solution)/shard_map/front/pallas_call | solution.py:728
  141.1 0.9 reduce_sum.18
  142.0 0.9 reduce_sum.19
  143.0 0.6 pad_maximum_fusion.sums
  143.6 418.9 %spread.1 = (bf16[4,6912,896]{2,1,0:T(8,128)(2,1)}, f32[512,1152]{1,0:T(8,128)}, f32[6,1152]{1,0:T(8,128)}) custom-call(bf16[2048,1152]{1,0:T(8,128)(2,1)} %bitcast.32, bf16[2048,1152]{1,0:T(8,128)(2,1)} %bitcast.31, bf16[2048,896]{1,0:T(8,128)(2,1)} %bitcast.33, bf16[528,3584]{1,0:T(8,128)(2,1)} %get-tuple-element.20.grads_one, ...), custom_call_target="tpu_custom_call" | custom-call | flops 25367150592 | bytes 99090432 | tf_op jit(solution)/shard_map/spread/pallas_call | solution.py:1369
  562.5 2.2 constant_dynamic-slice_fusion
  564.7 0.0 all-gather.2.cloned.1.call-update
  564.7 18.2 %widen.5 = f32[1,3,2304,1152]{3,2,1,0:T(8,128)} custom-call(s32[1]{0:T(128)} %bitcast.11.core, bf16[4,6912,896]{2,1,0:T(8,128)(2,1)} %get-tuple-element.24.given), custom_call_target="tpu_custom_call" | custom-call | bytes 48365568 | tf_op jit(solution)/shard_map/widen/pallas_call | solution.py:1445
  582.9 0.0 copy-start.3
  582.9 30.9 %widen.3.refs_0_ = f32[2,3,2304,1152]{3,2,1,0:T(8,128)} custom-call(s32[1]{0:T(128)} %bitcast.11.core, bf16[4,6912,896]{2,1,0:T(8,128)(2,1)} %get-tuple-element.24.given), custom_call_target="tpu_custom_call" | custom-call | bytes 85983232 | tf_op jit(solution)/shard_map/widen/pallas_call | solution.py:1445
  613.7 0.0 copy-done.3
  613.7 0.6 fusion
  614.4 0.0 all-gather.2.cloned.1.call-done.given
  614.4 0.0 copy-start
  614.4 2.0 copy-done
  616.4 0.0 copy-start.2
  616.4 0.0 copy-start.1
  616.4 3.5 widen.4
  619.9 0.0 copy-done.2
  619.9 1.0 copy.19
  620.9 0.0 copy-done.1
  620.9 1.4 copy.20
  (1 shorter events, 0.0 us)
Async XLA Ops:
  7.2 607.2 %all-gather.2.cloned.1.call-start = ((), (), s32[]{:S(2)}) async-start(), calls=%async_computation | async-start | bytes 4587520 | tf_op jit(solution)/shard_map/all_gather | solution.py:1546
  582.9 30.9 %copy-start.3 = (f32[6,1152]{1,0:T(8,128)S(1)}, f32[6,1152]{1,0:T(8,128)}, u32[]{:S(2)}) copy-start(f32[6,1152]{1,0:T(8,128)} %get-tuple-element.25) | copy-start | bytes 82948
  614.4 2.0 copy-start
  616.4 3.5 copy-start.2
  616.4 4.5 copy-start.1
Sparse Core Ops, SparseCore 0:
  564.8 46.3 all-gather.1

commit v8 on v7

--- a/solution.py
+++ b/solution.py
@@ -20,7 +20,8 @@
 
 
 def sigmoid(x):
-    return 0.5 * jnp.tanh(0.5 * x) + 0.5
+    small = jnp.exp(-jnp.abs(x))
+    return jnp.where(x >= 0.0, 1.0, small) / (1.0 + small)
 
 
 def lane_blocks(channels):

time: 630 us -> 631 us (level)
  no operation moved by 1% of the time
where the time goes in v8:
time: 631 us; the launch traced here: 630 us
  Pallas kernels  603 us (96%)
  between operations  14.1 us (2%)
  local copies, waits for them, and re-layouts  9.43 us (1%)
    pallas_call x1, Pallas kernels, spread(): pl.pallas_call(functools.partial(spread_kernel, seqs, tokens, PART, TURN,...  419 us
    pallas_call x1, Pallas kernels, front(): pl.pallas_call(functools.partial(front_kernel, seqs, tokens, channels), o...  132 us
    pallas_call x3, Pallas kernels, widen(): pl.pallas_call(functools.partial(widen_kernel, channels // 128), grid_spe...  52.5 us
  transfers between devices with their start and end apart: 1, of which 0 were waited for; matrix products, arithmetic and copies ran while one was open for 0% of the time, Pallas kernels for 8%

profile of v8, /device:TPU:0, one launch (start us, length us, event | category | flops | bytes accessed | tf_op | source)
XLA Modules:
  0.0 630.1 jit_solution(1294512253575473076)
XLA Ops:
  7.2 0.0 all-gather.2.cloned.1.call-start
  7.2 0.7 convert_bitcast_fusion
  7.9 1.3 slice_bitcast_fusion
  9.2 0.8 broadcast_in_dim.8.keep
  10.1 131.9 %front.1 = (bf16[512,1152]{1,0:T(8,128)(2,1)}, f32[3,8,1152]{2,1,0:T(8,128)}, f32[3,8,1152]{2,1,0:T(8,128)}, bf16[528,3584]{1,0:T(8,128)(2,1)}, bf16[4,512,1152]...) custom-call(bf16[512,1152]{1,0:T(8,128)(2,1)} %bitcast.29, ...), custom_call_target="tpu_custom_call" | custom-call | flops 32614907904 | bytes 94371840 | tf_op jit(solution)/shard_map/front/pallas_call | solution.py:729
  142.0 0.9 reduce_sum.18
  142.9 0.9 reduce_sum.19
  143.9 0.6 pad_maximum_fusion.sums
  144.5 418.9 %spread.1 = (bf16[4,6912,896]{2,1,0:T(8,128)(2,1)}, f32[512,1152]{1,0:T(8,128)}, f32[6,1152]{1,0:T(8,128)}) custom-call(bf16[2048,1152]{1,0:T(8,128)(2,1)} %bitcast.32, bf16[2048,1152]{1,0:T(8,128)(2,1)} %bitcast.31, bf16[2048,896]{1,0:T(8,128)(2,1)} %bitcast.33, bf16[528,3584]{1,0:T(8,128)(2,1)} %get-tuple-element.20.grads_one, ...), custom_call_target="tpu_custom_call" | custom-call | flops 25367150592 | bytes 99090432 | tf_op jit(solution)/shard_map/spread/pallas_call | solution.py:1370
  563.4 2.2 constant_dynamic-slice_fusion
  565.6 0.0 all-gather.2.cloned.1.call-update
  565.6 18.2 %widen.5 = f32[1,3,2304,1152]{3,2,1,0:T(8,128)} custom-call(s32[1]{0:T(128)} %bitcast.11.core, bf16[4,6912,896]{2,1,0:T(8,128)(2,1)} %get-tuple-element.24.given), custom_call_target="tpu_custom_call" | custom-call | bytes 48365568 | tf_op jit(solution)/shard_map/widen/pallas_call | solution.py:1446
  583.8 0.0 copy-start.3
  583.8 30.9 %widen.3.refs_0_ = f32[2,3,2304,1152]{3,2,1,0:T(8,128)} custom-call(s32[1]{0:T(128)} %bitcast.11.core, bf16[4,6912,896]{2,1,0:T(8,128)(2,1)} %get-tuple-element.24.given), custom_call_target="tpu_custom_call" | custom-call | bytes 85983232 | tf_op jit(solution)/shard_map/widen/pallas_call | solution.py:1446
  614.6 0.0 copy-done.3
  614.6 0.6 fusion
  615.3 0.0 all-gather.2.cloned.1.call-done.given
  615.3 0.0 copy-start
  615.3 2.0 copy-done
  617.3 0.0 copy-start.2
  617.3 0.0 copy-start.1
  617.3 3.5 widen.4
  620.8 0.0 copy-done.2
  620.8 1.0 copy.19
  621.8 0.0 copy-done.1
  621.8 1.4 copy.20
  (1 shorter events, 0.0 us)
Async XLA Ops:
  7.2 608.1 %all-gather.2.cloned.1.call-start = ((), (), s32[]{:S(2)}) async-start(), calls=%async_computation | async-start | bytes 4587520 | tf_op jit(solution)/shard_map/all_gather | solution.py:1547
  583.8 30.9 %copy-start.3 = (f32[6,1152]{1,0:T(8,128)S(1)}, f32[6,1152]{1,0:T(8,128)}, u32[]{:S(2)}) copy-start(f32[6,1152]{1,0:T(8,128)} %get-tuple-element.25) | copy-start | bytes 82948
  615.3 2.0 copy-start
  617.3 3.5 copy-start.2
  617.3 4.5 copy-start.1
Sparse Core Ops, SparseCore 0:
  565.7 46.2 all-gather.1
